TPU v7x, 32 devices: a whole 2x2x4 slice. The times are simulated.
32 devices in a mesh: parts: 2 (over x), docs: 16 (over z, y, core).
Axes of the slice: x: 2, y: 2, z: 4, core: 2. Of those that a mesh axis runs over, the one named last changes fastest.
Arguments:
- doc_grads: bfloat16 [4096, 8192], P('parts', 'docs'), parts along dimension 0, may hold values from -6 to 6
- query_grads: bfloat16 [16384, 8192], P(('parts', 'docs')), parts along dimension 0, may hold values from -6 to 6
- left_inv: bfloat16 [2, 32, 32], replicated, may hold values from -17 to 17, as said below
- right_inv: bfloat16 [2, 128, 128], replicated, may hold values from -17 to 17, as said below
- cand_owner: int32 [8192, 1], P(('parts', 'docs')), parts along dimension 0, may hold values from 0 to 15; in each aligned block of 256 rows (0 to 255, 256 to 511, ...) at most 32 rows name the same one
- cand_row: int32 [8192], P(('parts', 'docs')), parts along dimension 0, may hold values from 0 to 127
Outputs:
- scores: float32 [16384, 256], P(('parts', 'docs')), parts along dimension 0
There are 2 independent parts, one for each index of `parts`. A program takes and returns all parts, laid end to end along the dimension named above; an argument that names none is the same for every part. Nothing has to cross between parts.
Inputs may be any that keep to these rules, and one draw needn't show every extreme that they name: `cand_owner`: within the 256 entries of one query batch no owner is named more than 32 times, a bound that some block reaches. `left_inv`: symmetric positive definite. `right_inv`: symmetric positive definite.
All inputs are finite; a program needn't handle non-finite values.
Results may differ from a plain program's by a relative error of at most 0.004.
Values may be sent and summed in bfloat16 or wider, within the bound.
No kernel may reach another device: no remote copies, remote signals or barrier semaphores. Data moves between devices by JAX's collectives and lax.ppermute only.
A program may use at most 128 MiB of HBM per device.

v0:
```python
import jax
import jax.numpy as jnp
from jax import lax
from jax.experimental import pallas as pl
from jax.experimental.pallas import tpu as pltpu
from jax.sharding import PartitionSpec as P

LANES = 128
SUBLANES = 8
MXU = 256
VMEM_BYTES = 48 << 20
ALL_VMEM_BYTES = 63 << 20


def call(kernel, out_shape, grid, in_specs, out_specs, flops, bytes_accessed, scratch=(), prefetch=0, vmem=VMEM_BYTES):
    return pl.pallas_call(
        kernel,
        grid_spec=pltpu.PrefetchScalarGridSpec(
            num_scalar_prefetch=prefetch,
            grid=grid,
            in_specs=in_specs,
            out_specs=out_specs,
            scratch_shapes=scratch,
        ),
        out_shape=out_shape,
        compiler_params=pltpu.CompilerParams(vmem_limit_bytes=vmem),
        cost_estimate=pl.CostEstimate(flops=flops, bytes_accessed=bytes_accessed, transcendentals=0),
    )


def dot(a, b):
    return jnp.dot(a, b, preferred_element_type=jnp.float32)


def one_hot(ids, docs):
    group, row = ids // LANES, ids % LANES
    in_group = (lax.broadcasted_iota(jnp.int32, (LANES, ids.shape[1]), 0) == row).astype(jnp.bfloat16)
    return jnp.concatenate(
        [in_group * (group == g).astype(jnp.bfloat16) for g in range(docs // LANES)], axis=0
    )


def prepare(doc_grads, owners, rows, devices, tail):
    docs, width = doc_grads.shape
    entries = rows.shape[0]
    doc_count = docs // devices
    block = max(tail, LANES)

    def kernel(docs_hbm, owners_hbm, rows_hbm, tail_ref, ids_ref, docs_ref, owners_ref, rows_ref, sems):
        copies = [
            pltpu.make_async_copy(docs_hbm.at[:, width - block :], docs_ref, sems.at[0]),
            pltpu.make_async_copy(owners_hbm, owners_ref, sems.at[1]),
            pltpu.make_async_copy(rows_hbm, rows_ref, sems.at[2]),
        ]
        for copy in copies:
            copy.start()
        for copy in copies:
            copy.wait()
        tail_ref[...] = docs_ref[...].T[block - tail :, :]
        ids = owners_ref[...] * doc_count + rows_ref[...]
        ids_ref[...] = jnp.broadcast_to(ids[None], ids_ref.shape)

    return call(
        kernel,
        [
            pltpu.HBM((tail, docs), doc_grads.dtype),
            pltpu.HBM((devices, 1, entries), jnp.int32),
        ],
        (1,),
        [pl.BlockSpec(memory_space=pltpu.HBM)] * 3,
        [
            pl.BlockSpec((tail, docs), lambda i: (0, 0)),
            pl.BlockSpec((devices, 1, entries), lambda i: (0, 0, 0)),
        ],
        0,
        2 * docs * (block + tail),
        scratch=[
            pltpu.VMEM((docs, block), doc_grads.dtype),
            pltpu.VMEM((1, entries), jnp.int32),
            pltpu.VMEM((1, entries), jnp.int32),
            pltpu.SemaphoreType.DMA((3,)),
        ],
        vmem=ALL_VMEM_BYTES,
    )(doc_grads, owners.reshape(1, entries), rows.reshape(1, entries))


def gather_rows(base, ids, tables, count):
    entries = ids.shape[2]
    docs = tables[0].shape[1]
    features = sum(t.shape[0] for t in tables)

    def kernel(base_ref, ids_ref, *refs):
        out_ref = refs[-1]
        hot = one_hot(ids_ref[0], docs)
        start = 0
        for table_ref in refs[:-1]:
            stop = start + table_ref.shape[0]
            out_ref[0, start:stop, :] = dot(table_ref[...], hot).astype(out_ref.dtype)
            start = stop

    return call(
        kernel,
        pltpu.HBM((count, features, entries), tables[0].dtype),
        (count,),
        [pl.BlockSpec((1, 1, entries), lambda b, base: (base[0] + b, 0, 0))]
        + [pl.BlockSpec(t.shape, lambda b, base: (0, 0)) for t in tables],
        pl.BlockSpec((1, features, entries), lambda b, base: (b, 0, 0)),
        2 * count * features * docs * entries,
        2 * features * (docs + count * entries),
        prefetch=1,
    )(base, ids, *tables)


def gather_pieces(me, ids, tables, partners):
    entries = ids.shape[2]
    docs = tables[0][0].shape[1]
    features = sum(rows for _, rows in tables)
    count = len(partners)

    def kernel(me_ref, *refs):
        table_refs = refs[count : count + len(tables)]
        for ids_ref, out_ref in zip(refs[:count], refs[count + len(tables) :]):
            hot = one_hot(ids_ref[0], docs)
            start = 0
            for table_ref in table_refs:
                stop = start + table_ref.shape[0]
                out_ref[start:stop, :] = dot(table_ref[...], hot).astype(out_ref.dtype)
                start = stop

    return call(
        kernel,
        [pltpu.HBM((features, entries), tables[0][0].dtype)] * count,
        (1,),
        [pl.BlockSpec((1, 1, entries), lambda i, me, k=k: (me[0] ^ k, 0, 0)) for k in partners]
        + [pl.BlockSpec((rows, docs), lambda i, me: (0, 0)) for _, rows in tables],
        [pl.BlockSpec((features, entries), lambda i, me: (0, 0))] * count,
        2 * count * features * docs * entries,
        2 * features * (docs + count * entries),
        prefetch=1,
    )(me, *[ids] * count, *[table for table, _ in tables])


def padded(values, above, below):
    zeros = lambda rows: [jnp.zeros((rows, values.shape[1]), values.dtype)] if rows else []
    return jnp.concatenate([*zeros(above), values, *zeros(below)], axis=0)


def score_pieces(me, prepared, chosen, total, width, scale):
    queries = prepared.shape[0]
    features, entries = next(iter(chosen.values())).shape
    count = len(chosen)
    whole = pl.BlockSpec((queries, entries), lambda i, me: (0, 0))

    def kernel(me_ref, *refs):
        out = refs[-2][...]
        for prepared_ref, chosen_ref in zip(refs[:count], refs[count : 2 * count]):
            out = out + dot(prepared_ref[...], padded(chosen_ref[...], 0, width - features))
        refs[-1][...] = out * scale

    return call(
        kernel,
        jax.ShapeDtypeStruct((queries, entries), jnp.float32),
        (1,),
        [pl.BlockSpec((queries, width), lambda i, me, k=k: (0, me[0] ^ k)) for k in chosen]
        + [pl.BlockSpec((features, entries), lambda i, me: (0, 0))] * count
        + [whole],
        whole,
        2 * count * features * queries * entries,
        2 * count * features * (queries + entries) + 8 * queries * entries,
        prefetch=1,
    )(me, *[prepared] * count, *chosen.values(), total)


def score_near(base, prepared, chosen, width, half):
    queries = prepared.shape[0]
    count, features, entries = chosen.shape
    tail = features - width
    block = max(tail, LANES)
    stride = width // block

    def kernel(base_ref, own_ref, far_ref, chosen_ref, out_ref):
        part = dot(own_ref[...], chosen_ref[0, :width, :])
        part += dot(far_ref[...], padded(chosen_ref[0, width:, :], block - tail, 0))

        @pl.when(pl.program_id(0) == 0)
        def _():
            out_ref[...] = part

        @pl.when(pl.program_id(0) > 0)
        def _():
            out_ref[...] += part

    return call(
        kernel,
        jax.ShapeDtypeStruct((queries, entries), jnp.float32),
        (count,),
        [
            pl.BlockSpec((queries, width), lambda j, base: (0, base[0] + j)),
            pl.BlockSpec(
                (queries, block), lambda j, base: (0, ((base[0] + j) ^ half) * stride + stride - 1)
            ),
            pl.BlockSpec((1, features, entries), lambda j, base: (j, 0, 0)),
        ],
        pl.BlockSpec((queries, entries), lambda j, base: (0, 0)),
        2 * count * features * queries * entries,
        2 * count * features * (queries + entries) + 4 * queries * entries,
        prefetch=1,
    )(base, prepared, prepared, chosen)


def score_all(prepared, chosen, scale):
    queries = prepared.shape[0]
    devices, width, entries = chosen.shape

    def kernel(prepared_ref, chosen_ref, out_ref):
        part = dot(prepared_ref[...], chosen_ref[...]) * scale

        @pl.when(pl.program_id(0) == 0)
        def _():
            out_ref[...] = part

        @pl.when(pl.program_id(0) > 0)
        def _():
            out_ref[...] += part

    steps = 4
    block = devices * width // steps
    return call(
        kernel,
        jax.ShapeDtypeStruct((queries, entries), jnp.float32),
        (steps,),
        [
            pl.BlockSpec((queries, block), lambda i: (0, i)),
            pl.BlockSpec((block, entries), lambda i: (i, 0)),
        ],
        pl.BlockSpec((queries, entries), lambda i: (0, 0)),
        2 * devices * width * queries * entries,
        2 * devices * width * (queries + entries) + 4 * queries * entries,
    )(prepared, chosen.reshape(devices * width, entries))


def precondition(queries, left_inv, right_inv):
    total, features = queries.shape
    layers, k_out, _ = left_inv.shape
    k_in = right_inv.shape[1]
    group = MXU // k_out
    pair = MXU // k_in
    rows = 64
    wide = k_out // pair
    both = 2 * group

    def spread(values, times):
        size = values.shape[0]
        rows = lax.broadcasted_iota(jnp.int32, (MXU, size), 0) // times
        picks = (rows == lax.broadcasted_iota(jnp.int32, (MXU, size), 1)).astype(values.dtype)
        wide = dot(picks, values).astype(values.dtype)
        wide = lax.dot_general(
            wide, picks, (((1,), (1,)), ((), ())), preferred_element_type=jnp.float32
        )
        row = lax.broadcasted_iota(jnp.int32, (MXU, MXU), 0) % times
        column = lax.broadcasted_iota(jnp.int32, (MXU, MXU), 1) % times
        return jnp.where(row == column, wide, 0.0).astype(values.dtype)

    def repeat(values, times):
        empty = jnp.zeros_like(values)
        return jnp.concatenate(
            [
                jnp.concatenate([values if i == j else empty for j in range(times)], axis=1)
                for i in range(times)
            ],
            axis=0,
        )

    def kernel(queries_ref, left_inv_ref, right_inv_ref, out_ref, middle_ref, left_ref, right_ref):
        @pl.when(pl.program_id(0) == 0)
        def _():
            for layer in range(layers):
                left_ref[layer] = spread(left_inv_ref[layer], group)
                right_ref[layer] = repeat(right_inv_ref[layer], pair)

        for layer in range(layers):
            first = layer * k_out * k_in
            stack = jnp.concatenate(
                [queries_ref[:, first + p * MXU : first + (p + 1) * MXU] for p in range(wide)], axis=0
            )
            middle_ref[...] = dot(stack, right_ref[layer])
            for q in range(0, rows, both):
                halves = []
                for start in (q, q + group):
                    tiles = []
                    for p in range(wide):
                        at = p * rows + start
                        for s in range(pair):
                            tiles.append(middle_ref[at : at + group, s * k_in : (s + 1) * k_in])
                    halves.append(jnp.concatenate(tiles, axis=0))
                middle = jnp.concatenate(halves, axis=1).astype(queries_ref.dtype)
                result = dot(left_ref[layer], middle)
                for a in range(k_out):
                    at = a * group
                    tile = jnp.concatenate(
                        [result[at : at + group, :k_in], result[at : at + group, k_in:]], axis=0
                    )
                    lanes = first + a * k_in
                    out_ref[q : q + both, lanes : lanes + k_in] = tile.astype(out_ref.dtype)

    return call(
        kernel,
        jax.ShapeDtypeStruct(queries.shape, queries.dtype),
        (total // rows,),
        [
            pl.BlockSpec((rows, features), lambda i: (i, 0)),
            pl.BlockSpec(left_inv.shape, lambda i: (0, 0, 0)),
            pl.BlockSpec(right_inv.shape, lambda i: (0, 0, 0)),
        ],
        pl.BlockSpec((rows, features), lambda i: (i, 0)),
        40000 * total * features,
        4 * total * features,
        scratch=[
            pltpu.VMEM((wide * rows, MXU), jnp.float32),
            pltpu.VMEM((layers, MXU, MXU), left_inv.dtype),
            pltpu.VMEM((layers, MXU, MXU), right_inv.dtype),
        ],
    )(queries, left_inv, right_inv)


def after(value, *earlier):
    return lax.optimization_barrier((value, *earlier))[0]


def on_device(doc_grads, query_grads, left_inv, right_inv, cand_owner, cand_row):
    devices = lax.axis_size("docs")
    half = devices // 2
    me = lax.axis_index("docs").astype(jnp.int32).reshape(1)
    base = me & -half
    doc_count = doc_grads.shape[0] // devices
    entries = cand_row.shape[0]
    width = doc_grads.shape[1]
    scale = query_grads.shape[1] ** (-0.5)

    def swap(values, k):
        return lax.ppermute(values, "docs", [(i, i ^ k) for i in range(devices)])

    def exchange(values):
        return lax.all_to_all(values, "docs", split_axis=0, concat_axis=0, tiled=True)

    tail = width // 8 if width % (4 * LANES) == 0 else 0
    if not tail:
        own_ids = cand_owner[:, 0] * doc_count + cand_row
        ids = exchange(jnp.broadcast_to(own_ids, (devices, 1, entries)))
        picked = gather_rows(jnp.zeros((1,), jnp.int32), ids, [doc_grads.T], devices)
        return score_all(precondition(query_grads, left_inv, right_inv), exchange(picked), scale)

    own_tail, own_ids = prepare(doc_grads, cand_owner, cand_row, devices, tail)
    across = swap(own_tail, half)
    ids = exchange(own_ids)
    table = after(doc_grads, own_ids).T
    far = list(range(half, devices))
    first, flight = far[:2], 5
    body = [(table, width - tail)]
    ids = after(ids, across)
    pieces = dict(zip(far, gather_pieces(me, ids, body, first)))
    came = {k: swap(pieces[k], k) for k in first}
    ids = after(ids, pieces[far[0]])
    picked = gather_rows(base, ids, [table, across], half)
    near = lax.all_to_all(
        picked,
        "docs",
        split_axis=0,
        concat_axis=0,
        axis_index_groups=[list(range(half)), list(range(half, devices))],
        tiled=True,
    )
    ids = after(ids, picked)
    pieces.update(zip(far[2:], gather_pieces(me, ids, body, far[2:])))
    ready = [came[k] for k in first]
    prepared = precondition(after(query_grads, *ready), left_inv, right_inv)
    for i, k in enumerate(far[2:]):
        before = ready if i < flight else [came[far[2 + i - flight]], prepared]
        came[k] = swap(after(pieces[k], *before), k)
    total = score_near(base, prepared, near, width, half)
    return score_pieces(me, prepared, came, total, width, scale)


def solution(mesh):
    placed = (
        P("parts", "docs"),
        P(("parts", "docs"), None),
        P(),
        P(),
        P(("parts", "docs"), None),
        P(("parts", "docs")),
    )
    return jax.shard_map(
        on_device, mesh=mesh, in_specs=placed, out_specs=P(("parts", "docs"), None), check_vma=False
    )
```

profile of v0, /device:TPU:0, one launch (start us, length us, event | category | flops | bytes accessed | tf_op | source)
XLA Modules:
  0.0 138.2 jit_solution(11632743954918343192)
XLA Ops:
  0.0 2.0 %shard_map.64 = (bf16[64,2048]{1,0:T(8,128)(2,1)}, s32[16,1,256]{2,1,0:T(1,128)}) custom-call(bf16[2048,512]{1,0:T(8,128)(2,1)} %docs_hbm.1, s32[1,256]{1,0:T(1,128)} %bitcast.7, s32[1,256]{1,0:T(1,128)} %bitcast.8), custom_call_target="tpu_custom_call" | custom-call | bytes 786432 | tf_op jit(solution)/shard_map/pallas_call | solution.py:63
  2.0 4.1 %collective-permute-start = (bf16[64,2048]{1,0:T(8,128)(2,1)}, bf16[64,2048]{1,0:T(8,128)(2,1)S(1)}, u32[]{:S(2)}, u32[]{:S(2)}) collective-permute-start(bf16[64,2048]{1,0:T(8,128)(2,1)} %get-tuple-element.27), channel_id=1, source_target_pairs={{0,8},{1,9},{2,10},{3,11},{4,12},{5,13},{6,14},{7,15},{8,0},{9,1},... | collective-permute-start | bytes 786440 | tf_op jit(solution)/shard_map/ppermute | solution.py:341
  6.1 3.9 %all-to-all-start = ((s32[16,1,256]{2,1,0:T(1,128)}), s32[16,1,256]{2,1,0:T(1,128)S(1)}, u32[]{:S(2)}, u32[]{:S(2)}) async-start(s32[16,1,256]{2,1,0:T(1,128)} %get-tuple-element.26), calls=%async_computation | async-start | bytes 32768 | tf_op jit(solution)/shard_map/all_to_all | solution.py:344
  10.0 2.9 %copy.7 = bf16[2048,512]{0,1:T(8,128)(2,1)S(1)} copy(bf16[2048,512]{1,0:T(8,128)(2,1)} %docs_hbm.1) | data formatting | bytes 4194304 | tf_op jit(solution)/shard_map/optimization_barrier | solution.py:327
  12.9 6.5 %all-to-all-done.refs_0_.refs_1_.ids_ref.refs_2_.refs_3_.refs_4_.refs_5_ = s32[16,1,256]{2,1,0:T(1,128)S(1)} async-done(((s32[16,1,256]{2,1,0:T(1,128)}), s32[16,1,256]{2,1,0:T(1,128)S(1)}, u32[]{:S(2)}, u32[]{:S(2)}) %all-to-all-start) | async-done | bytes 16416 | tf_op jit(solution)/shard_map/all_to_all | solution.py:344
  19.5 0.0 collective-permute-done.refs_1_
  19.5 1.9 %shard_map.65 = (bf16[448,256]{1,0:T(8,128)(2,1)}, bf16[448,256]{1,0:T(8,128)(2,1)}) custom-call(s32[1]{0:T(128)} %bitcast.me_ref, s32[16,1,256]{2,1,0:T(1,128)S(1)} %all-to-all-done.refs_0_.refs_1_.ids_ref.refs_2_.refs_3_.refs_4_.refs_5_, s32[16,1,256]{2,1,0:T(1,128)S(1)} %all-to-all-done.refs_0_.refs_1_.ids_ref.refs_2_.refs_3_.refs_4_.refs_5_, ...), custom_call_target="tpu_custom_call" | custom-call | flops 939524096 | bytes 2293760 | tf_op jit(solution)/shard_map/pallas_call | solution.py:130
  21.4 2.7 %collective-permute-start.1 = (bf16[448,256]{1,0:T(8,128)(2,1)}, bf16[448,256]{1,0:T(8,128)(2,1)S(1)}, u32[]{:S(2)}, u32[]{:S(2)}) collective-permute-start(bf16[448,256]{1,0:T(8,128)(2,1)} %get-tuple-element.30), channel_id=1, source_target_pairs={{0,8},{1,9},{2,10},{3,11},{4,12},{5,13},{6,14},{7,15},{8,0},{9,1},... | collective-permute-start | bytes 688136 | tf_op jit(solution)/shard_map/ppermute | solution.py:341
  24.0 8.0 %shard_map.67 = bf16[8,576,256]{2,1,0:T(8,128)(2,1)} custom-call(s32[1]{0:T(128)S(6)} %and.4.base_ref, s32[16,1,256]{2,1,0:T(1,128)S(1)} %all-to-all-done.refs_0_.refs_1_.ids_ref.refs_2_.refs_3_.refs_4_.refs_5_, bf16[512,2048]{1,0:T(8,128)(2,1)S(1)} %bitcast.5, bf16[64,2048]{1,0:T(8,128)(2,1)S(1)} %collective-permute-done.refs_1_), custom_call_target="tpu_custom_call" | custom-call | flops 4831838208 | bytes 4718592 | tf_op jit(solution)/shard_map/pallas_call | solution.py:101
  32.1 0.0 copy-start.5
  32.1 4.5 %all-to-all-start.1 = ((bf16[8,576,256]{2,1,0:T(8,128)(2,1)}), bf16[8,576,256]{2,1,0:T(8,128)(2,1)}, u32[]{:S(2)}, u32[]{:S(2)}) async-start(bf16[8,576,256]{2,1,0:T(8,128)(2,1)} %shard_map.67), calls=%async_computation.1 | async-start | bytes 4718592 | tf_op jit(solution)/shard_map/all_to_all | solution.py:365
  36.6 0.0 copy-done.5
  36.6 0.0 copy-start.2
  36.6 0.0 copy-start.3
  36.6 0.3 collective-permute-start.2
  36.9 3.8 %shard_map.68 = (bf16[448,256]{1,0:T(8,128)(2,1)}, bf16[448,256]{1,0:T(8,128)(2,1)}, bf16[448,256]{1,0:T(8,128)(2,1)}, bf16[448,256]{1,0:T(8,128)(2,1)}, bf16[44...) custom-call(s32[1]{0:T(128)} %bitcast.me_ref, ...), custom_call_target="tpu_custom_call" | custom-call | flops 2818572288 | bytes 3211264 | tf_op jit(solution)/shard_map/pallas_call | solution.py:130
  40.7 27.1 %collective-permute-done.2.refs_9_ = bf16[448,256]{1,0:T(8,128)(2,1)S(1)} collective-permute-done((bf16[448,256]{1,0:T(8,128)(2,1)S(1)}, bf16[448,256]{1,0:T(8,128)(2,1)S(1)}, u32[]{:S(2)}, u32[]{:S(2)}) %collective-permute-start.2) | collective-permute-done | bytes 229408 | tf_op jit(solution)/shard_map/ppermute | solution.py:341
  67.8 0.0 copy-start
  67.8 0.7 copy-done
  68.5 0.0 collective-permute-done.1.refs_8_
  68.5 2.2 %collective-permute-start.7 = (bf16[448,256]{1,0:T(8,128)(2,1)}, bf16[448,256]{1,0:T(8,128)(2,1)}, u32[]{:S(2)}, u32[]{:S(2)}) collective-permute-start(bf16[448,256]{1,0:T(8,128)(2,1)} %get-tuple-element.44), channel_id=1, source_target_pairs={{0,14},{1,15},{2,12},{3,13},{4,10},{5,11},{6,8},{7,9},{8,6},{9,7},... | collective-permute-start | bytes 688136 | tf_op jit(solution)/shard_map/ppermute | solution.py:341
  70.7 1.6 %collective-permute-start.6 = (bf16[448,256]{1,0:T(8,128)(2,1)}, bf16[448,256]{1,0:T(8,128)(2,1)}, u32[]{:S(2)}, u32[]{:S(2)}) collective-permute-start(bf16[448,256]{1,0:T(8,128)(2,1)} %get-tuple-element.42), channel_id=1, source_target_pairs={{0,13},{1,12},{2,15},{3,14},{4,9},{5,8},{6,11},{7,10},{8,5},{9,4},... | collective-permute-start | bytes 688136 | tf_op jit(solution)/shard_map/ppermute | solution.py:341
  72.3 1.2 collective-permute-start.5
  73.5 0.8 collective-permute-start.4
  74.3 3.5 %collective-permute-start.3 = (bf16[448,256]{1,0:T(8,128)(2,1)}, bf16[448,256]{1,0:T(8,128)(2,1)}, u32[]{:S(2)}, u32[]{:S(2)}) collective-permute-start(bf16[448,256]{1,0:T(8,128)(2,1)} %get-tuple-element.36), channel_id=1, source_target_pairs={{0,10},{1,11},{2,8},{3,9},{4,14},{5,15},{6,12},{7,13},{8,2},{9,3},... | collective-permute-start | bytes 688136 | tf_op jit(solution)/shard_map/ppermute | solution.py:341
  77.8 0.0 copy-done.2
  77.8 0.0 copy-done.3
  77.8 0.0 copy-start.4
  77.8 13.1 %shard_map.66.own_ref.far_ref.refs_0_.refs_1_.refs_2_.refs_3_.refs_4_.refs_5_.refs_6_.refs_7_ = bf16[512,8192]{1,0:T(8,128)(2,1)} custom-call(bf16[512,8192]{1,0:T(8,128)(2,1)} %queries_ref, bf16[2,32,32]{2,1,0:T(8,128)(2,1)S(1)} %copy-done.3, bf16[2,128,128]{2,1,0:T(8,128)(2,1)S(1)} %copy-done.2), custom_call_target="tpu_custom_call" | custom-call | flops 167772160000 | bytes 16777216 | tf_op jit(solution)/shard_map/pallas_call | solution.py:306
  91.0 32.1 %collective-permute-done.3.refs_10_ = bf16[448,256]{1,0:T(8,128)(2,1)} collective-permute-done((bf16[448,256]{1,0:T(8,128)(2,1)}, bf16[448,256]{1,0:T(8,128)(2,1)}, u32[]{:S(2)}, u32[]{:S(2)}) %collective-permute-start.3) | collective-permute-done | bytes 229408 | tf_op jit(solution)/shard_map/ppermute | solution.py:341
  123.1 0.0 copy-done.4
  123.1 0.0 copy-start.1
  123.1 1.7 %collective-permute-start.8 = (bf16[448,256]{1,0:T(8,128)(2,1)S(1)}, bf16[448,256]{1,0:T(8,128)(2,1)S(1)}, u32[]{:S(2)}, u32[]{:S(2)}) collective-permute-start(bf16[448,256]{1,0:T(8,128)(2,1)S(1)} %copy-done.4), channel_id=1, source_target_pairs={{0,15},{1,14},{2,13},{3,12},{4,11},{5,10},{6,9},{7,8},{8,7},{9,6},... | collective-permute-start | bytes 688136 | tf_op jit(solution)/shard_map/ppermute | solution.py:341
  124.8 0.0 all-to-all-done.1.chosen_ref
  124.8 7.0 %shard_map.69.refs_16_ = f32[512,256]{1,0:T(8,128)S(1)} custom-call(s32[1]{0:T(128)S(6)} %and.4.base_ref, bf16[512,8192]{1,0:T(8,128)(2,1)} %shard_map.66.own_ref.far_ref.refs_0_.refs_1_.refs_2_.refs_3_.refs_4_.refs_5_.refs_6_.refs_7_, bf16[512,8192]{1,0:T(8,128)(2,1)} %shard_map.66.own_ref.far_ref.refs_0_.refs_1_.refs_2_.refs_3_.refs_4_.refs_5_.refs_6_.refs_7_, ...), custom_call_target="tpu_custom_call" | custom-call | flops 1207959552 | bytes 7602176 | tf_op jit(solution)/shard_map/pallas_call | solution.py:193
  131.8 0.0 collective-permute-done.7.refs_14_
  131.8 0.0 collective-permute-done.6.refs_13_
  131.8 0.0 collective-permute-done.5.refs_12_
  131.8 0.0 collective-permute-done.4.refs_11_
  131.9 1.8 %collective-permute-done.8.refs_15_ = bf16[448,256]{1,0:T(8,128)(2,1)S(1)} collective-permute-done((bf16[448,256]{1,0:T(8,128)(2,1)S(1)}, bf16[448,256]{1,0:T(8,128)(2,1)S(1)}, u32[]{:S(2)}, u32[]{:S(2)}) %collective-permute-start.8) | collective-permute-done | bytes 229408 | tf_op jit(solution)/shard_map/ppermute | solution.py:341
  133.6 0.0 copy-done.1
  133.6 4.5 %shard_map.70 = f32[512,256]{1,0:T(8,128)} custom-call(s32[1]{0:T(128)} %bitcast.me_ref, bf16[512,8192]{1,0:T(8,128)(2,1)} %shard_map.66.own_ref.far_ref.refs_0_.refs_1_.refs_2_.refs_3_.refs_4_.refs_5_.refs_6_.refs_7_, bf16[512,8192]{1,0:T(8,128)(2,1)} %shard_map.66.own_ref.far_ref.refs_0_.refs_1_.refs_2_.refs_3_.refs_4_.refs_5_.refs_6_.refs_7_, ...), custom_call_target="tpu_custom_call" | custom-call | flops 939524096 | bytes 6553600 | tf_op jit(solution)/shard_map/pallas_call | solution.py:160
Async XLA Ops:
  2.0 17.5 %collective-permute-start = (bf16[64,2048]{1,0:T(8,128)(2,1)}, bf16[64,2048]{1,0:T(8,128)(2,1)S(1)}, u32[]{:S(2)}, u32[]{:S(2)}) collective-permute-start(bf16[64,2048]{1,0:T(8,128)(2,1)} %get-tuple-element.27), channel_id=1, source_target_pairs={{0,8},{1,9},{2,10},{3,11},{4,12},{5,13},{6,14},{7,15},{8,0},{9,1},... | collective-permute-start | bytes 786440 | tf_op jit(solution)/shard_map/ppermute | solution.py:341
  6.1 13.4 %all-to-all-start = ((s32[16,1,256]{2,1,0:T(1,128)}), s32[16,1,256]{2,1,0:T(1,128)S(1)}, u32[]{:S(2)}, u32[]{:S(2)}) async-start(s32[16,1,256]{2,1,0:T(1,128)} %get-tuple-element.26), calls=%async_computation | async-start | bytes 32768 | tf_op jit(solution)/shard_map/all_to_all | solution.py:344
  21.4 47.1 %collective-permute-start.1 = (bf16[448,256]{1,0:T(8,128)(2,1)}, bf16[448,256]{1,0:T(8,128)(2,1)S(1)}, u32[]{:S(2)}, u32[]{:S(2)}) collective-permute-start(bf16[448,256]{1,0:T(8,128)(2,1)} %get-tuple-element.30), channel_id=1, source_target_pairs={{0,8},{1,9},{2,10},{3,11},{4,12},{5,13},{6,14},{7,15},{8,0},{9,1},... | collective-permute-start | bytes 688136 | tf_op jit(solution)/shard_map/ppermute | solution.py:341
  32.1 4.5 %copy-start.5 = (bf16[448,256]{1,0:T(8,128)(2,1)S(1)}, bf16[448,256]{1,0:T(8,128)(2,1)}, u32[]{:S(2)}) copy-start(bf16[448,256]{1,0:T(8,128)(2,1)} %get-tuple-element.31) | copy-start | bytes 688132
  32.1 92.7 %all-to-all-start.1 = ((bf16[8,576,256]{2,1,0:T(8,128)(2,1)}), bf16[8,576,256]{2,1,0:T(8,128)(2,1)}, u32[]{:S(2)}, u32[]{:S(2)}) async-start(bf16[8,576,256]{2,1,0:T(8,128)(2,1)} %shard_map.67), calls=%async_computation.1 | async-start | bytes 4718592 | tf_op jit(solution)/shard_map/all_to_all | solution.py:365
  36.6 41.2 %copy-start.2 = (bf16[2,128,128]{2,1,0:T(8,128)(2,1)S(1)}, bf16[2,128,128]{2,1,0:T(8,128)(2,1)}, u32[]{:S(2)}) copy-start(bf16[2,128,128]{2,1,0:T(8,128)(2,1)} %right_inv_ref.1) | copy-start | bytes 196612
  36.6 41.2 %copy-start.3 = (bf16[2,32,32]{2,1,0:T(8,128)(2,1)S(1)}, bf16[2,32,32]{2,1,0:T(8,128)(2,1)}, u32[]{:S(2)}) copy-start(bf16[2,32,32]{2,1,0:T(8,128)(2,1)} %left_inv_ref.1) | copy-start | bytes 12292
  36.6 31.2 %collective-permute-start.2 = (bf16[448,256]{1,0:T(8,128)(2,1)S(1)}, bf16[448,256]{1,0:T(8,128)(2,1)S(1)}, u32[]{:S(2)}, u32[]{:S(2)}) collective-permute-start(bf16[448,256]{1,0:T(8,128)(2,1)S(1)} %copy-done.5), channel_id=1, source_target_pairs={{0,9},{1,8},{2,11},{3,10},{4,13},{5,12},{6,15},{7,14},{8,1},{9,0},... | collective-permute-start | bytes 688136 | tf_op jit(solution)/shard_map/ppermute | solution.py:341
  67.8 0.7 copy-start
  68.5 63.3 %collective-permute-start.7 = (bf16[448,256]{1,0:T(8,128)(2,1)}, bf16[448,256]{1,0:T(8,128)(2,1)}, u32[]{:S(2)}, u32[]{:S(2)}) collective-permute-start(bf16[448,256]{1,0:T(8,128)(2,1)} %get-tuple-element.44), channel_id=1, source_target_pairs={{0,14},{1,15},{2,12},{3,13},{4,10},{5,11},{6,8},{7,9},{8,6},{9,7},... | collective-permute-start | bytes 688136 | tf_op jit(solution)/shard_map/ppermute | solution.py:341
  70.7 61.1 %collective-permute-start.6 = (bf16[448,256]{1,0:T(8,128)(2,1)}, bf16[448,256]{1,0:T(8,128)(2,1)}, u32[]{:S(2)}, u32[]{:S(2)}) collective-permute-start(bf16[448,256]{1,0:T(8,128)(2,1)} %get-tuple-element.42), channel_id=1, source_target_pairs={{0,13},{1,12},{2,15},{3,14},{4,9},{5,8},{6,11},{7,10},{8,5},{9,4},... | collective-permute-start | bytes 688136 | tf_op jit(solution)/shard_map/ppermute | solution.py:341
  72.3 59.5 %collective-permute-start.5 = (bf16[448,256]{1,0:T(8,128)(2,1)}, bf16[448,256]{1,0:T(8,128)(2,1)}, u32[]{:S(2)}, u32[]{:S(2)}) collective-permute-start(bf16[448,256]{1,0:T(8,128)(2,1)} %get-tuple-element.40), channel_id=1, source_target_pairs={{0,12},{1,13},{2,14},{3,15},{4,8},{5,9},{6,10},{7,11},{8,4},{9,5},... | collective-permute-start | bytes 688136 | tf_op jit(solution)/shard_map/ppermute | solution.py:341
  73.5 58.3 %collective-permute-start.4 = (bf16[448,256]{1,0:T(8,128)(2,1)}, bf16[448,256]{1,0:T(8,128)(2,1)}, u32[]{:S(2)}, u32[]{:S(2)}) collective-permute-start(bf16[448,256]{1,0:T(8,128)(2,1)} %get-tuple-element.38), channel_id=1, source_target_pairs={{0,11},{1,10},{2,9},{3,8},{4,15},{5,14},{6,13},{7,12},{8,3},{9,2},... | collective-permute-start | bytes 688136 | tf_op jit(solution)/shard_map/ppermute | solution.py:341
  74.3 48.8 %collective-permute-start.3 = (bf16[448,256]{1,0:T(8,128)(2,1)}, bf16[448,256]{1,0:T(8,128)(2,1)}, u32[]{:S(2)}, u32[]{:S(2)}) collective-permute-start(bf16[448,256]{1,0:T(8,128)(2,1)} %get-tuple-element.36), channel_id=1, source_target_pairs={{0,10},{1,11},{2,8},{3,9},{4,14},{5,15},{6,12},{7,13},{8,2},{9,3},... | collective-permute-start | bytes 688136 | tf_op jit(solution)/shard_map/ppermute | solution.py:341
  77.8 45.2 %copy-start.4 = (bf16[448,256]{1,0:T(8,128)(2,1)S(1)}, bf16[448,256]{1,0:T(8,128)(2,1)}, u32[]{:S(2)}) copy-start(bf16[448,256]{1,0:T(8,128)(2,1)} %get-tuple-element.46) | copy-start | bytes 688132
  123.1 10.6 %copy-start.1 = (bf16[448,256]{1,0:T(8,128)(2,1)S(1)}, bf16[448,256]{1,0:T(8,128)(2,1)}, u32[]{:S(2)}) copy-start(bf16[448,256]{1,0:T(8,128)(2,1)} %copy-done) | copy-start | bytes 688132
  123.1 10.6 %collective-permute-start.8 = (bf16[448,256]{1,0:T(8,128)(2,1)S(1)}, bf16[448,256]{1,0:T(8,128)(2,1)S(1)}, u32[]{:S(2)}, u32[]{:S(2)}) collective-permute-start(bf16[448,256]{1,0:T(8,128)(2,1)S(1)} %copy-done.4), channel_id=1, source_target_pairs={{0,15},{1,14},{2,13},{3,12},{4,11},{5,10},{6,9},{7,8},{8,7},{9,6},... | collective-permute-start | bytes 688136 | tf_op jit(solution)/shard_map/ppermute | solution.py:341
where the time goes:
time: 139 us; the launch traced here: 138 us
  waiting for transfers between devices  67.5 us (49%)
  Pallas kernels  40.4 us (29%)
  starting transfers between devices  26.5 us (19%)
  local copies, waits for them, and re-layouts  3.64 us (3%)
    ppermute x9, waiting for transfers between devices, swap(): return lax.ppermute(values, 'docs', [(i, i ^ k) for i in range(devices)])  61 us
    ppermute x9, starting transfers between devices, swap(): return lax.ppermute(values, 'docs', [(i, i ^ k) for i in range(devices)])  18.1 us
    pallas_call x1, Pallas kernels, precondition(): call(kernel, jax.ShapeDtypeStruct(queries.shape, queries.dtype), (total /...  13.1 us
    pallas_call x1, Pallas kernels, gather_rows(): call(kernel, pltpu.HBM((count, features, entries), tables[0].dtype), (cou...  8.01 us
    pallas_call x1, Pallas kernels, score_near(): call(kernel, jax.ShapeDtypeStruct((queries, entries), jnp.float32), (coun...  7 us
    all_to_all x1, waiting for transfers between devices, exchange(): lax.all_to_all(values, 'docs', split_axis=0, concat_axis=0, tiled=True)  6.54 us
    pallas_call x2, Pallas kernels, gather_pieces(): call(kernel, [pltpu.HBM((features, entries), tables[0][0].dtype)] * count...  5.72 us
    pallas_call x1, Pallas kernels, score_pieces(): call(kernel, jax.ShapeDtypeStruct((queries, entries), jnp.float32), (1,),...  4.55 us
  transfers between devices with their start and end apart: 11, of which 4 were waited for; matrix products, arithmetic and copies ran while one was open for 2% of the time, Pallas kernels for 23%

commit v1 on v0

--- a/solution.py
+++ b/solution.py
@@ -40,15 +40,16 @@
     )
 
 
-def prepare(doc_grads, owners, rows, devices, tail):
-    docs, width = doc_grads.shape
+def prepare(doc_grads, owners, rows, devices, first, size):
+    docs = doc_grads.shape[0]
     entries = rows.shape[0]
     doc_count = docs // devices
-    block = max(tail, LANES)
-
-    def kernel(docs_hbm, owners_hbm, rows_hbm, tail_ref, ids_ref, docs_ref, owners_ref, rows_ref, sems):
+    block = -(-size // LANES) * LANES
+    skip = first % LANES
+
+    def kernel(docs_hbm, owners_hbm, rows_hbm, some_ref, ids_ref, docs_ref, owners_ref, rows_ref, sems):
         copies = [
-            pltpu.make_async_copy(docs_hbm.at[:, width - block :], docs_ref, sems.at[0]),
+            pltpu.make_async_copy(docs_hbm.at[:, pl.ds(first - skip, block)], docs_ref, sems.at[0]),
             pltpu.make_async_copy(owners_hbm, owners_ref, sems.at[1]),
             pltpu.make_async_copy(rows_hbm, rows_ref, sems.at[2]),
         ]
@@ -56,24 +57,24 @@
             copy.start()
         for copy in copies:
             copy.wait()
-        tail_ref[...] = docs_ref[...].T[block - tail :, :]
+        some_ref[...] = docs_ref[...].T[skip : skip + size, :]
         ids = owners_ref[...] * doc_count + rows_ref[...]
         ids_ref[...] = jnp.broadcast_to(ids[None], ids_ref.shape)
 
     return call(
         kernel,
         [
-            pltpu.HBM((tail, docs), doc_grads.dtype),
+            pltpu.HBM((size, docs), doc_grads.dtype),
             pltpu.HBM((devices, 1, entries), jnp.int32),
         ],
         (1,),
         [pl.BlockSpec(memory_space=pltpu.HBM)] * 3,
         [
-            pl.BlockSpec((tail, docs), lambda i: (0, 0)),
+            pl.BlockSpec((size, docs), lambda i: (0, 0)),
             pl.BlockSpec((devices, 1, entries), lambda i: (0, 0, 0)),
         ],
         0,
-        2 * docs * (block + tail),
+        2 * docs * (block + size),
         scratch=[
             pltpu.VMEM((docs, block), doc_grads.dtype),
             pltpu.VMEM((1, entries), jnp.int32),
@@ -105,8 +106,8 @@
         [pl.BlockSpec((1, 1, entries), lambda b, base: (base[0] + b, 0, 0))]
         + [pl.BlockSpec(t.shape, lambda b, base: (0, 0)) for t in tables],
         pl.BlockSpec((1, features, entries), lambda b, base: (b, 0, 0)),
-        2 * count * features * docs * entries,
-        2 * features * (docs + count * entries),
+        1000,
+        1000,
         prefetch=1,
     )(base, ids, *tables)
 
@@ -134,8 +135,8 @@
         [pl.BlockSpec((1, 1, entries), lambda i, me, k=k: (me[0] ^ k, 0, 0)) for k in partners]
         + [pl.BlockSpec((rows, docs), lambda i, me: (0, 0)) for _, rows in tables],
         [pl.BlockSpec((features, entries), lambda i, me: (0, 0))] * count,
-        2 * count * features * docs * entries,
-        2 * features * (docs + count * entries),
+        1000,
+        1000,
         prefetch=1,
     )(me, *[ids] * count, *[table for table, _ in tables])
 
@@ -171,16 +172,16 @@
     )(me, *[prepared] * count, *chosen.values(), total)
 
 
-def score_near(base, prepared, chosen, width, half):
+def score_near(base, prepared, chosen, width, first, half):
     queries = prepared.shape[0]
     count, features, entries = chosen.shape
-    tail = features - width
-    block = max(tail, LANES)
-    stride = width // block
+    size = features - width
+    stride = width // LANES
 
     def kernel(base_ref, own_ref, far_ref, chosen_ref, out_ref):
+        above = first % LANES
         part = dot(own_ref[...], chosen_ref[0, :width, :])
-        part += dot(far_ref[...], padded(chosen_ref[0, width:, :], block - tail, 0))
+        part += dot(far_ref[...], padded(chosen_ref[0, width:, :], above, LANES - above - size))
 
         @pl.when(pl.program_id(0) == 0)
         def _():
@@ -197,7 +198,8 @@
         [
             pl.BlockSpec((queries, width), lambda j, base: (0, base[0] + j)),
             pl.BlockSpec(
-                (queries, block), lambda j, base: (0, ((base[0] + j) ^ half) * stride + stride - 1)
+                (queries, LANES),
+                lambda j, base: (0, ((base[0] + j) ^ half) * stride + first // LANES),
             ),
             pl.BlockSpec((1, features, entries), lambda j, base: (j, 0, 0)),
         ],
@@ -206,6 +208,37 @@
         2 * count * features * (queries + entries) + 4 * queries * entries,
         prefetch=1,
     )(base, prepared, prepared, chosen)
+
+
+def score_across(base, prepared, chosen, total, width, first, half):
+    queries = prepared.shape[0]
+    count, features, entries = chosen.shape
+    whole = pl.BlockSpec((queries, entries), lambda i, base: (0, 0))
+
+    def kernel(base_ref, *refs):
+        chosen_ref, total_ref, out_ref = refs[count:]
+        out = total_ref[...]
+        for j in range(count):
+            out = out + dot(refs[j][...], chosen_ref[j])
+        out_ref[...] = out
+
+    return call(
+        kernel,
+        jax.ShapeDtypeStruct((queries, entries), jnp.float32),
+        (1,),
+        [
+            pl.BlockSpec(
+                (queries, features),
+                lambda i, base, j=j: (0, (((base[0] + j) ^ half) * width + first) // features),
+            )
+            for j in range(count)
+        ]
+        + [pl.BlockSpec(chosen.shape, lambda i, base: (0, 0, 0)), whole],
+        whole,
+        2 * count * features * queries * entries,
+        2 * count * features * (queries + entries) + 8 * queries * entries,
+        prefetch=1,
+    )(base, *[prepared] * count, chosen, total)
 
 
 def score_all(prepared, chosen, scale):
@@ -343,41 +376,43 @@
     def exchange(values):
         return lax.all_to_all(values, "docs", split_axis=0, concat_axis=0, tiled=True)
 
-    tail = width // 8 if width % (4 * LANES) == 0 else 0
-    if not tail:
+    if width % (4 * LANES):
         own_ids = cand_owner[:, 0] * doc_count + cand_row
         ids = exchange(jnp.broadcast_to(own_ids, (devices, 1, entries)))
         picked = gather_rows(jnp.zeros((1,), jnp.int32), ids, [doc_grads.T], devices)
         return score_all(precondition(query_grads, left_inv, right_inv), exchange(picked), scale)
 
-    own_tail, own_ids = prepare(doc_grads, cand_owner, cand_row, devices, tail)
-    across = swap(own_tail, half)
+    def exchange_inside(values):
+        return lax.all_to_all(
+            values,
+            "docs",
+            split_axis=0,
+            concat_axis=0,
+            axis_index_groups=[list(range(half)), list(range(half, devices))],
+            tiled=True,
+        )
+
+    direct, first, second = width // 8 * 5, width // 8, width // 4
+    own_first, own_ids = prepare(doc_grads, cand_owner, cand_row, devices, direct, first)
+    across_first = swap(own_first, half)
     ids = exchange(own_ids)
     table = after(doc_grads, own_ids).T
+    across_second = swap(after(table[direct + first :], across_first), half)
+    ids = after(ids, across_first)
     far = list(range(half, devices))
-    first, flight = far[:2], 5
-    body = [(table, width - tail)]
-    ids = after(ids, across)
-    pieces = dict(zip(far, gather_pieces(me, ids, body, first)))
-    came = {k: swap(pieces[k], k) for k in first}
-    ids = after(ids, pieces[far[0]])
-    picked = gather_rows(base, ids, [table, across], half)
-    near = lax.all_to_all(
-        picked,
-        "docs",
-        split_axis=0,
-        concat_axis=0,
-        axis_index_groups=[list(range(half)), list(range(half, devices))],
-        tiled=True,
-    )
-    ids = after(ids, picked)
-    pieces.update(zip(far[2:], gather_pieces(me, ids, body, far[2:])))
-    ready = [came[k] for k in first]
-    prepared = precondition(after(query_grads, *ready), left_inv, right_inv)
-    for i, k in enumerate(far[2:]):
-        before = ready if i < flight else [came[far[2 + i - flight]], prepared]
+    pieces = dict(zip(far, gather_pieces(me, ids, [(table, direct)], far)))
+    picked = gather_rows(base, after(ids, pieces[far[0]]), [table, across_first], half)
+    near = exchange_inside(picked)
+    prepared = precondition(after(query_grads, across_second), left_inv, right_inv)
+    flight = 5
+    came = {}
+    for i, k in enumerate(far):
+        before = [across_second] if i < flight else [came[far[i - flight]], prepared]
         came[k] = swap(after(pieces[k], *before), k)
-    total = score_near(base, prepared, near, width, half)
+    picked = gather_rows(base, after(ids, came[far[2]]), [across_second], half)
+    near_second = exchange_inside(picked)
+    total = score_near(base, prepared, after(near, came[far[2]]), width, direct, half)
+    total = score_across(base, prepared, near_second, total, width, direct + first, half)
     return score_pieces(me, prepared, came, total, width, scale)
 
 

time: 139 us -> 152 us (1.094)
  the two profiles are of different devices: /device:TPU:0 before, /device:TPU:11 now
where the time goes in v1:
time: 152 us; the launch traced here: 151 us
  waiting for transfers between devices  70 us (46%)
  Pallas kernels  44.5 us (29%)
  starting transfers between devices  32.5 us (21%)
  local copies, waits for them, and re-layouts  3.65 us (2%)
    ppermute x10, waiting for transfers between devices, swap(): return lax.ppermute(values, 'docs', [(i, i ^ k) for i in range(devices)])  64.8 us
    all_to_all x2, starting transfers between devices, exchange_inside(): lax.all_to_all(values, 'docs', split_axis=0, concat_axis=0, axis_index_gr...  13.8 us
    ppermute x10, starting transfers between devices, swap(): return lax.ppermute(values, 'docs', [(i, i ^ k) for i in range(devices)])  13.8 us
    pallas_call x1, Pallas kernels, precondition(): call(kernel, jax.ShapeDtypeStruct(queries.shape, queries.dtype), (total /...  13.2 us
    pallas_call x2, Pallas kernels, gather_rows(): call(kernel, pltpu.HBM((count, features, entries), tables[0].dtype), (cou...  12.2 us
    pallas_call x1, Pallas kernels, score_near(): call(kernel, jax.ShapeDtypeStruct((queries, entries), jnp.float32), (coun...  7 us
    all_to_all x1, waiting for transfers between devices, exchange(): lax.all_to_all(values, 'docs', split_axis=0, concat_axis=0, tiled=True)  5.17 us
    all_to_all x1, starting transfers between devices, exchange(): lax.all_to_all(values, 'docs', split_axis=0, concat_axis=0, tiled=True)  4.87 us
  transfers between devices with their start and end apart: 13, of which 6 were waited for; matrix products, arithmetic and copies ran while one was open for 2% of the time, Pallas kernels for 18%

profile of v1, /device:TPU:11, one launch (start us, length us, event | category | flops | bytes accessed | tf_op | source)
XLA Modules:
  0.0 150.7 jit_solution(10549275428544000934)
XLA Ops:
  0.0 2.0 %shard_map.64 = (bf16[64,2048]{1,0:T(8,128)(2,1)}, s32[16,1,256]{2,1,0:T(1,128)}) custom-call(bf16[2048,512]{1,0:T(8,128)(2,1)} %docs_hbm.1, s32[1,256]{1,0:T(1,128)} %bitcast.7, s32[1,256]{1,0:T(1,128)} %bitcast.8), custom_call_target="tpu_custom_call" | custom-call | bytes 786432 | tf_op jit(solution)/shard_map/pallas_call | solution.py:64
  2.0 2.4 %collective-permute-start = (bf16[64,2048]{1,0:T(8,128)(2,1)}, bf16[64,2048]{1,0:T(8,128)(2,1)S(1)}, u32[]{:S(2)}, u32[]{:S(2)}) collective-permute-start(bf16[64,2048]{1,0:T(8,128)(2,1)} %get-tuple-element.32), channel_id=1, source_target_pairs={{0,8},{1,9},{2,10},{3,11},{4,12},{5,13},{6,14},{7,15},{8,0},{9,1},... | collective-permute-start | bytes 786440 | tf_op jit(solution)/shard_map/ppermute | solution.py:374
  4.3 4.9 %all-to-all-start = ((s32[16,1,256]{2,1,0:T(1,128)}), s32[16,1,256]{2,1,0:T(1,128)S(1)}, u32[]{:S(2)}, u32[]{:S(2)}) async-start(s32[16,1,256]{2,1,0:T(1,128)} %get-tuple-element.30), calls=%async_computation | async-start | bytes 32768 | tf_op jit(solution)/shard_map/all_to_all | solution.py:377
  9.2 2.9 %copy.7 = bf16[2048,512]{0,1:T(8,128)(2,1)S(1)} copy(bf16[2048,512]{1,0:T(8,128)(2,1)} %docs_hbm.1) | data formatting | bytes 4194304 | tf_op jit(solution)/shard_map/optimization_barrier | solution.py:360
  12.2 5.2 %all-to-all-done.refs_0_.refs_1_.refs_2_.refs_3_.refs_4_.refs_5_.refs_6_.refs_7_.ids_ref = s32[16,1,256]{2,1,0:T(1,128)S(1)} async-done(((s32[16,1,256]{2,1,0:T(1,128)}), s32[16,1,256]{2,1,0:T(1,128)S(1)}, u32[]{:S(2)}, u32[]{:S(2)}) %all-to-all-start) | async-done | bytes 16416 | tf_op jit(solution)/shard_map/all_to_all | solution.py:377
  17.3 0.0 collective-permute-done.refs_1_
  17.3 3.6 %shard_map.66 = (bf16[320,256]{1,0:T(8,128)(2,1)}, bf16[320,256]{1,0:T(8,128)(2,1)}, bf16[320,256]{1,0:T(8,128)(2,1)}, bf16[320,256]{1,0:T(8,128)(2,1)}, bf16[32...) custom-call(s32[1]{0:T(128)} %bitcast.me_ref, ...), custom_call_target="tpu_custom_call" | custom-call | flops 1000 | bytes 1000 | tf_op jit(solution)/shard_map/pallas_call | solution.py:131
  21.0 8.0 %shard_map.68 = bf16[8,576,256]{2,1,0:T(8,128)(2,1)} custom-call(s32[1]{0:T(128)S(6)} %and.4.base_ref, s32[16,1,256]{2,1,0:T(1,128)S(1)} %all-to-all-done.refs_0_.refs_1_.refs_2_.refs_3_.refs_4_.refs_5_.refs_6_.refs_7_.ids_ref, bf16[512,2048]{1,0:T(8,128)(2,1)S(1)} %bitcast.5, bf16[64,2048]{1,0:T(8,128)(2,1)S(1)} %collective-permute-done.refs_1_), custom_call_target="tpu_custom_call" | custom-call | flops 1000 | bytes 1000 | tf_op jit(solution)/shard_map/pallas_call | solution.py:102
  28.9 0.0 copy-start.7
  28.9 5.9 %all-to-all-start.2 = ((bf16[8,576,256]{2,1,0:T(8,128)(2,1)}), bf16[8,576,256]{2,1,0:T(8,128)(2,1)}, u32[]{:S(2)}, u32[]{:S(2)}) async-start(bf16[8,576,256]{2,1,0:T(8,128)(2,1)} %shard_map.68), calls=%async_computation.2 | async-start | bytes 4718592 | tf_op jit(solution)/shard_map/all_to_all | solution.py:386
  34.8 0.0 copy-start.2
  34.8 0.0 copy-start.3
  34.9 2.5 %collective-permute-start.1 = (bf16[128,2048]{1,0:T(8,128)(2,1)S(1)}, bf16[128,2048]{1,0:T(8,128)(2,1)S(1)}, u32[]{:S(2)}, u32[]{:S(2)}) collective-permute-start(bf16[128,2048]{1,0:T(8,128)(2,1)S(1)} %slice.4), channel_id=1, source_target_pairs={{0,8},{1,9},{2,10},{3,11},{4,12},{5,13},{6,14},{7,15},{8,0},{9,1},... | collective-permute-start | bytes 1572872 | tf_op jit(solution)/shard_map/ppermute | solution.py:374
  37.3 37.4 %collective-permute-done.1.refs_0_ = bf16[128,2048]{1,0:T(8,128)(2,1)S(1)} collective-permute-done((bf16[128,2048]{1,0:T(8,128)(2,1)S(1)}, bf16[128,2048]{1,0:T(8,128)(2,1)S(1)}, u32[]{:S(2)}, u32[]{:S(2)}) %collective-permute-start.1) | collective-permute-done | bytes 524320 | tf_op jit(solution)/shard_map/ppermute | solution.py:374
  74.7 0.0 copy-done.7
  74.7 0.2 collective-permute-start.4
  74.9 3.1 %collective-permute-start.2 = (bf16[320,256]{1,0:T(8,128)(2,1)}, bf16[320,256]{1,0:T(8,128)(2,1)}, u32[]{:S(2)}, u32[]{:S(2)}) collective-permute-start(bf16[320,256]{1,0:T(8,128)(2,1)} %get-tuple-element.37), channel_id=1, source_target_pairs={{0,8},{1,9},{2,10},{3,11},{4,12},{5,13},{6,14},{7,15},{8,0},{9,1},... | collective-permute-start | bytes 491528 | tf_op jit(solution)/shard_map/ppermute | solution.py:374
  78.0 0.0 collective-permute-start.6
  78.0 1.3 collective-permute-start.5
  79.3 1.4 collective-permute-start.3
  80.6 15.0 %collective-permute-done.4.refs_10_ = bf16[320,256]{1,0:T(8,128)(2,1)S(1)} collective-permute-done((bf16[320,256]{1,0:T(8,128)(2,1)S(1)}, bf16[320,256]{1,0:T(8,128)(2,1)S(1)}, u32[]{:S(2)}, u32[]{:S(2)}) %collective-permute-start.4) | collective-permute-done | bytes 163872 | tf_op jit(solution)/shard_map/ppermute | solution.py:374
  95.6 0.0 copy-start
  95.6 0.7 copy-done
  96.3 4.2 %shard_map.67 = bf16[8,128,256]{2,1,0:T(8,128)(2,1)} custom-call(s32[1]{0:T(128)S(6)} %and.4.base_ref, s32[16,1,256]{2,1,0:T(1,128)S(1)} %all-to-all-done.refs_0_.refs_1_.refs_2_.refs_3_.refs_4_.refs_5_.refs_6_.refs_7_.ids_ref, bf16[128,2048]{1,0:T(8,128)(2,1)S(1)} %collective-permute-done.1.refs_0_), custom_call_target="tpu_custom_call" | custom-call | flops 1000 | bytes 1000 | tf_op jit(solution)/shard_map/pallas_call | solution.py:102
  100.5 0.0 all-to-all-done.2.chosen_ref
  100.5 8.0 %all-to-all-start.1 = ((bf16[8,128,256]{2,1,0:T(8,128)(2,1)}), bf16[8,128,256]{2,1,0:T(8,128)(2,1)}, u32[]{:S(2)}, u32[]{:S(2)}) async-start(bf16[8,128,256]{2,1,0:T(8,128)(2,1)} %shard_map.67), calls=%async_computation.1 | async-start | bytes 1048576 | tf_op jit(solution)/shard_map/all_to_all | solution.py:386
  108.4 0.0 copy-done.2
  108.4 0.0 copy-done.3
  108.4 0.0 copy-start.6
  108.5 0.0 copy-start.5
  108.5 0.0 copy-start.4
  108.5 13.2 %shard_map.65.own_ref.far_ref.refs_0_.refs_1_.refs_2_.refs_3_.refs_4_.refs_5_.refs_6_.refs_7_ = bf16[512,8192]{1,0:T(8,128)(2,1)} custom-call(bf16[512,8192]{1,0:T(8,128)(2,1)} %queries_ref, bf16[2,32,32]{2,1,0:T(8,128)(2,1)S(1)} %copy-done.3, bf16[2,128,128]{2,1,0:T(8,128)(2,1)S(1)} %copy-done.2), custom_call_target="tpu_custom_call" | custom-call | flops 167772160000 | bytes 16777216 | tf_op jit(solution)/shard_map/pallas_call | solution.py:339
  121.6 0.0 collective-permute-done.3.refs_9_
  121.6 0.0 collective-permute-done.2.refs_8_
  121.6 0.0 copy-done.6
  121.6 0.1 collective-permute-start.7
  121.7 0.0 copy-done.5
  121.7 2.6 %collective-permute-start.8 = (bf16[320,256]{1,0:T(8,128)(2,1)S(1)}, bf16[320,256]{1,0:T(8,128)(2,1)S(1)}, u32[]{:S(2)}, u32[]{:S(2)}) collective-permute-start(bf16[320,256]{1,0:T(8,128)(2,1)S(1)} %copy-done.5), channel_id=1, source_target_pairs={{0,14},{1,15},{2,12},{3,13},{4,10},{5,11},{6,8},{7,9},{8,6},{9,7},... | collective-permute-start | bytes 491528 | tf_op jit(solution)/shard_map/ppermute | solution.py:374
  124.3 0.0 copy-done.4
  124.3 0.4 collective-permute-start.9
  124.7 7.0 %shard_map.69.refs_9_ = f32[512,256]{1,0:T(8,128)S(1)} custom-call(s32[1]{0:T(128)S(6)} %and.4.base_ref, bf16[512,8192]{1,0:T(8,128)(2,1)} %shard_map.65.own_ref.far_ref.refs_0_.refs_1_.refs_2_.refs_3_.refs_4_.refs_5_.refs_6_.refs_7_, bf16[512,8192]{1,0:T(8,128)(2,1)} %shard_map.65.own_ref.far_ref.refs_0_.refs_1_.refs_2_.refs_3_.refs_4_.refs_5_.refs_6_.refs_7_, ...), custom_call_target="tpu_custom_call" | custom-call | flops 1207959552 | bytes 7602176 | tf_op jit(solution)/shard_map/pallas_call | solution.py:194
  131.7 0.0 copy-start.1
  131.7 0.0 all-to-all-done.1.refs_8_
  131.7 2.2 %shard_map.70.refs_16_ = f32[512,256]{1,0:T(8,128)S(1)} custom-call(s32[1]{0:T(128)S(6)} %and.4.base_ref, bf16[512,8192]{1,0:T(8,128)(2,1)} %shard_map.65.own_ref.far_ref.refs_0_.refs_1_.refs_2_.refs_3_.refs_4_.refs_5_.refs_6_.refs_7_, bf16[512,8192]{1,0:T(8,128)(2,1)} %shard_map.65.own_ref.far_ref.refs_0_.refs_1_.refs_2_.refs_3_.refs_4_.refs_5_.refs_6_.refs_7_, ...), custom_call_target="tpu_custom_call" | custom-call | flops 268435456 | bytes 2621440 | tf_op jit(solution)/shard_map/pallas_call | solution.py:225
  133.9 0.0 collective-permute-done.6.refs_12_
  133.9 0.0 collective-permute-done.5.refs_11_
  133.9 4.8 %collective-permute-done.7.refs_13_ = bf16[320,256]{1,0:T(8,128)(2,1)S(1)} collective-permute-done((bf16[320,256]{1,0:T(8,128)(2,1)S(1)}, bf16[320,256]{1,0:T(8,128)(2,1)S(1)}, u32[]{:S(2)}, u32[]{:S(2)}) %collective-permute-start.7) | collective-permute-done | bytes 163872 | tf_op jit(solution)/shard_map/ppermute | solution.py:374
  138.7 4.1 %collective-permute-done.8.refs_14_ = bf16[320,256]{1,0:T(8,128)(2,1)S(1)} collective-permute-done((bf16[320,256]{1,0:T(8,128)(2,1)S(1)}, bf16[320,256]{1,0:T(8,128)(2,1)S(1)}, u32[]{:S(2)}, u32[]{:S(2)}) %collective-permute-start.8) | collective-permute-done | bytes 163872 | tf_op jit(solution)/shard_map/ppermute | solution.py:374
  142.8 3.5 %collective-permute-done.9.refs_15_ = bf16[320,256]{1,0:T(8,128)(2,1)S(1)} collective-permute-done((bf16[320,256]{1,0:T(8,128)(2,1)S(1)}, bf16[320,256]{1,0:T(8,128)(2,1)S(1)}, u32[]{:S(2)}, u32[]{:S(2)}) %collective-permute-start.9) | collective-permute-done | bytes 163872 | tf_op jit(solution)/shard_map/ppermute | solution.py:374
  146.3 0.0 copy-done.1
  146.3 4.4 %shard_map.71 = f32[512,256]{1,0:T(8,128)} custom-call(s32[1]{0:T(128)} %bitcast.me_ref, bf16[512,8192]{1,0:T(8,128)(2,1)} %shard_map.65.own_ref.far_ref.refs_0_.refs_1_.refs_2_.refs_3_.refs_4_.refs_5_.refs_6_.refs_7_, bf16[512,8192]{1,0:T(8,128)(2,1)} %shard_map.65.own_ref.far_ref.refs_0_.refs_1_.refs_2_.refs_3_.refs_4_.refs_5_.refs_6_.refs_7_, ...), custom_call_target="tpu_custom_call" | custom-call | flops 671088640 | bytes 4980736 | tf_op jit(solution)/shard_map/pallas_call | solution.py:161
  (1 shorter events, 0.0 us)
Async XLA Ops:
  2.0 15.4 %collective-permute-start = (bf16[64,2048]{1,0:T(8,128)(2,1)}, bf16[64,2048]{1,0:T(8,128)(2,1)S(1)}, u32[]{:S(2)}, u32[]{:S(2)}) collective-permute-start(bf16[64,2048]{1,0:T(8,128)(2,1)} %get-tuple-element.32), channel_id=1, source_target_pairs={{0,8},{1,9},{2,10},{3,11},{4,12},{5,13},{6,14},{7,15},{8,0},{9,1},... | collective-permute-start | bytes 786440 | tf_op jit(solution)/shard_map/ppermute | solution.py:374
  4.3 13.0 %all-to-all-start = ((s32[16,1,256]{2,1,0:T(1,128)}), s32[16,1,256]{2,1,0:T(1,128)S(1)}, u32[]{:S(2)}, u32[]{:S(2)}) async-start(s32[16,1,256]{2,1,0:T(1,128)} %get-tuple-element.30), calls=%async_computation | async-start | bytes 32768 | tf_op jit(solution)/shard_map/all_to_all | solution.py:377
  28.9 45.8 %copy-start.7 = (bf16[320,256]{1,0:T(8,128)(2,1)S(1)}, bf16[320,256]{1,0:T(8,128)(2,1)}, u32[]{:S(2)}) copy-start(bf16[320,256]{1,0:T(8,128)(2,1)} %get-tuple-element.41) | copy-start | bytes 491524
  28.9 71.5 %all-to-all-start.2 = ((bf16[8,576,256]{2,1,0:T(8,128)(2,1)}), bf16[8,576,256]{2,1,0:T(8,128)(2,1)}, u32[]{:S(2)}, u32[]{:S(2)}) async-start(bf16[8,576,256]{2,1,0:T(8,128)(2,1)} %shard_map.68), calls=%async_computation.2 | async-start | bytes 4718592 | tf_op jit(solution)/shard_map/all_to_all | solution.py:386
  34.8 73.6 %copy-start.2 = (bf16[2,128,128]{2,1,0:T(8,128)(2,1)S(1)}, bf16[2,128,128]{2,1,0:T(8,128)(2,1)}, u32[]{:S(2)}) copy-start(bf16[2,128,128]{2,1,0:T(8,128)(2,1)} %right_inv_ref.1) | copy-start | bytes 196612
  34.8 73.6 %copy-start.3 = (bf16[2,32,32]{2,1,0:T(8,128)(2,1)S(1)}, bf16[2,32,32]{2,1,0:T(8,128)(2,1)}, u32[]{:S(2)}) copy-start(bf16[2,32,32]{2,1,0:T(8,128)(2,1)} %left_inv_ref.1) | copy-start | bytes 12292
  34.9 39.8 %collective-permute-start.1 = (bf16[128,2048]{1,0:T(8,128)(2,1)S(1)}, bf16[128,2048]{1,0:T(8,128)(2,1)S(1)}, u32[]{:S(2)}, u32[]{:S(2)}) collective-permute-start(bf16[128,2048]{1,0:T(8,128)(2,1)S(1)} %slice.4), channel_id=1, source_target_pairs={{0,8},{1,9},{2,10},{3,11},{4,12},{5,13},{6,14},{7,15},{8,0},{9,1},... | collective-permute-start | bytes 1572872 | tf_op jit(solution)/shard_map/ppermute | solution.py:374
  74.7 20.9 %collective-permute-start.4 = (bf16[320,256]{1,0:T(8,128)(2,1)S(1)}, bf16[320,256]{1,0:T(8,128)(2,1)S(1)}, u32[]{:S(2)}, u32[]{:S(2)}) collective-permute-start(bf16[320,256]{1,0:T(8,128)(2,1)S(1)} %copy-done.7), channel_id=1, source_target_pairs={{0,10},{1,11},{2,8},{3,9},{4,14},{5,15},{6,12},{7,13},{8,2},{9,3},... | collective-permute-start | bytes 491528 | tf_op jit(solution)/shard_map/ppermute | solution.py:374
  74.9 46.7 %collective-permute-start.2 = (bf16[320,256]{1,0:T(8,128)(2,1)}, bf16[320,256]{1,0:T(8,128)(2,1)}, u32[]{:S(2)}, u32[]{:S(2)}) collective-permute-start(bf16[320,256]{1,0:T(8,128)(2,1)} %get-tuple-element.37), channel_id=1, source_target_pairs={{0,8},{1,9},{2,10},{3,11},{4,12},{5,13},{6,14},{7,15},{8,0},{9,1},... | collective-permute-start | bytes 491528 | tf_op jit(solution)/shard_map/ppermute | solution.py:374
  78.0 55.9 %collective-permute-start.6 = (bf16[320,256]{1,0:T(8,128)(2,1)}, bf16[320,256]{1,0:T(8,128)(2,1)}, u32[]{:S(2)}, u32[]{:S(2)}) collective-permute-start(bf16[320,256]{1,0:T(8,128)(2,1)} %get-tuple-element.45), channel_id=1, source_target_pairs={{0,12},{1,13},{2,14},{3,15},{4,8},{5,9},{6,10},{7,11},{8,4},{9,5},... | collective-permute-start | bytes 491528 | tf_op jit(solution)/shard_map/ppermute | solution.py:374
  78.0 56.0 %collective-permute-start.5 = (bf16[320,256]{1,0:T(8,128)(2,1)}, bf16[320,256]{1,0:T(8,128)(2,1)}, u32[]{:S(2)}, u32[]{:S(2)}) collective-permute-start(bf16[320,256]{1,0:T(8,128)(2,1)} %get-tuple-element.43), channel_id=1, source_target_pairs={{0,11},{1,10},{2,9},{3,8},{4,15},{5,14},{6,13},{7,12},{8,3},{9,2},... | collective-permute-start | bytes 491528 | tf_op jit(solution)/shard_map/ppermute | solution.py:374
  79.3 42.4 %collective-permute-start.3 = (bf16[320,256]{1,0:T(8,128)(2,1)}, bf16[320,256]{1,0:T(8,128)(2,1)}, u32[]{:S(2)}, u32[]{:S(2)}) collective-permute-start(bf16[320,256]{1,0:T(8,128)(2,1)} %get-tuple-element.39), channel_id=1, source_target_pairs={{0,9},{1,8},{2,11},{3,10},{4,13},{5,12},{6,15},{7,14},{8,1},{9,0},... | collective-permute-start | bytes 491528 | tf_op jit(solution)/shard_map/ppermute | solution.py:374
  95.6 0.7 copy-start
  100.5 31.2 %all-to-all-start.1 = ((bf16[8,128,256]{2,1,0:T(8,128)(2,1)}), bf16[8,128,256]{2,1,0:T(8,128)(2,1)}, u32[]{:S(2)}, u32[]{:S(2)}) async-start(bf16[8,128,256]{2,1,0:T(8,128)(2,1)} %shard_map.67), calls=%async_computation.1 | async-start | bytes 1048576 | tf_op jit(solution)/shard_map/all_to_all | solution.py:386
  108.4 13.2 %copy-start.6 = (bf16[320,256]{1,0:T(8,128)(2,1)S(1)}, bf16[320,256]{1,0:T(8,128)(2,1)}, u32[]{:S(2)}) copy-start(bf16[320,256]{1,0:T(8,128)(2,1)} %get-tuple-element.47) | copy-start | bytes 491524
  108.5 13.3 %copy-start.5 = (bf16[320,256]{1,0:T(8,128)(2,1)S(1)}, bf16[320,256]{1,0:T(8,128)(2,1)}, u32[]{:S(2)}) copy-start(bf16[320,256]{1,0:T(8,128)(2,1)} %get-tuple-element.49) | copy-start | bytes 491524
  108.5 15.9 %copy-start.4 = (bf16[320,256]{1,0:T(8,128)(2,1)S(1)}, bf16[320,256]{1,0:T(8,128)(2,1)}, u32[]{:S(2)}) copy-start(bf16[320,256]{1,0:T(8,128)(2,1)} %get-tuple-element.51) | copy-start | bytes 491524
  121.6 17.1 %collective-permute-start.7 = (bf16[320,256]{1,0:T(8,128)(2,1)S(1)}, bf16[320,256]{1,0:T(8,128)(2,1)S(1)}, u32[]{:S(2)}, u32[]{:S(2)}) collective-permute-start(bf16[320,256]{1,0:T(8,128)(2,1)S(1)} %copy-done.6), channel_id=1, source_target_pairs={{0,13},{1,12},{2,15},{3,14},{4,9},{5,8},{6,11},{7,10},{8,5},{9,4},... | collective-permute-start | bytes 491528 | tf_op jit(solution)/shard_map/ppermute | solution.py:374
  121.7 21.1 %collective-permute-start.8 = (bf16[320,256]{1,0:T(8,128)(2,1)S(1)}, bf16[320,256]{1,0:T(8,128)(2,1)S(1)}, u32[]{:S(2)}, u32[]{:S(2)}) collective-permute-start(bf16[320,256]{1,0:T(8,128)(2,1)S(1)} %copy-done.5), channel_id=1, source_target_pairs={{0,14},{1,15},{2,12},{3,13},{4,10},{5,11},{6,8},{7,9},{8,6},{9,7},... | collective-permute-start | bytes 491528 | tf_op jit(solution)/shard_map/ppermute | solution.py:374
  124.3 22.0 %collective-permute-start.9 = (bf16[320,256]{1,0:T(8,128)(2,1)S(1)}, bf16[320,256]{1,0:T(8,128)(2,1)S(1)}, u32[]{:S(2)}, u32[]{:S(2)}) collective-permute-start(bf16[320,256]{1,0:T(8,128)(2,1)S(1)} %copy-done.4), channel_id=1, source_target_pairs={{0,15},{1,14},{2,13},{3,12},{4,11},{5,10},{6,9},{7,8},{8,7},{9,6},... | collective-permute-start | bytes 491528 | tf_op jit(solution)/shard_map/ppermute | solution.py:374
  131.7 14.6 %copy-start.1 = (bf16[320,256]{1,0:T(8,128)(2,1)S(1)}, bf16[320,256]{1,0:T(8,128)(2,1)}, u32[]{:S(2)}) copy-start(bf16[320,256]{1,0:T(8,128)(2,1)} %copy-done) | copy-start | bytes 491524

commit v2 on v0

--- a/solution.py
+++ b/solution.py
@@ -354,7 +354,8 @@
     across = swap(own_tail, half)
     ids = exchange(own_ids)
     table = after(doc_grads, own_ids).T
-    far = list(range(half, devices))
+    quarter = half // 2
+    far = [half, half + 1, *range(half + quarter, devices), *range(half + 2, half + quarter)]
     first, flight = far[:2], 5
     body = [(table, width - tail)]
     ids = after(ids, across)
@@ -362,23 +363,24 @@
     came = {k: swap(pieces[k], k) for k in first}
     ids = after(ids, pieces[far[0]])
     picked = gather_rows(base, ids, [table, across], half)
+    ids = after(ids, picked)
+    pieces.update(zip(far[2:], gather_pieces(me, ids, body, far[2:])))
+    ready = [came[k] for k in first]
     near = lax.all_to_all(
-        picked,
+        after(picked, *ready),
         "docs",
         split_axis=0,
         concat_axis=0,
         axis_index_groups=[list(range(half)), list(range(half, devices))],
         tiled=True,
     )
-    ids = after(ids, picked)
-    pieces.update(zip(far[2:], gather_pieces(me, ids, body, far[2:])))
-    ready = [came[k] for k in first]
     prepared = precondition(after(query_grads, *ready), left_inv, right_inv)
     for i, k in enumerate(far[2:]):
-        before = ready if i < flight else [came[far[2 + i - flight]], prepared]
+        before = ready if i < flight else [*ready, prepared]
         came[k] = swap(after(pieces[k], *before), k)
     total = score_near(base, prepared, near, width, half)
-    return score_pieces(me, prepared, came, total, width, scale)
+    total = score_pieces(me, prepared, {k: came[k] for k in far[:2]}, total, width, 1.0)
+    return score_pieces(me, prepared, {k: came[k] for k in far[2:]}, total, width, scale)
 
 
 def solution(mesh):

time: 139 us -> 127 us (0.914)
  waiting for transfers between devices: 67.5 us -> 50.4 us
  starting transfers between devices: 26.5 us -> 30.1 us
    ppermute x9, waiting for transfers between devices: 61 us -> 43.8 us  [swap(): return lax.ppermute(values, 'docs', [(i, i ^ k) for i in range(devices)])]
    ppermute x9, starting transfers between devices: 18.1 us -> 21.7 us  [swap(): return lax.ppermute(values, 'docs', [(i, i ^ k) for i in range(devices)])]
    pallas_call x1 -> x2, Pallas kernels: 4.55 us -> 5.59 us  [score_pieces(): call(kernel, jax.ShapeDtypeStruct((queries, entries), jnp.float32), (1,),...]
  transfers between devices with their start and end apart: 11 -> 11, of which waited for: 4 -> 7; matrix products, arithmetic and copies ran while one was open for 2% -> 2% of each run, Pallas kernels for 23% -> 27%
where the time goes in v2:
time: 127 us; the launch traced here: 126 us
  waiting for transfers between devices  50.4 us (40%)
  Pallas kernels  41.5 us (33%)
  starting transfers between devices  30.1 us (24%)
  local copies, waits for them, and re-layouts  4.35 us (3%)
    ppermute x9, waiting for transfers between devices, swap(): return lax.ppermute(values, 'docs', [(i, i ^ k) for i in range(devices)])  43.8 us
    ppermute x9, starting transfers between devices, swap(): return lax.ppermute(values, 'docs', [(i, i ^ k) for i in range(devices)])  21.7 us
    pallas_call x1, Pallas kernels, precondition(): call(kernel, jax.ShapeDtypeStruct(queries.shape, queries.dtype), (total /...  13.1 us
    pallas_call x1, Pallas kernels, gather_rows(): call(kernel, pltpu.HBM((count, features, entries), tables[0].dtype), (cou...  8.01 us
    pallas_call x1, Pallas kernels, score_near(): call(kernel, jax.ShapeDtypeStruct((queries, entries), jnp.float32), (coun...  7 us
    all_to_all x1, waiting for transfers between devices, exchange(): lax.all_to_all(values, 'docs', split_axis=0, concat_axis=0, tiled=True)  6.54 us
    pallas_call x2, Pallas kernels, gather_pieces(): call(kernel, [pltpu.HBM((features, entries), tables[0][0].dtype)] * count...  5.77 us
    pallas_call x2, Pallas kernels, score_pieces(): call(kernel, jax.ShapeDtypeStruct((queries, entries), jnp.float32), (1,),...  5.59 us
  transfers between devices with their start and end apart: 11, of which 7 were waited for; matrix products, arithmetic and copies ran while one was open for 2% of the time, Pallas kernels for 27%

profile of v2, /device:TPU:0, one launch (start us, length us, event | category | flops | bytes accessed | tf_op | source)
XLA Modules:
  0.0 126.4 jit_solution(12588732062396374981)
XLA Ops:
  0.0 2.0 %shard_map.64 = (bf16[64,2048]{1,0:T(8,128)(2,1)}, s32[16,1,256]{2,1,0:T(1,128)}) custom-call(bf16[2048,512]{1,0:T(8,128)(2,1)} %docs_hbm.1, s32[1,256]{1,0:T(1,128)} %bitcast.7, s32[1,256]{1,0:T(1,128)} %bitcast.8), custom_call_target="tpu_custom_call" | custom-call | bytes 786432 | tf_op jit(solution)/shard_map/pallas_call | solution.py:63
  2.0 4.1 %collective-permute-start = (bf16[64,2048]{1,0:T(8,128)(2,1)}, bf16[64,2048]{1,0:T(8,128)(2,1)S(1)}, u32[]{:S(2)}, u32[]{:S(2)}) collective-permute-start(bf16[64,2048]{1,0:T(8,128)(2,1)} %get-tuple-element.28), channel_id=1, source_target_pairs={{0,8},{1,9},{2,10},{3,11},{4,12},{5,13},{6,14},{7,15},{8,0},{9,1},... | collective-permute-start | bytes 786440 | tf_op jit(solution)/shard_map/ppermute | solution.py:341
  6.1 3.9 %all-to-all-start = ((s32[16,1,256]{2,1,0:T(1,128)}), s32[16,1,256]{2,1,0:T(1,128)S(1)}, u32[]{:S(2)}, u32[]{:S(2)}) async-start(s32[16,1,256]{2,1,0:T(1,128)} %get-tuple-element.27), calls=%async_computation | async-start | bytes 32768 | tf_op jit(solution)/shard_map/all_to_all | solution.py:344
  10.0 2.9 %copy.7 = bf16[2048,512]{0,1:T(8,128)(2,1)S(1)} copy(bf16[2048,512]{1,0:T(8,128)(2,1)} %docs_hbm.1) | data formatting | bytes 4194304 | tf_op jit(solution)/shard_map/optimization_barrier | solution.py:327
  12.9 6.5 %all-to-all-done.refs_0_.refs_1_.ids_ref.refs_2_.refs_3_.refs_4_.refs_5_ = s32[16,1,256]{2,1,0:T(1,128)S(1)} async-done(((s32[16,1,256]{2,1,0:T(1,128)}), s32[16,1,256]{2,1,0:T(1,128)S(1)}, u32[]{:S(2)}, u32[]{:S(2)}) %all-to-all-start) | async-done | bytes 16416 | tf_op jit(solution)/shard_map/all_to_all | solution.py:344
  19.5 0.0 collective-permute-done.refs_1_
  19.5 2.0 %shard_map.65 = (bf16[448,256]{1,0:T(8,128)(2,1)}, bf16[448,256]{1,0:T(8,128)(2,1)}) custom-call(s32[1]{0:T(128)} %bitcast.me_ref, s32[16,1,256]{2,1,0:T(1,128)S(1)} %all-to-all-done.refs_0_.refs_1_.ids_ref.refs_2_.refs_3_.refs_4_.refs_5_, s32[16,1,256]{2,1,0:T(1,128)S(1)} %all-to-all-done.refs_0_.refs_1_.ids_ref.refs_2_.refs_3_.refs_4_.refs_5_, ...), custom_call_target="tpu_custom_call" | custom-call | flops 939524096 | bytes 2293760 | tf_op jit(solution)/shard_map/pallas_call | solution.py:130
  21.4 2.7 %collective-permute-start.1 = (bf16[448,256]{1,0:T(8,128)(2,1)}, bf16[448,256]{1,0:T(8,128)(2,1)S(1)}, u32[]{:S(2)}, u32[]{:S(2)}) collective-permute-start(bf16[448,256]{1,0:T(8,128)(2,1)} %get-tuple-element.31), channel_id=1, source_target_pairs={{0,8},{1,9},{2,10},{3,11},{4,12},{5,13},{6,14},{7,15},{8,0},{9,1},... | collective-permute-start | bytes 688136 | tf_op jit(solution)/shard_map/ppermute | solution.py:341
  24.1 0.0 collective-permute-start.2
  24.1 8.0 %shard_map.67 = bf16[8,576,256]{2,1,0:T(8,128)(2,1)} custom-call(s32[1]{0:T(128)S(6)} %and.4.base_ref, s32[16,1,256]{2,1,0:T(1,128)S(1)} %all-to-all-done.refs_0_.refs_1_.ids_ref.refs_2_.refs_3_.refs_4_.refs_5_, bf16[512,2048]{1,0:T(8,128)(2,1)S(1)} %bitcast.5, bf16[64,2048]{1,0:T(8,128)(2,1)S(1)} %collective-permute-done.refs_1_), custom_call_target="tpu_custom_call" | custom-call | flops 4831838208 | bytes 4718592 | tf_op jit(solution)/shard_map/pallas_call | solution.py:101
  32.1 3.8 %shard_map.68 = (bf16[448,256]{1,0:T(8,128)(2,1)}, bf16[448,256]{1,0:T(8,128)(2,1)}, bf16[448,256]{1,0:T(8,128)(2,1)}, bf16[448,256]{1,0:T(8,128)(2,1)}, bf16[44...) custom-call(s32[1]{0:T(128)} %bitcast.me_ref, ...), custom_call_target="tpu_custom_call" | custom-call | flops 2818572288 | bytes 3211264 | tf_op jit(solution)/shard_map/pallas_call | solution.py:130
  35.9 8.2 %collective-permute-done.2.refs_3_ = bf16[448,256]{1,0:T(8,128)(2,1)S(1)} collective-permute-done((bf16[448,256]{1,0:T(8,128)(2,1)}, bf16[448,256]{1,0:T(8,128)(2,1)S(1)}, u32[]{:S(2)}, u32[]{:S(2)}) %collective-permute-start.2) | collective-permute-done | bytes 229408 | tf_op jit(solution)/shard_map/ppermute | solution.py:341
  44.1 0.0 copy-start.2
  44.1 0.7 copy-done.2
  44.8 0.0 collective-permute-done.1.refs_2_
  44.8 0.0 copy-start
  44.8 0.7 copy-done
  45.5 0.0 copy-start.4
  45.5 0.0 copy-start.5
  45.5 4.5 %all-to-all-start.1 = ((bf16[8,576,256]{2,1,0:T(8,128)(2,1)}), bf16[8,576,256]{2,1,0:T(8,128)(2,1)}, u32[]{:S(2)}, u32[]{:S(2)}) async-start(bf16[8,576,256]{2,1,0:T(8,128)(2,1)} %shard_map.67), calls=%async_computation.1 | async-start | bytes 4718592 | tf_op jit(solution)/shard_map/all_to_all | solution.py:369
  50.0 3.1 %collective-permute-start.7 = (bf16[448,256]{1,0:T(8,128)(2,1)}, bf16[448,256]{1,0:T(8,128)(2,1)}, u32[]{:S(2)}, u32[]{:S(2)}) collective-permute-start(bf16[448,256]{1,0:T(8,128)(2,1)} %get-tuple-element.45), channel_id=1, source_target_pairs={{0,10},{1,11},{2,8},{3,9},{4,14},{5,15},{6,12},{7,13},{8,2},{9,3},... | collective-permute-start | bytes 688136 | tf_op jit(solution)/shard_map/ppermute | solution.py:341
  53.2 1.5 %collective-permute-start.6 = (bf16[448,256]{1,0:T(8,128)(2,1)}, bf16[448,256]{1,0:T(8,128)(2,1)}, u32[]{:S(2)}, u32[]{:S(2)}) collective-permute-start(bf16[448,256]{1,0:T(8,128)(2,1)} %get-tuple-element.43), channel_id=1, source_target_pairs={{0,15},{1,14},{2,13},{3,12},{4,11},{5,10},{6,9},{7,8},{8,7},{9,6},... | collective-permute-start | bytes 688136 | tf_op jit(solution)/shard_map/ppermute | solution.py:341
  54.7 2.7 %collective-permute-start.5 = (bf16[448,256]{1,0:T(8,128)(2,1)}, bf16[448,256]{1,0:T(8,128)(2,1)}, u32[]{:S(2)}, u32[]{:S(2)}) collective-permute-start(bf16[448,256]{1,0:T(8,128)(2,1)} %get-tuple-element.41), channel_id=1, source_target_pairs={{0,14},{1,15},{2,12},{3,13},{4,10},{5,11},{6,8},{7,9},{8,6},{9,7},... | collective-permute-start | bytes 688136 | tf_op jit(solution)/shard_map/ppermute | solution.py:341
  57.4 2.0 %collective-permute-start.4 = (bf16[448,256]{1,0:T(8,128)(2,1)}, bf16[448,256]{1,0:T(8,128)(2,1)}, u32[]{:S(2)}, u32[]{:S(2)}) collective-permute-start(bf16[448,256]{1,0:T(8,128)(2,1)} %get-tuple-element.39), channel_id=1, source_target_pairs={{0,13},{1,12},{2,15},{3,14},{4,9},{5,8},{6,11},{7,10},{8,5},{9,4},... | collective-permute-start | bytes 688136 | tf_op jit(solution)/shard_map/ppermute | solution.py:341
  59.4 1.8 %collective-permute-start.3 = (bf16[448,256]{1,0:T(8,128)(2,1)}, bf16[448,256]{1,0:T(8,128)(2,1)}, u32[]{:S(2)}, u32[]{:S(2)}) collective-permute-start(bf16[448,256]{1,0:T(8,128)(2,1)} %get-tuple-element.37), channel_id=1, source_target_pairs={{0,12},{1,13},{2,14},{3,15},{4,8},{5,9},{6,10},{7,11},{8,4},{9,5},... | collective-permute-start | bytes 688136 | tf_op jit(solution)/shard_map/ppermute | solution.py:341
  61.1 0.0 copy-done.4
  61.1 0.0 copy-done.5
  61.1 0.0 copy-start.6
  61.2 13.1 %shard_map.66.own_ref.far_ref.refs_0_.refs_1_.refs_2_.refs_3_.refs_4_.refs_5_ = bf16[512,8192]{1,0:T(8,128)(2,1)} custom-call(bf16[512,8192]{1,0:T(8,128)(2,1)} %queries_ref, bf16[2,32,32]{2,1,0:T(8,128)(2,1)S(1)} %copy-done.5, bf16[2,128,128]{2,1,0:T(8,128)(2,1)S(1)} %copy-done.4), custom_call_target="tpu_custom_call" | custom-call | flops 167772160000 | bytes 16777216 | tf_op jit(solution)/shard_map/pallas_call | solution.py:306
  74.3 0.0 copy-start.1
  74.3 0.0 copy-start.3
  74.3 12.4 %collective-permute-done.7.refs_10_ = bf16[448,256]{1,0:T(8,128)(2,1)} collective-permute-done((bf16[448,256]{1,0:T(8,128)(2,1)}, bf16[448,256]{1,0:T(8,128)(2,1)}, u32[]{:S(2)}, u32[]{:S(2)}) %collective-permute-start.7) | collective-permute-done | bytes 229408 | tf_op jit(solution)/shard_map/ppermute | solution.py:341
  86.7 0.0 copy-done.6
  86.7 3.8 %collective-permute-start.8 = (bf16[448,256]{1,0:T(8,128)(2,1)S(1)}, bf16[448,256]{1,0:T(8,128)(2,1)S(1)}, u32[]{:S(2)}, u32[]{:S(2)}) collective-permute-start(bf16[448,256]{1,0:T(8,128)(2,1)S(1)} %copy-done.6), channel_id=1, source_target_pairs={{0,11},{1,10},{2,9},{3,8},{4,15},{5,14},{6,13},{7,12},{8,3},{9,2},... | collective-permute-start | bytes 688136 | tf_op jit(solution)/shard_map/ppermute | solution.py:341
  90.5 0.0 all-to-all-done.1.chosen_ref
  90.5 7.0 %shard_map.69.refs_4_ = f32[512,256]{1,0:T(8,128)S(1)} custom-call(s32[1]{0:T(128)S(6)} %and.4.base_ref, bf16[512,8192]{1,0:T(8,128)(2,1)} %shard_map.66.own_ref.far_ref.refs_0_.refs_1_.refs_2_.refs_3_.refs_4_.refs_5_, bf16[512,8192]{1,0:T(8,128)(2,1)} %shard_map.66.own_ref.far_ref.refs_0_.refs_1_.refs_2_.refs_3_.refs_4_.refs_5_, ...), custom_call_target="tpu_custom_call" | custom-call | flops 1207959552 | bytes 7602176 | tf_op jit(solution)/shard_map/pallas_call | solution.py:193
  97.5 0.0 copy-done.1
  97.5 0.0 copy-done.3
  97.6 1.6 %shard_map.70.refs_12_ = f32[512,256]{1,0:T(8,128)S(1)} custom-call(s32[1]{0:T(128)} %bitcast.me_ref, bf16[512,8192]{1,0:T(8,128)(2,1)} %shard_map.66.own_ref.far_ref.refs_0_.refs_1_.refs_2_.refs_3_.refs_4_.refs_5_, bf16[512,8192]{1,0:T(8,128)(2,1)} %shard_map.66.own_ref.far_ref.refs_0_.refs_1_.refs_2_.refs_3_.refs_4_.refs_5_, ...), custom_call_target="tpu_custom_call" | custom-call | flops 234881024 | bytes 2424832 | tf_op jit(solution)/shard_map/pallas_call | solution.py:160
  99.2 0.0 collective-permute-done.6.refs_9_
  99.2 2.4 %collective-permute-done.5.refs_8_ = bf16[448,256]{1,0:T(8,128)(2,1)} collective-permute-done((bf16[448,256]{1,0:T(8,128)(2,1)}, bf16[448,256]{1,0:T(8,128)(2,1)}, u32[]{:S(2)}, u32[]{:S(2)}) %collective-permute-start.5) | collective-permute-done | bytes 229408 | tf_op jit(solution)/shard_map/ppermute | solution.py:341
  101.6 4.3 %collective-permute-done.4.refs_7_ = bf16[448,256]{1,0:T(8,128)(2,1)} collective-permute-done((bf16[448,256]{1,0:T(8,128)(2,1)}, bf16[448,256]{1,0:T(8,128)(2,1)}, u32[]{:S(2)}, u32[]{:S(2)}) %collective-permute-start.4) | collective-permute-done | bytes 229408 | tf_op jit(solution)/shard_map/ppermute | solution.py:341
  105.8 5.9 %collective-permute-done.3.refs_6_ = bf16[448,256]{1,0:T(8,128)(2,1)} collective-permute-done((bf16[448,256]{1,0:T(8,128)(2,1)}, bf16[448,256]{1,0:T(8,128)(2,1)}, u32[]{:S(2)}, u32[]{:S(2)}) %collective-permute-start.3) | collective-permute-done | bytes 229408 | tf_op jit(solution)/shard_map/ppermute | solution.py:341
  111.8 10.7 %collective-permute-done.8.refs_11_ = bf16[448,256]{1,0:T(8,128)(2,1)S(1)} collective-permute-done((bf16[448,256]{1,0:T(8,128)(2,1)S(1)}, bf16[448,256]{1,0:T(8,128)(2,1)S(1)}, u32[]{:S(2)}, u32[]{:S(2)}) %collective-permute-start.8) | collective-permute-done | bytes 229408 | tf_op jit(solution)/shard_map/ppermute | solution.py:341
  122.5 4.0 %shard_map.71 = f32[512,256]{1,0:T(8,128)} custom-call(s32[1]{0:T(128)} %bitcast.me_ref, bf16[512,8192]{1,0:T(8,128)(2,1)} %shard_map.66.own_ref.far_ref.refs_0_.refs_1_.refs_2_.refs_3_.refs_4_.refs_5_, bf16[512,8192]{1,0:T(8,128)(2,1)} %shard_map.66.own_ref.far_ref.refs_0_.refs_1_.refs_2_.refs_3_.refs_4_.refs_5_, ...), custom_call_target="tpu_custom_call" | custom-call | flops 704643072 | bytes 5177344 | tf_op jit(solution)/shard_map/pallas_call | solution.py:160
Async XLA Ops:
  2.0 17.5 %collective-permute-start = (bf16[64,2048]{1,0:T(8,128)(2,1)}, bf16[64,2048]{1,0:T(8,128)(2,1)S(1)}, u32[]{:S(2)}, u32[]{:S(2)}) collective-permute-start(bf16[64,2048]{1,0:T(8,128)(2,1)} %get-tuple-element.28), channel_id=1, source_target_pairs={{0,8},{1,9},{2,10},{3,11},{4,12},{5,13},{6,14},{7,15},{8,0},{9,1},... | collective-permute-start | bytes 786440 | tf_op jit(solution)/shard_map/ppermute | solution.py:341
  6.1 13.4 %all-to-all-start = ((s32[16,1,256]{2,1,0:T(1,128)}), s32[16,1,256]{2,1,0:T(1,128)S(1)}, u32[]{:S(2)}, u32[]{:S(2)}) async-start(s32[16,1,256]{2,1,0:T(1,128)} %get-tuple-element.27), calls=%async_computation | async-start | bytes 32768 | tf_op jit(solution)/shard_map/all_to_all | solution.py:344
  21.4 23.3 %collective-permute-start.1 = (bf16[448,256]{1,0:T(8,128)(2,1)}, bf16[448,256]{1,0:T(8,128)(2,1)S(1)}, u32[]{:S(2)}, u32[]{:S(2)}) collective-permute-start(bf16[448,256]{1,0:T(8,128)(2,1)} %get-tuple-element.31), channel_id=1, source_target_pairs={{0,8},{1,9},{2,10},{3,11},{4,12},{5,13},{6,14},{7,15},{8,0},{9,1},... | collective-permute-start | bytes 688136 | tf_op jit(solution)/shard_map/ppermute | solution.py:341
  24.1 20.0 %collective-permute-start.2 = (bf16[448,256]{1,0:T(8,128)(2,1)}, bf16[448,256]{1,0:T(8,128)(2,1)S(1)}, u32[]{:S(2)}, u32[]{:S(2)}) collective-permute-start(bf16[448,256]{1,0:T(8,128)(2,1)} %get-tuple-element.32), channel_id=1, source_target_pairs={{0,9},{1,8},{2,11},{3,10},{4,13},{5,12},{6,15},{7,14},{8,1},{9,0},... | collective-permute-start | bytes 688136 | tf_op jit(solution)/shard_map/ppermute | solution.py:341
  44.1 0.7 copy-start.2
  44.8 0.7 copy-start
  45.5 15.7 %copy-start.4 = (bf16[2,128,128]{2,1,0:T(8,128)(2,1)S(1)}, bf16[2,128,128]{2,1,0:T(8,128)(2,1)}, u32[]{:S(2)}) copy-start(bf16[2,128,128]{2,1,0:T(8,128)(2,1)} %right_inv_ref.1) | copy-start | bytes 196612
  45.5 15.7 %copy-start.5 = (bf16[2,32,32]{2,1,0:T(8,128)(2,1)S(1)}, bf16[2,32,32]{2,1,0:T(8,128)(2,1)}, u32[]{:S(2)}) copy-start(bf16[2,32,32]{2,1,0:T(8,128)(2,1)} %left_inv_ref.1) | copy-start | bytes 12292
  45.5 45.0 %all-to-all-start.1 = ((bf16[8,576,256]{2,1,0:T(8,128)(2,1)}), bf16[8,576,256]{2,1,0:T(8,128)(2,1)}, u32[]{:S(2)}, u32[]{:S(2)}) async-start(bf16[8,576,256]{2,1,0:T(8,128)(2,1)} %shard_map.67), calls=%async_computation.1 | async-start | bytes 4718592 | tf_op jit(solution)/shard_map/all_to_all | solution.py:369
  50.0 36.7 %collective-permute-start.7 = (bf16[448,256]{1,0:T(8,128)(2,1)}, bf16[448,256]{1,0:T(8,128)(2,1)}, u32[]{:S(2)}, u32[]{:S(2)}) collective-permute-start(bf16[448,256]{1,0:T(8,128)(2,1)} %get-tuple-element.45), channel_id=1, source_target_pairs={{0,10},{1,11},{2,8},{3,9},{4,14},{5,15},{6,12},{7,13},{8,2},{9,3},... | collective-permute-start | bytes 688136 | tf_op jit(solution)/shard_map/ppermute | solution.py:341
  53.2 46.0 %collective-permute-start.6 = (bf16[448,256]{1,0:T(8,128)(2,1)}, bf16[448,256]{1,0:T(8,128)(2,1)}, u32[]{:S(2)}, u32[]{:S(2)}) collective-permute-start(bf16[448,256]{1,0:T(8,128)(2,1)} %get-tuple-element.43), channel_id=1, source_target_pairs={{0,15},{1,14},{2,13},{3,12},{4,11},{5,10},{6,9},{7,8},{8,7},{9,6},... | collective-permute-start | bytes 688136 | tf_op jit(solution)/shard_map/ppermute | solution.py:341
  54.7 46.9 %collective-permute-start.5 = (bf16[448,256]{1,0:T(8,128)(2,1)}, bf16[448,256]{1,0:T(8,128)(2,1)}, u32[]{:S(2)}, u32[]{:S(2)}) collective-permute-start(bf16[448,256]{1,0:T(8,128)(2,1)} %get-tuple-element.41), channel_id=1, source_target_pairs={{0,14},{1,15},{2,12},{3,13},{4,10},{5,11},{6,8},{7,9},{8,6},{9,7},... | collective-permute-start | bytes 688136 | tf_op jit(solution)/shard_map/ppermute | solution.py:341
  57.4 48.5 %collective-permute-start.4 = (bf16[448,256]{1,0:T(8,128)(2,1)}, bf16[448,256]{1,0:T(8,128)(2,1)}, u32[]{:S(2)}, u32[]{:S(2)}) collective-permute-start(bf16[448,256]{1,0:T(8,128)(2,1)} %get-tuple-element.39), channel_id=1, source_target_pairs={{0,13},{1,12},{2,15},{3,14},{4,9},{5,8},{6,11},{7,10},{8,5},{9,4},... | collective-permute-start | bytes 688136 | tf_op jit(solution)/shard_map/ppermute | solution.py:341
  59.4 52.4 %collective-permute-start.3 = (bf16[448,256]{1,0:T(8,128)(2,1)}, bf16[448,256]{1,0:T(8,128)(2,1)}, u32[]{:S(2)}, u32[]{:S(2)}) collective-permute-start(bf16[448,256]{1,0:T(8,128)(2,1)} %get-tuple-element.37), channel_id=1, source_target_pairs={{0,12},{1,13},{2,14},{3,15},{4,8},{5,9},{6,10},{7,11},{8,4},{9,5},... | collective-permute-start | bytes 688136 | tf_op jit(solution)/shard_map/ppermute | solution.py:341
  61.1 25.6 %copy-start.6 = (bf16[448,256]{1,0:T(8,128)(2,1)S(1)}, bf16[448,256]{1,0:T(8,128)(2,1)}, u32[]{:S(2)}) copy-start(bf16[448,256]{1,0:T(8,128)(2,1)} %get-tuple-element.47) | copy-start | bytes 688132
  74.3 23.3 %copy-start.1 = (bf16[448,256]{1,0:T(8,128)(2,1)S(1)}, bf16[448,256]{1,0:T(8,128)(2,1)}, u32[]{:S(2)}) copy-start(bf16[448,256]{1,0:T(8,128)(2,1)} %copy-done) | copy-start | bytes 688132
  74.3 23.3 %copy-start.3 = (bf16[448,256]{1,0:T(8,128)(2,1)S(1)}, bf16[448,256]{1,0:T(8,128)(2,1)}, u32[]{:S(2)}) copy-start(bf16[448,256]{1,0:T(8,128)(2,1)} %copy-done.2) | copy-start | bytes 688132
  86.7 35.7 %collective-permute-start.8 = (bf16[448,256]{1,0:T(8,128)(2,1)S(1)}, bf16[448,256]{1,0:T(8,128)(2,1)S(1)}, u32[]{:S(2)}, u32[]{:S(2)}) collective-permute-start(bf16[448,256]{1,0:T(8,128)(2,1)S(1)} %copy-done.6), channel_id=1, source_target_pairs={{0,11},{1,10},{2,9},{3,8},{4,15},{5,14},{6,13},{7,12},{8,3},{9,2},... | collective-permute-start | bytes 688136 | tf_op jit(solution)/shard_map/ppermute | solution.py:341

commit v3 on v0

--- a/solution.py
+++ b/solution.py
@@ -105,8 +105,8 @@
         [pl.BlockSpec((1, 1, entries), lambda b, base: (base[0] + b, 0, 0))]
         + [pl.BlockSpec(t.shape, lambda b, base: (0, 0)) for t in tables],
         pl.BlockSpec((1, features, entries), lambda b, base: (b, 0, 0)),
-        2 * count * features * docs * entries,
-        2 * features * (docs + count * entries),
+        1000,
+        1000,
         prefetch=1,
     )(base, ids, *tables)
 
@@ -134,8 +134,8 @@
         [pl.BlockSpec((1, 1, entries), lambda i, me, k=k: (me[0] ^ k, 0, 0)) for k in partners]
         + [pl.BlockSpec((rows, docs), lambda i, me: (0, 0)) for _, rows in tables],
         [pl.BlockSpec((features, entries), lambda i, me: (0, 0))] * count,
-        2 * count * features * docs * entries,
-        2 * features * (docs + count * entries),
+        1000,
+        1000,
         prefetch=1,
     )(me, *[ids] * count, *[table for table, _ in tables])
 
@@ -354,13 +354,16 @@
     across = swap(own_tail, half)
     ids = exchange(own_ids)
     table = after(doc_grads, own_ids).T
-    far = list(range(half, devices))
-    first, flight = far[:2], 5
+    quarter = half // 2
+    far = [half, half + 1, *range(half + quarter, devices), *range(half + 2, half + quarter)]
+    first, second, third = far[:2], far[2 : 2 + quarter], far[2 + quarter :]
     body = [(table, width - tail)]
     ids = after(ids, across)
     pieces = dict(zip(far, gather_pieces(me, ids, body, first)))
     came = {k: swap(pieces[k], k) for k in first}
-    ids = after(ids, pieces[far[0]])
+    ids = after(ids, pieces[first[0]])
+    pieces.update(zip(far[2:], gather_pieces(me, ids, body, far[2:])))
+    ids = after(ids, pieces[second[0]])
     picked = gather_rows(base, ids, [table, across], half)
     near = lax.all_to_all(
         picked,
@@ -370,15 +373,15 @@
         axis_index_groups=[list(range(half)), list(range(half, devices))],
         tiled=True,
     )
-    ids = after(ids, picked)
-    pieces.update(zip(far[2:], gather_pieces(me, ids, body, far[2:])))
     ready = [came[k] for k in first]
     prepared = precondition(after(query_grads, *ready), left_inv, right_inv)
-    for i, k in enumerate(far[2:]):
-        before = ready if i < flight else [came[far[2 + i - flight]], prepared]
-        came[k] = swap(after(pieces[k], *before), k)
+    for k in second:
+        came[k] = swap(after(pieces[k], *ready), k)
+    for k, earlier in zip(third, second[::-1]):
+        came[k] = swap(after(pieces[k], came[earlier], prepared), k)
     total = score_near(base, prepared, near, width, half)
-    return score_pieces(me, prepared, came, total, width, scale)
+    total = score_pieces(me, prepared, {k: came[k] for k in first}, total, width, 1.0)
+    return score_pieces(me, prepared, {k: came[k] for k in second + third}, total, width, scale)
 
 
 def solution(mesh):

time: 139 us -> 121 us (0.87)
  waiting for transfers between devices: 67.5 us -> 50.6 us
    ppermute x9, waiting for transfers between devices: 61 us -> 44.1 us  [swap(): return lax.ppermute(values, 'docs', [(i, i ^ k) for i in range(devices)])]
    pallas_call x1 -> x2, Pallas kernels: 4.55 us -> 5.53 us  [score_pieces(): call(kernel, jax.ShapeDtypeStruct((queries, entries), jnp.float32), (1,),...]
  transfers between devices with their start and end apart: 11 -> 11, of which waited for: 4 -> 5; matrix products, arithmetic and copies ran while one was open for 2% -> 2% of each run, Pallas kernels for 23% -> 28%
where the time goes in v3:
time: 121 us
  waiting for transfers between devices  50.6 us (42%)
  Pallas kernels  41.3 us (34%)
  starting transfers between devices  25.5 us (21%)
  local copies, waits for them, and re-layouts  2.95 us (2%)
    ppermute x9, waiting for transfers between devices, swap(): return lax.ppermute(values, 'docs', [(i, i ^ k) for i in range(devices)])  44.1 us
    ppermute x9, starting transfers between devices, swap(): return lax.ppermute(values, 'docs', [(i, i ^ k) for i in range(devices)])  17.1 us
    pallas_call x1, Pallas kernels, precondition(): call(kernel, jax.ShapeDtypeStruct(queries.shape, queries.dtype), (total /...  13.1 us
    pallas_call x1, Pallas kernels, gather_rows(): call(kernel, pltpu.HBM((count, features, entries), tables[0].dtype), (cou...  8.02 us
    pallas_call x1, Pallas kernels, score_near(): call(kernel, jax.ShapeDtypeStruct((queries, entries), jnp.float32), (coun...  7 us
    all_to_all x1, waiting for transfers between devices, exchange(): lax.all_to_all(values, 'docs', split_axis=0, concat_axis=0, tiled=True)  6.54 us
    pallas_call x2, Pallas kernels, gather_pieces(): call(kernel, [pltpu.HBM((features, entries), tables[0][0].dtype)] * count...  5.71 us
    pallas_call x2, Pallas kernels, score_pieces(): call(kernel, jax.ShapeDtypeStruct((queries, entries), jnp.float32), (1,),...  5.53 us
  transfers between devices with their start and end apart: 11, of which 5 were waited for; matrix products, arithmetic and copies ran while one was open for 2% of the time, Pallas kernels for 28%

profile of v3, /device:TPU:0, one launch (start us, length us, event | category | flops | bytes accessed | tf_op | source)
XLA Modules:
  0.0 120.5 jit_solution(2419459089503458447)
XLA Ops:
  0.0 2.0 %shard_map.64 = (bf16[64,2048]{1,0:T(8,128)(2,1)}, s32[16,1,256]{2,1,0:T(1,128)}) custom-call(bf16[2048,512]{1,0:T(8,128)(2,1)} %docs_hbm.1, s32[1,256]{1,0:T(1,128)} %bitcast.7, s32[1,256]{1,0:T(1,128)} %bitcast.8), custom_call_target="tpu_custom_call" | custom-call | bytes 786432 | tf_op jit(solution)/shard_map/pallas_call | solution.py:63
  2.0 4.1 %collective-permute-start = (bf16[64,2048]{1,0:T(8,128)(2,1)}, bf16[64,2048]{1,0:T(8,128)(2,1)S(1)}, u32[]{:S(2)}, u32[]{:S(2)}) collective-permute-start(bf16[64,2048]{1,0:T(8,128)(2,1)} %get-tuple-element.27), channel_id=1, source_target_pairs={{0,8},{1,9},{2,10},{3,11},{4,12},{5,13},{6,14},{7,15},{8,0},{9,1},... | collective-permute-start | bytes 786440 | tf_op jit(solution)/shard_map/ppermute | solution.py:341
  6.1 3.9 %all-to-all-start = ((s32[16,1,256]{2,1,0:T(1,128)}), s32[16,1,256]{2,1,0:T(1,128)S(1)}, u32[]{:S(2)}, u32[]{:S(2)}) async-start(s32[16,1,256]{2,1,0:T(1,128)} %get-tuple-element.26), calls=%async_computation | async-start | bytes 32768 | tf_op jit(solution)/shard_map/all_to_all | solution.py:344
  10.0 2.9 %copy.7 = bf16[2048,512]{0,1:T(8,128)(2,1)S(1)} copy(bf16[2048,512]{1,0:T(8,128)(2,1)} %docs_hbm.1) | data formatting | bytes 4194304 | tf_op jit(solution)/shard_map/optimization_barrier | solution.py:327
  12.9 6.5 %all-to-all-done.refs_0_.refs_1_.refs_2_.refs_3_.refs_4_.refs_5_.ids_ref = s32[16,1,256]{2,1,0:T(1,128)S(1)} async-done(((s32[16,1,256]{2,1,0:T(1,128)}), s32[16,1,256]{2,1,0:T(1,128)S(1)}, u32[]{:S(2)}, u32[]{:S(2)}) %all-to-all-start) | async-done | bytes 16416 | tf_op jit(solution)/shard_map/all_to_all | solution.py:344
  19.5 0.0 collective-permute-done.refs_1_
  19.5 1.9 %shard_map.65 = (bf16[448,256]{1,0:T(8,128)(2,1)}, bf16[448,256]{1,0:T(8,128)(2,1)}) custom-call(s32[1]{0:T(128)} %bitcast.me_ref, s32[16,1,256]{2,1,0:T(1,128)S(1)} %all-to-all-done.refs_0_.refs_1_.refs_2_.refs_3_.refs_4_.refs_5_.ids_ref, s32[16,1,256]{2,1,0:T(1,128)S(1)} %all-to-all-done.refs_0_.refs_1_.refs_2_.refs_3_.refs_4_.refs_5_.ids_ref, ...), custom_call_target="tpu_custom_call" | custom-call | flops 1000 | bytes 1000 | tf_op jit(solution)/shard_map/pallas_call | solution.py:130
  21.4 2.2 %collective-permute-start.2 = (bf16[448,256]{1,0:T(8,128)(2,1)}, bf16[448,256]{1,0:T(8,128)(2,1)S(1)}, u32[]{:S(2)}, u32[]{:S(2)}) collective-permute-start(bf16[448,256]{1,0:T(8,128)(2,1)} %get-tuple-element.31), channel_id=1, source_target_pairs={{0,9},{1,8},{2,11},{3,10},{4,13},{5,12},{6,15},{7,14},{8,1},{9,0},... | collective-permute-start | bytes 688136 | tf_op jit(solution)/shard_map/ppermute | solution.py:341
  23.6 0.5 collective-permute-start.1
  24.1 3.8 %shard_map.67 = (bf16[448,256]{1,0:T(8,128)(2,1)}, bf16[448,256]{1,0:T(8,128)(2,1)}, bf16[448,256]{1,0:T(8,128)(2,1)}, bf16[448,256]{1,0:T(8,128)(2,1)}, bf16[44...) custom-call(s32[1]{0:T(128)} %bitcast.me_ref, ...), custom_call_target="tpu_custom_call" | custom-call | flops 1000 | bytes 1000 | tf_op jit(solution)/shard_map/pallas_call | solution.py:130
  27.9 8.0 %shard_map.68 = bf16[8,576,256]{2,1,0:T(8,128)(2,1)} custom-call(s32[1]{0:T(128)S(6)} %and.4.base_ref, s32[16,1,256]{2,1,0:T(1,128)S(1)} %all-to-all-done.refs_0_.refs_1_.refs_2_.refs_3_.refs_4_.refs_5_.ids_ref, bf16[512,2048]{1,0:T(8,128)(2,1)S(1)} %bitcast.6, bf16[64,2048]{1,0:T(8,128)(2,1)S(1)} %collective-permute-done.refs_1_), custom_call_target="tpu_custom_call" | custom-call | flops 1000 | bytes 1000 | tf_op jit(solution)/shard_map/pallas_call | solution.py:101
  35.9 0.0 copy-start
  35.9 0.0 copy-start.1
  35.9 4.5 %all-to-all-start.1 = ((bf16[8,576,256]{2,1,0:T(8,128)(2,1)}), bf16[8,576,256]{2,1,0:T(8,128)(2,1)}, u32[]{:S(2)}, u32[]{:S(2)}) async-start(bf16[8,576,256]{2,1,0:T(8,128)(2,1)} %shard_map.68), calls=%async_computation.1 | async-start | bytes 4718592 | tf_op jit(solution)/shard_map/all_to_all | solution.py:368
  40.4 0.0 collective-permute-done.2.refs_3_
  40.5 4.8 %collective-permute-done.1.refs_2_ = bf16[448,256]{1,0:T(8,128)(2,1)S(1)} collective-permute-done((bf16[448,256]{1,0:T(8,128)(2,1)}, bf16[448,256]{1,0:T(8,128)(2,1)S(1)}, u32[]{:S(2)}, u32[]{:S(2)}) %collective-permute-start.1) | collective-permute-done | bytes 229408 | tf_op jit(solution)/shard_map/ppermute | solution.py:341
  45.3 3.5 %collective-permute-start.3 = (bf16[448,256]{1,0:T(8,128)(2,1)}, bf16[448,256]{1,0:T(8,128)(2,1)}, u32[]{:S(2)}, u32[]{:S(2)}) collective-permute-start(bf16[448,256]{1,0:T(8,128)(2,1)} %get-tuple-element.35), channel_id=1, source_target_pairs={{0,12},{1,13},{2,14},{3,15},{4,8},{5,9},{6,10},{7,11},{8,4},{9,5},... | collective-permute-start | bytes 688136 | tf_op jit(solution)/shard_map/ppermute | solution.py:341
  48.8 0.0 collective-permute-start.6
  48.8 3.9 %collective-permute-start.5 = (bf16[448,256]{1,0:T(8,128)(2,1)}, bf16[448,256]{1,0:T(8,128)(2,1)}, u32[]{:S(2)}, u32[]{:S(2)}) collective-permute-start(bf16[448,256]{1,0:T(8,128)(2,1)} %get-tuple-element.39), channel_id=1, source_target_pairs={{0,14},{1,15},{2,12},{3,13},{4,10},{5,11},{6,8},{7,9},{8,6},{9,7},... | collective-permute-start | bytes 688136 | tf_op jit(solution)/shard_map/ppermute | solution.py:341
  52.7 0.6 collective-permute-start.4
  53.2 0.0 copy-done
  53.2 0.0 copy-done.1
  53.3 0.0 copy-start.3
  53.3 0.0 copy-start.2
  53.3 13.1 %shard_map.66.own_ref.far_ref.refs_0_.refs_1_.refs_2_.refs_3_.refs_4_.refs_5_ = bf16[512,8192]{1,0:T(8,128)(2,1)} custom-call(bf16[512,8192]{1,0:T(8,128)(2,1)} %queries_ref, bf16[2,32,32]{2,1,0:T(8,128)(2,1)S(1)} %copy-done.1, bf16[2,128,128]{2,1,0:T(8,128)(2,1)S(1)} %copy-done), custom_call_target="tpu_custom_call" | custom-call | flops 167772160000 | bytes 16777216 | tf_op jit(solution)/shard_map/pallas_call | solution.py:306
  66.4 26.3 %collective-permute-done.5.refs_8_ = bf16[448,256]{1,0:T(8,128)(2,1)} collective-permute-done((bf16[448,256]{1,0:T(8,128)(2,1)}, bf16[448,256]{1,0:T(8,128)(2,1)}, u32[]{:S(2)}, u32[]{:S(2)}) %collective-permute-start.5) | collective-permute-done | bytes 229408 | tf_op jit(solution)/shard_map/ppermute | solution.py:341
  92.7 0.0 collective-permute-done.6.refs_9_
  92.7 0.0 copy-done.3
  92.7 0.0 collective-permute-start.7
  92.7 0.0 copy-done.2
  92.7 2.3 %collective-permute-start.8 = (bf16[448,256]{1,0:T(8,128)(2,1)S(1)}, bf16[448,256]{1,0:T(8,128)(2,1)S(1)}, u32[]{:S(2)}, u32[]{:S(2)}) collective-permute-start(bf16[448,256]{1,0:T(8,128)(2,1)S(1)} %copy-done.2), channel_id=1, source_target_pairs={{0,11},{1,10},{2,9},{3,8},{4,15},{5,14},{6,13},{7,12},{8,3},{9,2},... | collective-permute-start | bytes 688136 | tf_op jit(solution)/shard_map/ppermute | solution.py:341
  95.0 0.0 all-to-all-done.1.chosen_ref
  95.0 7.0 %shard_map.69.refs_4_ = f32[512,256]{1,0:T(8,128)S(1)} custom-call(s32[1]{0:T(128)S(6)} %and.4.base_ref, bf16[512,8192]{1,0:T(8,128)(2,1)} %shard_map.66.own_ref.far_ref.refs_0_.refs_1_.refs_2_.refs_3_.refs_4_.refs_5_, bf16[512,8192]{1,0:T(8,128)(2,1)} %shard_map.66.own_ref.far_ref.refs_0_.refs_1_.refs_2_.refs_3_.refs_4_.refs_5_, ...), custom_call_target="tpu_custom_call" | custom-call | flops 1207959552 | bytes 7602176 | tf_op jit(solution)/shard_map/pallas_call | solution.py:193
  102.1 1.6 %shard_map.70.refs_12_ = f32[512,256]{1,0:T(8,128)S(1)} custom-call(s32[1]{0:T(128)} %bitcast.me_ref, bf16[512,8192]{1,0:T(8,128)(2,1)} %shard_map.66.own_ref.far_ref.refs_0_.refs_1_.refs_2_.refs_3_.refs_4_.refs_5_, bf16[512,8192]{1,0:T(8,128)(2,1)} %shard_map.66.own_ref.far_ref.refs_0_.refs_1_.refs_2_.refs_3_.refs_4_.refs_5_, ...), custom_call_target="tpu_custom_call" | custom-call | flops 234881024 | bytes 2424832 | tf_op jit(solution)/shard_map/pallas_call | solution.py:160
  103.7 0.0 collective-permute-done.3.refs_6_
  103.7 0.0 collective-permute-done.4.refs_7_
  103.7 8.2 %collective-permute-done.7.refs_10_ = bf16[448,256]{1,0:T(8,128)(2,1)S(1)} collective-permute-done((bf16[448,256]{1,0:T(8,128)(2,1)S(1)}, bf16[448,256]{1,0:T(8,128)(2,1)S(1)}, u32[]{:S(2)}, u32[]{:S(2)}) %collective-permute-start.7) | collective-permute-done | bytes 229408 | tf_op jit(solution)/shard_map/ppermute | solution.py:341
  111.9 4.7 %collective-permute-done.8.refs_11_ = bf16[448,256]{1,0:T(8,128)(2,1)S(1)} collective-permute-done((bf16[448,256]{1,0:T(8,128)(2,1)S(1)}, bf16[448,256]{1,0:T(8,128)(2,1)S(1)}, u32[]{:S(2)}, u32[]{:S(2)}) %collective-permute-start.8) | collective-permute-done | bytes 229408 | tf_op jit(solution)/shard_map/ppermute | solution.py:341
  116.6 3.9 %shard_map.71 = f32[512,256]{1,0:T(8,128)} custom-call(s32[1]{0:T(128)} %bitcast.me_ref, bf16[512,8192]{1,0:T(8,128)(2,1)} %shard_map.66.own_ref.far_ref.refs_0_.refs_1_.refs_2_.refs_3_.refs_4_.refs_5_, bf16[512,8192]{1,0:T(8,128)(2,1)} %shard_map.66.own_ref.far_ref.refs_0_.refs_1_.refs_2_.refs_3_.refs_4_.refs_5_, ...), custom_call_target="tpu_custom_call" | custom-call | flops 704643072 | bytes 5177344 | tf_op jit(solution)/shard_map/pallas_call | solution.py:160
Async XLA Ops:
  2.0 17.5 %collective-permute-start = (bf16[64,2048]{1,0:T(8,128)(2,1)}, bf16[64,2048]{1,0:T(8,128)(2,1)S(1)}, u32[]{:S(2)}, u32[]{:S(2)}) collective-permute-start(bf16[64,2048]{1,0:T(8,128)(2,1)} %get-tuple-element.27), channel_id=1, source_target_pairs={{0,8},{1,9},{2,10},{3,11},{4,12},{5,13},{6,14},{7,15},{8,0},{9,1},... | collective-permute-start | bytes 786440 | tf_op jit(solution)/shard_map/ppermute | solution.py:341
  6.1 13.4 %all-to-all-start = ((s32[16,1,256]{2,1,0:T(1,128)}), s32[16,1,256]{2,1,0:T(1,128)S(1)}, u32[]{:S(2)}, u32[]{:S(2)}) async-start(s32[16,1,256]{2,1,0:T(1,128)} %get-tuple-element.26), calls=%async_computation | async-start | bytes 32768 | tf_op jit(solution)/shard_map/all_to_all | solution.py:344
  21.4 19.0 %collective-permute-start.2 = (bf16[448,256]{1,0:T(8,128)(2,1)}, bf16[448,256]{1,0:T(8,128)(2,1)S(1)}, u32[]{:S(2)}, u32[]{:S(2)}) collective-permute-start(bf16[448,256]{1,0:T(8,128)(2,1)} %get-tuple-element.31), channel_id=1, source_target_pairs={{0,9},{1,8},{2,11},{3,10},{4,13},{5,12},{6,15},{7,14},{8,1},{9,0},... | collective-permute-start | bytes 688136 | tf_op jit(solution)/shard_map/ppermute | solution.py:341
  23.6 21.7 %collective-permute-start.1 = (bf16[448,256]{1,0:T(8,128)(2,1)}, bf16[448,256]{1,0:T(8,128)(2,1)S(1)}, u32[]{:S(2)}, u32[]{:S(2)}) collective-permute-start(bf16[448,256]{1,0:T(8,128)(2,1)} %get-tuple-element.30), channel_id=1, source_target_pairs={{0,8},{1,9},{2,10},{3,11},{4,12},{5,13},{6,14},{7,15},{8,0},{9,1},... | collective-permute-start | bytes 688136 | tf_op jit(solution)/shard_map/ppermute | solution.py:341
  35.9 17.3 %copy-start = (bf16[2,128,128]{2,1,0:T(8,128)(2,1)S(1)}, bf16[2,128,128]{2,1,0:T(8,128)(2,1)}, u32[]{:S(2)}) copy-start(bf16[2,128,128]{2,1,0:T(8,128)(2,1)} %right_inv_ref.1) | copy-start | bytes 196612
  35.9 17.3 %copy-start.1 = (bf16[2,32,32]{2,1,0:T(8,128)(2,1)S(1)}, bf16[2,32,32]{2,1,0:T(8,128)(2,1)}, u32[]{:S(2)}) copy-start(bf16[2,32,32]{2,1,0:T(8,128)(2,1)} %left_inv_ref.1) | copy-start | bytes 12292
  35.9 59.1 %all-to-all-start.1 = ((bf16[8,576,256]{2,1,0:T(8,128)(2,1)}), bf16[8,576,256]{2,1,0:T(8,128)(2,1)}, u32[]{:S(2)}, u32[]{:S(2)}) async-start(bf16[8,576,256]{2,1,0:T(8,128)(2,1)} %shard_map.68), calls=%async_computation.1 | async-start | bytes 4718592 | tf_op jit(solution)/shard_map/all_to_all | solution.py:368
  45.3 58.5 %collective-permute-start.3 = (bf16[448,256]{1,0:T(8,128)(2,1)}, bf16[448,256]{1,0:T(8,128)(2,1)}, u32[]{:S(2)}, u32[]{:S(2)}) collective-permute-start(bf16[448,256]{1,0:T(8,128)(2,1)} %get-tuple-element.35), channel_id=1, source_target_pairs={{0,12},{1,13},{2,14},{3,15},{4,8},{5,9},{6,10},{7,11},{8,4},{9,5},... | collective-permute-start | bytes 688136 | tf_op jit(solution)/shard_map/ppermute | solution.py:341
  48.8 44.0 %collective-permute-start.6 = (bf16[448,256]{1,0:T(8,128)(2,1)}, bf16[448,256]{1,0:T(8,128)(2,1)}, u32[]{:S(2)}, u32[]{:S(2)}) collective-permute-start(bf16[448,256]{1,0:T(8,128)(2,1)} %get-tuple-element.41), channel_id=1, source_target_pairs={{0,15},{1,14},{2,13},{3,12},{4,11},{5,10},{6,9},{7,8},{8,7},{9,6},... | collective-permute-start | bytes 688136 | tf_op jit(solution)/shard_map/ppermute | solution.py:341
  48.8 44.0 %collective-permute-start.5 = (bf16[448,256]{1,0:T(8,128)(2,1)}, bf16[448,256]{1,0:T(8,128)(2,1)}, u32[]{:S(2)}, u32[]{:S(2)}) collective-permute-start(bf16[448,256]{1,0:T(8,128)(2,1)} %get-tuple-element.39), channel_id=1, source_target_pairs={{0,14},{1,15},{2,12},{3,13},{4,10},{5,11},{6,8},{7,9},{8,6},{9,7},... | collective-permute-start | bytes 688136 | tf_op jit(solution)/shard_map/ppermute | solution.py:341
  52.7 51.0 %collective-permute-start.4 = (bf16[448,256]{1,0:T(8,128)(2,1)}, bf16[448,256]{1,0:T(8,128)(2,1)}, u32[]{:S(2)}, u32[]{:S(2)}) collective-permute-start(bf16[448,256]{1,0:T(8,128)(2,1)} %get-tuple-element.37), channel_id=1, source_target_pairs={{0,13},{1,12},{2,15},{3,14},{4,9},{5,8},{6,11},{7,10},{8,5},{9,4},... | collective-permute-start | bytes 688136 | tf_op jit(solution)/shard_map/ppermute | solution.py:341
  53.3 39.5 %copy-start.3 = (bf16[448,256]{1,0:T(8,128)(2,1)S(1)}, bf16[448,256]{1,0:T(8,128)(2,1)}, u32[]{:S(2)}) copy-start(bf16[448,256]{1,0:T(8,128)(2,1)} %get-tuple-element.43) | copy-start | bytes 688132
  53.3 39.5 %copy-start.2 = (bf16[448,256]{1,0:T(8,128)(2,1)S(1)}, bf16[448,256]{1,0:T(8,128)(2,1)}, u32[]{:S(2)}) copy-start(bf16[448,256]{1,0:T(8,128)(2,1)} %get-tuple-element.45) | copy-start | bytes 688132
  92.7 19.2 %collective-permute-start.7 = (bf16[448,256]{1,0:T(8,128)(2,1)S(1)}, bf16[448,256]{1,0:T(8,128)(2,1)S(1)}, u32[]{:S(2)}, u32[]{:S(2)}) collective-permute-start(bf16[448,256]{1,0:T(8,128)(2,1)S(1)} %copy-done.3), channel_id=1, source_target_pairs={{0,10},{1,11},{2,8},{3,9},{4,14},{5,15},{6,12},{7,13},{8,2},{9,3},... | collective-permute-start | bytes 688136 | tf_op jit(solution)/shard_map/ppermute | solution.py:341
  92.7 23.9 %collective-permute-start.8 = (bf16[448,256]{1,0:T(8,128)(2,1)S(1)}, bf16[448,256]{1,0:T(8,128)(2,1)S(1)}, u32[]{:S(2)}, u32[]{:S(2)}) collective-permute-start(bf16[448,256]{1,0:T(8,128)(2,1)S(1)} %copy-done.2), channel_id=1, source_target_pairs={{0,11},{1,10},{2,9},{3,8},{4,15},{5,14},{6,13},{7,12},{8,3},{9,2},... | collective-permute-start | bytes 688136 | tf_op jit(solution)/shard_map/ppermute | solution.py:341

commit v4 on v3

--- a/solution.py
+++ b/solution.py
@@ -355,15 +355,12 @@
     ids = exchange(own_ids)
     table = after(doc_grads, own_ids).T
     quarter = half // 2
-    far = [half, half + 1, *range(half + quarter, devices), *range(half + 2, half + quarter)]
-    first, second, third = far[:2], far[2 : 2 + quarter], far[2 + quarter :]
+    first, second = list(range(half + quarter, devices)), list(range(half, half + quarter))
     body = [(table, width - tail)]
     ids = after(ids, across)
-    pieces = dict(zip(far, gather_pieces(me, ids, body, first)))
+    pieces = dict(zip(first, gather_pieces(me, ids, body, first)))
     came = {k: swap(pieces[k], k) for k in first}
     ids = after(ids, pieces[first[0]])
-    pieces.update(zip(far[2:], gather_pieces(me, ids, body, far[2:])))
-    ids = after(ids, pieces[second[0]])
     picked = gather_rows(base, ids, [table, across], half)
     near = lax.all_to_all(
         picked,
@@ -373,15 +370,17 @@
         axis_index_groups=[list(range(half)), list(range(half, devices))],
         tiled=True,
     )
-    ready = [came[k] for k in first]
-    prepared = precondition(after(query_grads, *ready), left_inv, right_inv)
-    for k in second:
-        came[k] = swap(after(pieces[k], *ready), k)
-    for k, earlier in zip(third, second[::-1]):
-        came[k] = swap(after(pieces[k], came[earlier], prepared), k)
+    ids = after(ids, picked)
+    pieces.update(zip(second, gather_pieces(me, ids, body, second)))
+    prepared = precondition(after(query_grads, *[came[k] for k in first[:2]]), left_inv, right_inv)
+    for i, (k, earlier) in enumerate(zip(second, first)):
+        before = [came[earlier], prepared] if i == quarter - 1 else [came[earlier]]
+        came[k] = swap(after(pieces[k], *before), k)
     total = score_near(base, prepared, near, width, half)
-    total = score_pieces(me, prepared, {k: came[k] for k in first}, total, width, 1.0)
-    return score_pieces(me, prepared, {k: came[k] for k in second + third}, total, width, scale)
+    last = second[quarter // 2 :]
+    others = [k for k in came if k not in last]
+    total = score_pieces(me, prepared, {k: came[k] for k in others}, total, width, 1.0)
+    return score_pieces(me, prepared, {k: came[k] for k in last}, total, width, scale)
 
 
 def solution(mesh):

time: 121 us -> 115 us (0.950)
  waiting for transfers between devices: 50.6 us -> 29.5 us
  starting transfers between devices: 25.5 us -> 40.7 us
    ppermute x9, waiting for transfers between devices: 44.1 us -> 22.9 us  [swap(): return lax.ppermute(values, 'docs', [(i, i ^ k) for i in range(devices)])]
    ppermute x9, starting transfers between devices: 17.1 us -> 32.2 us  [swap(): return lax.ppermute(values, 'docs', [(i, i ^ k) for i in range(devices)])]
  transfers between devices with their start and end apart: 11 -> 11, of which waited for: 5 -> 6; matrix products, arithmetic and copies ran while one was open for 2% -> 3% of each run, Pallas kernels for 28% -> 30%
where the time goes in v4:
time: 115 us; the launch traced here: 114 us
  Pallas kernels  41.3 us (36%)
  starting transfers between devices  40.7 us (35%)
  waiting for transfers between devices  29.5 us (26%)
  local copies, waits for them, and re-layouts  2.94 us (3%)
    ppermute x9, starting transfers between devices, swap(): return lax.ppermute(values, 'docs', [(i, i ^ k) for i in range(devices)])  32.2 us
    ppermute x9, waiting for transfers between devices, swap(): return lax.ppermute(values, 'docs', [(i, i ^ k) for i in range(devices)])  22.9 us
    pallas_call x1, Pallas kernels, precondition(): call(kernel, jax.ShapeDtypeStruct(queries.shape, queries.dtype), (total /...  13.1 us
    pallas_call x1, Pallas kernels, gather_rows(): call(kernel, pltpu.HBM((count, features, entries), tables[0].dtype), (cou...  8.01 us
    pallas_call x1, Pallas kernels, score_near(): call(kernel, jax.ShapeDtypeStruct((queries, entries), jnp.float32), (coun...  7 us
    all_to_all x1, waiting for transfers between devices, exchange(): lax.all_to_all(values, 'docs', split_axis=0, concat_axis=0, tiled=True)  6.54 us
    pallas_call x2, Pallas kernels, gather_pieces(): call(kernel, [pltpu.HBM((features, entries), tables[0][0].dtype)] * count...  5.7 us
    pallas_call x2, Pallas kernels, score_pieces(): call(kernel, jax.ShapeDtypeStruct((queries, entries), jnp.float32), (1,),...  5.51 us
  transfers between devices with their start and end apart: 11, of which 6 were waited for; matrix products, arithmetic and copies ran while one was open for 3% of the time, Pallas kernels for 30%

profile of v4, /device:TPU:0, one launch (start us, length us, event | category | flops | bytes accessed | tf_op | source)
XLA Modules:
  0.0 114.4 jit_solution(2267043082498704592)
XLA Ops:
  0.0 2.0 %shard_map.64 = (bf16[64,2048]{1,0:T(8,128)(2,1)}, s32[16,1,256]{2,1,0:T(1,128)}) custom-call(bf16[2048,512]{1,0:T(8,128)(2,1)} %docs_hbm.1, s32[1,256]{1,0:T(1,128)} %bitcast.7, s32[1,256]{1,0:T(1,128)} %bitcast.8), custom_call_target="tpu_custom_call" | custom-call | bytes 786432 | tf_op jit(solution)/shard_map/pallas_call | solution.py:63
  2.0 4.1 %collective-permute-start = (bf16[64,2048]{1,0:T(8,128)(2,1)}, bf16[64,2048]{1,0:T(8,128)(2,1)S(1)}, u32[]{:S(2)}, u32[]{:S(2)}) collective-permute-start(bf16[64,2048]{1,0:T(8,128)(2,1)} %get-tuple-element.25), channel_id=1, source_target_pairs={{0,8},{1,9},{2,10},{3,11},{4,12},{5,13},{6,14},{7,15},{8,0},{9,1},... | collective-permute-start | bytes 786440 | tf_op jit(solution)/shard_map/ppermute | solution.py:341
  6.1 3.9 %all-to-all-start = ((s32[16,1,256]{2,1,0:T(1,128)}), s32[16,1,256]{2,1,0:T(1,128)S(1)}, u32[]{:S(2)}, u32[]{:S(2)}) async-start(s32[16,1,256]{2,1,0:T(1,128)} %get-tuple-element.24), calls=%async_computation | async-start | bytes 32768 | tf_op jit(solution)/shard_map/all_to_all | solution.py:344
  10.0 2.9 %copy.7 = bf16[2048,512]{0,1:T(8,128)(2,1)S(1)} copy(bf16[2048,512]{1,0:T(8,128)(2,1)} %docs_hbm.1) | data formatting | bytes 4194304 | tf_op jit(solution)/shard_map/optimization_barrier | solution.py:327
  12.9 6.5 %all-to-all-done.refs_0_.refs_1_.refs_2_.refs_3_.ids_ref = s32[16,1,256]{2,1,0:T(1,128)S(1)} async-done(((s32[16,1,256]{2,1,0:T(1,128)}), s32[16,1,256]{2,1,0:T(1,128)S(1)}, u32[]{:S(2)}, u32[]{:S(2)}) %all-to-all-start) | async-done | bytes 16416 | tf_op jit(solution)/shard_map/all_to_all | solution.py:344
  19.5 0.0 collective-permute-done.refs_1_
  19.5 2.9 %shard_map.65 = (bf16[448,256]{1,0:T(8,128)(2,1)}, bf16[448,256]{1,0:T(8,128)(2,1)}, bf16[448,256]{1,0:T(8,128)(2,1)}, bf16[448,256]{1,0:T(8,128)(2,1)}) custom-call(s32[1]{0:T(128)} %bitcast.me_ref, s32[16,1,256]{2,1,0:T(1,128)S(1)} %all-to-all-done.refs_0_.refs_1_.refs_2_.refs_3_.ids_ref, ...), custom_call_target="tpu_custom_call" | custom-call | flops 1000 | bytes 1000 | tf_op jit(solution)/shard_map/pallas_call | solution.py:130
  22.3 3.2 %collective-permute-start.2 = (bf16[448,256]{1,0:T(8,128)(2,1)}, bf16[448,256]{1,0:T(8,128)(2,1)S(1)}, u32[]{:S(2)}, u32[]{:S(2)}) collective-permute-start(bf16[448,256]{1,0:T(8,128)(2,1)} %get-tuple-element.29), channel_id=1, source_target_pairs={{0,13},{1,12},{2,15},{3,14},{4,9},{5,8},{6,11},{7,10},{8,5},{9,4},... | collective-permute-start | bytes 688136 | tf_op jit(solution)/shard_map/ppermute | solution.py:341
  25.6 0.3 collective-permute-start.1
  25.9 3.5 %collective-permute-start.3 = (bf16[448,256]{1,0:T(8,128)(2,1)}, bf16[448,256]{1,0:T(8,128)(2,1)S(1)}, u32[]{:S(2)}, u32[]{:S(2)}) collective-permute-start(bf16[448,256]{1,0:T(8,128)(2,1)} %get-tuple-element.34), channel_id=1, source_target_pairs={{0,14},{1,15},{2,12},{3,13},{4,10},{5,11},{6,8},{7,9},{8,6},{9,7},... | collective-permute-start | bytes 688136 | tf_op jit(solution)/shard_map/ppermute | solution.py:341
  29.4 8.0 %shard_map.67 = bf16[8,576,256]{2,1,0:T(8,128)(2,1)} custom-call(s32[1]{0:T(128)S(6)} %and.4.base_ref, s32[16,1,256]{2,1,0:T(1,128)S(1)} %all-to-all-done.refs_0_.refs_1_.refs_2_.refs_3_.ids_ref, bf16[512,2048]{1,0:T(8,128)(2,1)S(1)} %bitcast.5, bf16[64,2048]{1,0:T(8,128)(2,1)S(1)} %collective-permute-done.refs_1_), custom_call_target="tpu_custom_call" | custom-call | flops 1000 | bytes 1000 | tf_op jit(solution)/shard_map/pallas_call | solution.py:101
  37.4 0.0 copy-start
  37.4 0.0 copy-start.1
  37.4 4.5 %all-to-all-start.1 = ((bf16[8,576,256]{2,1,0:T(8,128)(2,1)}), bf16[8,576,256]{2,1,0:T(8,128)(2,1)}, u32[]{:S(2)}, u32[]{:S(2)}) async-start(bf16[8,576,256]{2,1,0:T(8,128)(2,1)} %shard_map.67), calls=%async_computation.1 | async-start | bytes 4718592 | tf_op jit(solution)/shard_map/all_to_all | solution.py:365
  41.9 0.8 collective-permute-start.5
  42.7 2.8 %shard_map.68 = (bf16[448,256]{1,0:T(8,128)(2,1)}, bf16[448,256]{1,0:T(8,128)(2,1)}, bf16[448,256]{1,0:T(8,128)(2,1)}, bf16[448,256]{1,0:T(8,128)(2,1)}) custom-call(s32[1]{0:T(128)} %bitcast.me_ref, s32[16,1,256]{2,1,0:T(1,128)S(1)} %all-to-all-done.refs_0_.refs_1_.refs_2_.refs_3_.ids_ref, ...), custom_call_target="tpu_custom_call" | custom-call | flops 1000 | bytes 1000 | tf_op jit(solution)/shard_map/pallas_call | solution.py:130
  45.5 0.0 collective-permute-done.2.refs_7_
  45.6 0.0 collective-permute-done.1.refs_6_
  45.6 0.0 collective-permute-done.3.refs_8_
  45.6 15.8 %collective-permute-start.8 = (bf16[448,256]{1,0:T(8,128)(2,1)}, bf16[448,256]{1,0:T(8,128)(2,1)}, u32[]{:S(2)}, u32[]{:S(2)}) collective-permute-start(bf16[448,256]{1,0:T(8,128)(2,1)} %get-tuple-element.42), channel_id=1, source_target_pairs={{0,9},{1,8},{2,11},{3,10},{4,13},{5,12},{6,15},{7,14},{8,1},{9,0},... | collective-permute-start | bytes 688136 | tf_op jit(solution)/shard_map/ppermute | solution.py:341
  61.4 1.8 %collective-permute-start.7 = (bf16[448,256]{1,0:T(8,128)(2,1)}, bf16[448,256]{1,0:T(8,128)(2,1)}, u32[]{:S(2)}, u32[]{:S(2)}) collective-permute-start(bf16[448,256]{1,0:T(8,128)(2,1)} %get-tuple-element.40), channel_id=1, source_target_pairs={{0,8},{1,9},{2,10},{3,11},{4,12},{5,13},{6,14},{7,15},{8,0},{9,1},... | collective-permute-start | bytes 688136 | tf_op jit(solution)/shard_map/ppermute | solution.py:341
  63.2 2.4 %collective-permute-start.4 = (bf16[448,256]{1,0:T(8,128)(2,1)}, bf16[448,256]{1,0:T(8,128)(2,1)}, u32[]{:S(2)}, u32[]{:S(2)}) collective-permute-start(bf16[448,256]{1,0:T(8,128)(2,1)} %get-tuple-element.35), channel_id=1, source_target_pairs={{0,10},{1,11},{2,8},{3,9},{4,14},{5,15},{6,12},{7,13},{8,2},{9,3},... | collective-permute-start | bytes 688136 | tf_op jit(solution)/shard_map/ppermute | solution.py:341
  65.6 0.0 copy-done
  65.7 0.0 copy-done.1
  65.7 0.0 copy-start.2
  65.7 13.1 %shard_map.66.own_ref.far_ref.refs_0_.refs_1_.refs_2_.refs_3_.refs_4_.refs_5_ = bf16[512,8192]{1,0:T(8,128)(2,1)} custom-call(bf16[512,8192]{1,0:T(8,128)(2,1)} %queries_ref, bf16[2,32,32]{2,1,0:T(8,128)(2,1)S(1)} %copy-done.1, bf16[2,128,128]{2,1,0:T(8,128)(2,1)S(1)} %copy-done), custom_call_target="tpu_custom_call" | custom-call | flops 167772160000 | bytes 16777216 | tf_op jit(solution)/shard_map/pallas_call | solution.py:306
  78.7 0.6 collective-permute-done.5.refs_9_
  79.3 0.0 copy-done.2
  79.3 0.2 collective-permute-start.6
  79.5 0.0 all-to-all-done.1.chosen_ref
  79.5 7.0 %shard_map.69.refs_12_ = f32[512,256]{1,0:T(8,128)S(1)} custom-call(s32[1]{0:T(128)S(6)} %and.4.base_ref, bf16[512,8192]{1,0:T(8,128)(2,1)} %shard_map.66.own_ref.far_ref.refs_0_.refs_1_.refs_2_.refs_3_.refs_4_.refs_5_, bf16[512,8192]{1,0:T(8,128)(2,1)} %shard_map.66.own_ref.far_ref.refs_0_.refs_1_.refs_2_.refs_3_.refs_4_.refs_5_, ...), custom_call_target="tpu_custom_call" | custom-call | flops 1207959552 | bytes 7602176 | tf_op jit(solution)/shard_map/pallas_call | solution.py:193
  86.6 10.3 %collective-permute-done.8.refs_11_ = bf16[448,256]{1,0:T(8,128)(2,1)} collective-permute-done((bf16[448,256]{1,0:T(8,128)(2,1)}, bf16[448,256]{1,0:T(8,128)(2,1)}, u32[]{:S(2)}, u32[]{:S(2)}) %collective-permute-start.8) | collective-permute-done | bytes 229408 | tf_op jit(solution)/shard_map/ppermute | solution.py:341
  96.9 6.4 %collective-permute-done.7.refs_10_ = bf16[448,256]{1,0:T(8,128)(2,1)} collective-permute-done((bf16[448,256]{1,0:T(8,128)(2,1)}, bf16[448,256]{1,0:T(8,128)(2,1)}, u32[]{:S(2)}, u32[]{:S(2)}) %collective-permute-start.7) | collective-permute-done | bytes 229408 | tf_op jit(solution)/shard_map/ppermute | solution.py:341
  103.3 3.0 %shard_map.70.refs_4_ = f32[512,256]{1,0:T(8,128)S(1)} custom-call(s32[1]{0:T(128)} %bitcast.me_ref, bf16[512,8192]{1,0:T(8,128)(2,1)} %shard_map.66.own_ref.far_ref.refs_0_.refs_1_.refs_2_.refs_3_.refs_4_.refs_5_, bf16[512,8192]{1,0:T(8,128)(2,1)} %shard_map.66.own_ref.far_ref.refs_0_.refs_1_.refs_2_.refs_3_.refs_4_.refs_5_, ...), custom_call_target="tpu_custom_call" | custom-call | flops 704643072 | bytes 5177344 | tf_op jit(solution)/shard_map/pallas_call | solution.py:160
  106.3 1.9 %collective-permute-done.4.refs_2_ = bf16[448,256]{1,0:T(8,128)(2,1)} collective-permute-done((bf16[448,256]{1,0:T(8,128)(2,1)}, bf16[448,256]{1,0:T(8,128)(2,1)}, u32[]{:S(2)}, u32[]{:S(2)}) %collective-permute-start.4) | collective-permute-done | bytes 229408 | tf_op jit(solution)/shard_map/ppermute | solution.py:341
  108.2 3.8 %collective-permute-done.6.refs_3_ = bf16[448,256]{1,0:T(8,128)(2,1)S(1)} collective-permute-done((bf16[448,256]{1,0:T(8,128)(2,1)S(1)}, bf16[448,256]{1,0:T(8,128)(2,1)S(1)}, u32[]{:S(2)}, u32[]{:S(2)}) %collective-permute-start.6) | collective-permute-done | bytes 229408 | tf_op jit(solution)/shard_map/ppermute | solution.py:341
  111.9 2.5 %shard_map.71 = f32[512,256]{1,0:T(8,128)} custom-call(s32[1]{0:T(128)} %bitcast.me_ref, bf16[512,8192]{1,0:T(8,128)(2,1)} %shard_map.66.own_ref.far_ref.refs_0_.refs_1_.refs_2_.refs_3_.refs_4_.refs_5_, bf16[512,8192]{1,0:T(8,128)(2,1)} %shard_map.66.own_ref.far_ref.refs_0_.refs_1_.refs_2_.refs_3_.refs_4_.refs_5_, ...), custom_call_target="tpu_custom_call" | custom-call | flops 234881024 | bytes 2424832 | tf_op jit(solution)/shard_map/pallas_call | solution.py:160
Async XLA Ops:
  2.0 17.5 %collective-permute-start = (bf16[64,2048]{1,0:T(8,128)(2,1)}, bf16[64,2048]{1,0:T(8,128)(2,1)S(1)}, u32[]{:S(2)}, u32[]{:S(2)}) collective-permute-start(bf16[64,2048]{1,0:T(8,128)(2,1)} %get-tuple-element.25), channel_id=1, source_target_pairs={{0,8},{1,9},{2,10},{3,11},{4,12},{5,13},{6,14},{7,15},{8,0},{9,1},... | collective-permute-start | bytes 786440 | tf_op jit(solution)/shard_map/ppermute | solution.py:341
  6.1 13.4 %all-to-all-start = ((s32[16,1,256]{2,1,0:T(1,128)}), s32[16,1,256]{2,1,0:T(1,128)S(1)}, u32[]{:S(2)}, u32[]{:S(2)}) async-start(s32[16,1,256]{2,1,0:T(1,128)} %get-tuple-element.24), calls=%async_computation | async-start | bytes 32768 | tf_op jit(solution)/shard_map/all_to_all | solution.py:344
  22.3 23.2 %collective-permute-start.2 = (bf16[448,256]{1,0:T(8,128)(2,1)}, bf16[448,256]{1,0:T(8,128)(2,1)S(1)}, u32[]{:S(2)}, u32[]{:S(2)}) collective-permute-start(bf16[448,256]{1,0:T(8,128)(2,1)} %get-tuple-element.29), channel_id=1, source_target_pairs={{0,13},{1,12},{2,15},{3,14},{4,9},{5,8},{6,11},{7,10},{8,5},{9,4},... | collective-permute-start | bytes 688136 | tf_op jit(solution)/shard_map/ppermute | solution.py:341
  25.6 20.0 %collective-permute-start.1 = (bf16[448,256]{1,0:T(8,128)(2,1)}, bf16[448,256]{1,0:T(8,128)(2,1)S(1)}, u32[]{:S(2)}, u32[]{:S(2)}) collective-permute-start(bf16[448,256]{1,0:T(8,128)(2,1)} %get-tuple-element.28), channel_id=1, source_target_pairs={{0,12},{1,13},{2,14},{3,15},{4,8},{5,9},{6,10},{7,11},{8,4},{9,5},... | collective-permute-start | bytes 688136 | tf_op jit(solution)/shard_map/ppermute | solution.py:341
  25.9 19.7 %collective-permute-start.3 = (bf16[448,256]{1,0:T(8,128)(2,1)}, bf16[448,256]{1,0:T(8,128)(2,1)S(1)}, u32[]{:S(2)}, u32[]{:S(2)}) collective-permute-start(bf16[448,256]{1,0:T(8,128)(2,1)} %get-tuple-element.34), channel_id=1, source_target_pairs={{0,14},{1,15},{2,12},{3,13},{4,10},{5,11},{6,8},{7,9},{8,6},{9,7},... | collective-permute-start | bytes 688136 | tf_op jit(solution)/shard_map/ppermute | solution.py:341
  37.4 28.2 %copy-start = (bf16[2,128,128]{2,1,0:T(8,128)(2,1)S(1)}, bf16[2,128,128]{2,1,0:T(8,128)(2,1)}, u32[]{:S(2)}) copy-start(bf16[2,128,128]{2,1,0:T(8,128)(2,1)} %right_inv_ref.1) | copy-start | bytes 196612
  37.4 28.2 %copy-start.1 = (bf16[2,32,32]{2,1,0:T(8,128)(2,1)S(1)}, bf16[2,32,32]{2,1,0:T(8,128)(2,1)}, u32[]{:S(2)}) copy-start(bf16[2,32,32]{2,1,0:T(8,128)(2,1)} %left_inv_ref.1) | copy-start | bytes 12292
  37.4 42.1 %all-to-all-start.1 = ((bf16[8,576,256]{2,1,0:T(8,128)(2,1)}), bf16[8,576,256]{2,1,0:T(8,128)(2,1)}, u32[]{:S(2)}, u32[]{:S(2)}) async-start(bf16[8,576,256]{2,1,0:T(8,128)(2,1)} %shard_map.67), calls=%async_computation.1 | async-start | bytes 4718592 | tf_op jit(solution)/shard_map/all_to_all | solution.py:365
  41.9 37.4 %collective-permute-start.5 = (bf16[448,256]{1,0:T(8,128)(2,1)}, bf16[448,256]{1,0:T(8,128)(2,1)}, u32[]{:S(2)}, u32[]{:S(2)}) collective-permute-start(bf16[448,256]{1,0:T(8,128)(2,1)} %get-tuple-element.37), channel_id=1, source_target_pairs={{0,15},{1,14},{2,13},{3,12},{4,11},{5,10},{6,9},{7,8},{8,7},{9,6},... | collective-permute-start | bytes 688136 | tf_op jit(solution)/shard_map/ppermute | solution.py:341
  45.6 51.3 %collective-permute-start.8 = (bf16[448,256]{1,0:T(8,128)(2,1)}, bf16[448,256]{1,0:T(8,128)(2,1)}, u32[]{:S(2)}, u32[]{:S(2)}) collective-permute-start(bf16[448,256]{1,0:T(8,128)(2,1)} %get-tuple-element.42), channel_id=1, source_target_pairs={{0,9},{1,8},{2,11},{3,10},{4,13},{5,12},{6,15},{7,14},{8,1},{9,0},... | collective-permute-start | bytes 688136 | tf_op jit(solution)/shard_map/ppermute | solution.py:341
  61.4 41.9 %collective-permute-start.7 = (bf16[448,256]{1,0:T(8,128)(2,1)}, bf16[448,256]{1,0:T(8,128)(2,1)}, u32[]{:S(2)}, u32[]{:S(2)}) collective-permute-start(bf16[448,256]{1,0:T(8,128)(2,1)} %get-tuple-element.40), channel_id=1, source_target_pairs={{0,8},{1,9},{2,10},{3,11},{4,12},{5,13},{6,14},{7,15},{8,0},{9,1},... | collective-permute-start | bytes 688136 | tf_op jit(solution)/shard_map/ppermute | solution.py:341
  63.2 45.0 %collective-permute-start.4 = (bf16[448,256]{1,0:T(8,128)(2,1)}, bf16[448,256]{1,0:T(8,128)(2,1)}, u32[]{:S(2)}, u32[]{:S(2)}) collective-permute-start(bf16[448,256]{1,0:T(8,128)(2,1)} %get-tuple-element.35), channel_id=1, source_target_pairs={{0,10},{1,11},{2,8},{3,9},{4,14},{5,15},{6,12},{7,13},{8,2},{9,3},... | collective-permute-start | bytes 688136 | tf_op jit(solution)/shard_map/ppermute | solution.py:341
  65.7 13.7 %copy-start.2 = (bf16[448,256]{1,0:T(8,128)(2,1)S(1)}, bf16[448,256]{1,0:T(8,128)(2,1)}, u32[]{:S(2)}) copy-start(bf16[448,256]{1,0:T(8,128)(2,1)} %get-tuple-element.38) | copy-start | bytes 688132
  79.3 32.6 %collective-permute-start.6 = (bf16[448,256]{1,0:T(8,128)(2,1)S(1)}, bf16[448,256]{1,0:T(8,128)(2,1)S(1)}, u32[]{:S(2)}, u32[]{:S(2)}) collective-permute-start(bf16[448,256]{1,0:T(8,128)(2,1)S(1)} %copy-done.2), channel_id=1, source_target_pairs={{0,11},{1,10},{2,9},{3,8},{4,15},{5,14},{6,13},{7,12},{8,3},{9,2},... | collective-permute-start | bytes 688136 | tf_op jit(solution)/shard_map/ppermute | solution.py:341

commit v5 on v4

--- a/solution.py
+++ b/solution.py
@@ -373,11 +373,13 @@
     ids = after(ids, picked)
     pieces.update(zip(second, gather_pieces(me, ids, body, second)))
     prepared = precondition(after(query_grads, *[came[k] for k in first[:2]]), left_inv, right_inv)
-    for i, (k, earlier) in enumerate(zip(second, first)):
-        before = [came[earlier], prepared] if i == quarter - 1 else [came[earlier]]
-        came[k] = swap(after(pieces[k], *before), k)
+    for i, k in enumerate(second):
+        before = [came[first[i - 1]]] if i else []
+        if i == quarter - 1:
+            before.append(prepared)
+        came[k] = swap(after(pieces[k], *before) if before else pieces[k], k)
     total = score_near(base, prepared, near, width, half)
-    last = second[quarter // 2 :]
+    last = second[-1:]
     others = [k for k in came if k not in last]
     total = score_pieces(me, prepared, {k: came[k] for k in others}, total, width, 1.0)
     return score_pieces(me, prepared, {k: came[k] for k in last}, total, width, scale)

time: 115 us -> 115 us (level)
  starting transfers between devices: 40.7 us -> 24.6 us
  waiting for transfers between devices: 29.5 us -> 44.7 us
    ppermute x9, starting transfers between devices: 32.2 us -> 16.1 us  [swap(): return lax.ppermute(values, 'docs', [(i, i ^ k) for i in range(devices)])]
    all_to_all x1, waiting for transfers between devices: 0.01 us -> 8.42 us  [on_device(): lax.all_to_all(picked, 'docs', split_axis=0, concat_axis=0, axis_index_gr...]
    ppermute x9, waiting for transfers between devices: 22.9 us -> 29.8 us  [swap(): return lax.ppermute(values, 'docs', [(i, i ^ k) for i in range(devices)])]
  transfers between devices with their start and end apart: 11 -> 11, of which waited for: 6 -> 5; matrix products, arithmetic and copies ran while one was open for 3% -> 3% of each run, Pallas kernels for 30% -> 30%
where the time goes in v5:
time: 115 us; the launch traced here: 114 us
  waiting for transfers between devices  44.7 us (39%)
  Pallas kernels  41.4 us (36%)
  starting transfers between devices  24.6 us (21%)
  local copies, waits for them, and re-layouts  2.94 us (3%)
    ppermute x9, waiting for transfers between devices, swap(): return lax.ppermute(values, 'docs', [(i, i ^ k) for i in range(devices)])  29.8 us
    ppermute x9, starting transfers between devices, swap(): return lax.ppermute(values, 'docs', [(i, i ^ k) for i in range(devices)])  16.1 us
    pallas_call x1, Pallas kernels, precondition(): call(kernel, jax.ShapeDtypeStruct(queries.shape, queries.dtype), (total /...  13.1 us
    all_to_all x1, waiting for transfers between devices, on_device(): lax.all_to_all(picked, 'docs', split_axis=0, concat_axis=0, axis_index_gr...  8.42 us
    pallas_call x1, Pallas kernels, gather_rows(): call(kernel, pltpu.HBM((count, features, entries), tables[0].dtype), (cou...  8 us
    pallas_call x1, Pallas kernels, score_near(): call(kernel, jax.ShapeDtypeStruct((queries, entries), jnp.float32), (coun...  7 us
    all_to_all x1, waiting for transfers between devices, exchange(): lax.all_to_all(values, 'docs', split_axis=0, concat_axis=0, tiled=True)  6.54 us
    pallas_call x2, Pallas kernels, gather_pieces(): call(kernel, [pltpu.HBM((features, entries), tables[0][0].dtype)] * count...  5.74 us
  transfers between devices with their start and end apart: 11, of which 5 were waited for; matrix products, arithmetic and copies ran while one was open for 3% of the time, Pallas kernels for 30%

profile of v5, /device:TPU:0, one launch (start us, length us, event | category | flops | bytes accessed | tf_op | source)
XLA Modules:
  0.0 113.7 jit_solution(4425350305630804937)
XLA Ops:
  0.0 2.0 %shard_map.64 = (bf16[64,2048]{1,0:T(8,128)(2,1)}, s32[16,1,256]{2,1,0:T(1,128)}) custom-call(bf16[2048,512]{1,0:T(8,128)(2,1)} %docs_hbm.1, s32[1,256]{1,0:T(1,128)} %bitcast.7, s32[1,256]{1,0:T(1,128)} %bitcast.8), custom_call_target="tpu_custom_call" | custom-call | bytes 786432 | tf_op jit(solution)/shard_map/pallas_call | solution.py:63
  2.0 4.1 %collective-permute-start = (bf16[64,2048]{1,0:T(8,128)(2,1)}, bf16[64,2048]{1,0:T(8,128)(2,1)S(1)}, u32[]{:S(2)}, u32[]{:S(2)}) collective-permute-start(bf16[64,2048]{1,0:T(8,128)(2,1)} %get-tuple-element.24), channel_id=1, source_target_pairs={{0,8},{1,9},{2,10},{3,11},{4,12},{5,13},{6,14},{7,15},{8,0},{9,1},... | collective-permute-start | bytes 786440 | tf_op jit(solution)/shard_map/ppermute | solution.py:341
  6.1 3.9 %all-to-all-start = ((s32[16,1,256]{2,1,0:T(1,128)}), s32[16,1,256]{2,1,0:T(1,128)S(1)}, u32[]{:S(2)}, u32[]{:S(2)}) async-start(s32[16,1,256]{2,1,0:T(1,128)} %get-tuple-element.23), calls=%async_computation | async-start | bytes 32768 | tf_op jit(solution)/shard_map/all_to_all | solution.py:344
  10.0 2.9 %copy.7 = bf16[2048,512]{0,1:T(8,128)(2,1)S(1)} copy(bf16[2048,512]{1,0:T(8,128)(2,1)} %docs_hbm.1) | data formatting | bytes 4194304 | tf_op jit(solution)/shard_map/optimization_barrier | solution.py:327
  12.9 6.5 %all-to-all-done.refs_0_.refs_1_.refs_2_.refs_3_.ids_ref = s32[16,1,256]{2,1,0:T(1,128)S(1)} async-done(((s32[16,1,256]{2,1,0:T(1,128)}), s32[16,1,256]{2,1,0:T(1,128)S(1)}, u32[]{:S(2)}, u32[]{:S(2)}) %all-to-all-start) | async-done | bytes 16416 | tf_op jit(solution)/shard_map/all_to_all | solution.py:344
  19.5 0.0 collective-permute-done.refs_1_
  19.5 2.9 %shard_map.65 = (bf16[448,256]{1,0:T(8,128)(2,1)}, bf16[448,256]{1,0:T(8,128)(2,1)}, bf16[448,256]{1,0:T(8,128)(2,1)}, bf16[448,256]{1,0:T(8,128)(2,1)}) custom-call(s32[1]{0:T(128)} %bitcast.me_ref, s32[16,1,256]{2,1,0:T(1,128)S(1)} %all-to-all-done.refs_0_.refs_1_.refs_2_.refs_3_.ids_ref, ...), custom_call_target="tpu_custom_call" | custom-call | flops 1000 | bytes 1000 | tf_op jit(solution)/shard_map/pallas_call | solution.py:130
  22.4 3.2 %collective-permute-start.2 = (bf16[448,256]{1,0:T(8,128)(2,1)}, bf16[448,256]{1,0:T(8,128)(2,1)S(1)}, u32[]{:S(2)}, u32[]{:S(2)}) collective-permute-start(bf16[448,256]{1,0:T(8,128)(2,1)} %get-tuple-element.28), channel_id=1, source_target_pairs={{0,13},{1,12},{2,15},{3,14},{4,9},{5,8},{6,11},{7,10},{8,5},{9,4},... | collective-permute-start | bytes 688136 | tf_op jit(solution)/shard_map/ppermute | solution.py:341
  25.6 0.3 collective-permute-start.1
  25.9 8.0 %shard_map.67 = bf16[8,576,256]{2,1,0:T(8,128)(2,1)} custom-call(s32[1]{0:T(128)S(6)} %and.4.base_ref, s32[16,1,256]{2,1,0:T(1,128)S(1)} %all-to-all-done.refs_0_.refs_1_.refs_2_.refs_3_.ids_ref, bf16[512,2048]{1,0:T(8,128)(2,1)S(1)} %bitcast.5, bf16[64,2048]{1,0:T(8,128)(2,1)S(1)} %collective-permute-done.refs_1_), custom_call_target="tpu_custom_call" | custom-call | flops 1000 | bytes 1000 | tf_op jit(solution)/shard_map/pallas_call | solution.py:101
  33.9 0.0 copy-start
  33.9 0.0 copy-start.1
  33.9 4.5 %all-to-all-start.1 = ((bf16[8,576,256]{2,1,0:T(8,128)(2,1)}), bf16[8,576,256]{2,1,0:T(8,128)(2,1)}, u32[]{:S(2)}, u32[]{:S(2)}) async-start(bf16[8,576,256]{2,1,0:T(8,128)(2,1)} %shard_map.67), calls=%async_computation.1 | async-start | bytes 4718592 | tf_op jit(solution)/shard_map/all_to_all | solution.py:365
  38.4 3.5 %collective-permute-start.3 = (bf16[448,256]{1,0:T(8,128)(2,1)}, bf16[448,256]{1,0:T(8,128)(2,1)}, u32[]{:S(2)}, u32[]{:S(2)}) collective-permute-start(bf16[448,256]{1,0:T(8,128)(2,1)} %get-tuple-element.33), channel_id=1, source_target_pairs={{0,14},{1,15},{2,12},{3,13},{4,10},{5,11},{6,8},{7,9},{8,6},{9,7},... | collective-permute-start | bytes 688136 | tf_op jit(solution)/shard_map/ppermute | solution.py:341
  42.0 0.9 collective-permute-start.5
  42.9 2.9 %shard_map.68 = (bf16[448,256]{1,0:T(8,128)(2,1)}, bf16[448,256]{1,0:T(8,128)(2,1)}, bf16[448,256]{1,0:T(8,128)(2,1)}, bf16[448,256]{1,0:T(8,128)(2,1)}) custom-call(s32[1]{0:T(128)} %bitcast.me_ref, s32[16,1,256]{2,1,0:T(1,128)S(1)} %all-to-all-done.refs_0_.refs_1_.refs_2_.refs_3_.ids_ref, ...), custom_call_target="tpu_custom_call" | custom-call | flops 1000 | bytes 1000 | tf_op jit(solution)/shard_map/pallas_call | solution.py:130
  45.7 0.0 collective-permute-start.6
  45.7 0.0 collective-permute-done.2.refs_8_
  45.7 0.0 collective-permute-done.1.refs_7_
  45.7 4.0 %collective-permute-start.8 = (bf16[448,256]{1,0:T(8,128)(2,1)}, bf16[448,256]{1,0:T(8,128)(2,1)}, u32[]{:S(2)}, u32[]{:S(2)}) collective-permute-start(bf16[448,256]{1,0:T(8,128)(2,1)} %get-tuple-element.40), channel_id=1, source_target_pairs={{0,10},{1,11},{2,8},{3,9},{4,14},{5,15},{6,12},{7,13},{8,2},{9,3},... | collective-permute-start | bytes 688136 | tf_op jit(solution)/shard_map/ppermute | solution.py:341
  49.8 0.0 collective-permute-start.7
  49.8 0.0 copy-done
  49.8 0.0 copy-done.1
  49.8 0.0 copy-start.2
  49.8 13.1 %shard_map.66.own_ref.far_ref.refs_0_.refs_1_.refs_2_.refs_3_.refs_4_.refs_5_.refs_6_ = bf16[512,8192]{1,0:T(8,128)(2,1)} custom-call(bf16[512,8192]{1,0:T(8,128)(2,1)} %queries_ref, bf16[2,32,32]{2,1,0:T(8,128)(2,1)S(1)} %copy-done.1, bf16[2,128,128]{2,1,0:T(8,128)(2,1)S(1)} %copy-done), custom_call_target="tpu_custom_call" | custom-call | flops 167772160000 | bytes 16777216 | tf_op jit(solution)/shard_map/pallas_call | solution.py:306
  62.9 17.9 %collective-permute-done.3.refs_9_ = bf16[448,256]{1,0:T(8,128)(2,1)} collective-permute-done((bf16[448,256]{1,0:T(8,128)(2,1)}, bf16[448,256]{1,0:T(8,128)(2,1)}, u32[]{:S(2)}, u32[]{:S(2)}) %collective-permute-start.3) | collective-permute-done | bytes 229408 | tf_op jit(solution)/shard_map/ppermute | solution.py:341
  80.9 0.0 copy-done.2
  80.9 0.0 collective-permute-start.4
  80.9 8.4 %all-to-all-done.1.chosen_ref = bf16[8,576,256]{2,1,0:T(8,128)(2,1)} async-done(((bf16[8,576,256]{2,1,0:T(8,128)(2,1)}), bf16[8,576,256]{2,1,0:T(8,128)(2,1)}, u32[]{:S(2)}, u32[]{:S(2)}) %all-to-all-start.1) | async-done | bytes 2359328 | tf_op jit(solution)/shard_map/all_to_all | solution.py:365
  89.3 7.0 %shard_map.69.refs_14_ = f32[512,256]{1,0:T(8,128)S(1)} custom-call(s32[1]{0:T(128)S(6)} %and.4.base_ref, bf16[512,8192]{1,0:T(8,128)(2,1)} %shard_map.66.own_ref.far_ref.refs_0_.refs_1_.refs_2_.refs_3_.refs_4_.refs_5_.refs_6_, bf16[512,8192]{1,0:T(8,128)(2,1)} %shard_map.66.own_ref.far_ref.refs_0_.refs_1_.refs_2_.refs_3_.refs_4_.refs_5_.refs_6_, ...), custom_call_target="tpu_custom_call" | custom-call | flops 1207959552 | bytes 7602176 | tf_op jit(solution)/shard_map/pallas_call | solution.py:193
  96.3 0.0 collective-permute-done.5.refs_10_
  96.3 0.0 collective-permute-done.6.refs_11_
  96.3 0.0 collective-permute-done.8.refs_13_
  96.3 10.0 %collective-permute-done.7.refs_12_ = bf16[448,256]{1,0:T(8,128)(2,1)} collective-permute-done((bf16[448,256]{1,0:T(8,128)(2,1)}, bf16[448,256]{1,0:T(8,128)(2,1)}, u32[]{:S(2)}, u32[]{:S(2)}) %collective-permute-start.7) | collective-permute-done | bytes 229408 | tf_op jit(solution)/shard_map/ppermute | solution.py:341
  106.3 3.5 %shard_map.70.refs_2_ = f32[512,256]{1,0:T(8,128)S(1)} custom-call(s32[1]{0:T(128)} %bitcast.me_ref, bf16[512,8192]{1,0:T(8,128)(2,1)} %shard_map.66.own_ref.far_ref.refs_0_.refs_1_.refs_2_.refs_3_.refs_4_.refs_5_.refs_6_, bf16[512,8192]{1,0:T(8,128)(2,1)} %shard_map.66.own_ref.far_ref.refs_0_.refs_1_.refs_2_.refs_3_.refs_4_.refs_5_.refs_6_, ...), custom_call_target="tpu_custom_call" | custom-call | flops 822083584 | bytes 5865472 | tf_op jit(solution)/shard_map/pallas_call | solution.py:160
  109.8 1.8 %collective-permute-done.4.refs_1_ = bf16[448,256]{1,0:T(8,128)(2,1)S(1)} collective-permute-done((bf16[448,256]{1,0:T(8,128)(2,1)S(1)}, bf16[448,256]{1,0:T(8,128)(2,1)S(1)}, u32[]{:S(2)}, u32[]{:S(2)}) %collective-permute-start.4) | collective-permute-done | bytes 229408 | tf_op jit(solution)/shard_map/ppermute | solution.py:341
  111.6 2.1 %shard_map.71 = f32[512,256]{1,0:T(8,128)} custom-call(s32[1]{0:T(128)} %bitcast.me_ref, bf16[512,8192]{1,0:T(8,128)(2,1)} %shard_map.66.own_ref.far_ref.refs_0_.refs_1_.refs_2_.refs_3_.refs_4_.refs_5_.refs_6_, bf16[448,256]{1,0:T(8,128)(2,1)S(1)} %collective-permute-done.4.refs_1_, f32[512,256]{1,0:T(8,128)S(1)} %shard_map.70.refs_2_), custom_call_target="tpu_custom_call" | custom-call | flops 117440512 | bytes 1736704 | tf_op jit(solution)/shard_map/pallas_call | solution.py:160
Async XLA Ops:
  2.0 17.5 %collective-permute-start = (bf16[64,2048]{1,0:T(8,128)(2,1)}, bf16[64,2048]{1,0:T(8,128)(2,1)S(1)}, u32[]{:S(2)}, u32[]{:S(2)}) collective-permute-start(bf16[64,2048]{1,0:T(8,128)(2,1)} %get-tuple-element.24), channel_id=1, source_target_pairs={{0,8},{1,9},{2,10},{3,11},{4,12},{5,13},{6,14},{7,15},{8,0},{9,1},... | collective-permute-start | bytes 786440 | tf_op jit(solution)/shard_map/ppermute | solution.py:341
  6.1 13.4 %all-to-all-start = ((s32[16,1,256]{2,1,0:T(1,128)}), s32[16,1,256]{2,1,0:T(1,128)S(1)}, u32[]{:S(2)}, u32[]{:S(2)}) async-start(s32[16,1,256]{2,1,0:T(1,128)} %get-tuple-element.23), calls=%async_computation | async-start | bytes 32768 | tf_op jit(solution)/shard_map/all_to_all | solution.py:344
  22.4 23.4 %collective-permute-start.2 = (bf16[448,256]{1,0:T(8,128)(2,1)}, bf16[448,256]{1,0:T(8,128)(2,1)S(1)}, u32[]{:S(2)}, u32[]{:S(2)}) collective-permute-start(bf16[448,256]{1,0:T(8,128)(2,1)} %get-tuple-element.28), channel_id=1, source_target_pairs={{0,13},{1,12},{2,15},{3,14},{4,9},{5,8},{6,11},{7,10},{8,5},{9,4},... | collective-permute-start | bytes 688136 | tf_op jit(solution)/shard_map/ppermute | solution.py:341
  25.6 20.2 %collective-permute-start.1 = (bf16[448,256]{1,0:T(8,128)(2,1)}, bf16[448,256]{1,0:T(8,128)(2,1)S(1)}, u32[]{:S(2)}, u32[]{:S(2)}) collective-permute-start(bf16[448,256]{1,0:T(8,128)(2,1)} %get-tuple-element.27), channel_id=1, source_target_pairs={{0,12},{1,13},{2,14},{3,15},{4,8},{5,9},{6,10},{7,11},{8,4},{9,5},... | collective-permute-start | bytes 688136 | tf_op jit(solution)/shard_map/ppermute | solution.py:341
  33.9 15.9 %copy-start = (bf16[2,128,128]{2,1,0:T(8,128)(2,1)S(1)}, bf16[2,128,128]{2,1,0:T(8,128)(2,1)}, u32[]{:S(2)}) copy-start(bf16[2,128,128]{2,1,0:T(8,128)(2,1)} %right_inv_ref.1) | copy-start | bytes 196612
  33.9 15.9 %copy-start.1 = (bf16[2,32,32]{2,1,0:T(8,128)(2,1)S(1)}, bf16[2,32,32]{2,1,0:T(8,128)(2,1)}, u32[]{:S(2)}) copy-start(bf16[2,32,32]{2,1,0:T(8,128)(2,1)} %left_inv_ref.1) | copy-start | bytes 12292
  33.9 55.4 %all-to-all-start.1 = ((bf16[8,576,256]{2,1,0:T(8,128)(2,1)}), bf16[8,576,256]{2,1,0:T(8,128)(2,1)}, u32[]{:S(2)}, u32[]{:S(2)}) async-start(bf16[8,576,256]{2,1,0:T(8,128)(2,1)} %shard_map.67), calls=%async_computation.1 | async-start | bytes 4718592 | tf_op jit(solution)/shard_map/all_to_all | solution.py:365
  38.4 42.4 %collective-permute-start.3 = (bf16[448,256]{1,0:T(8,128)(2,1)}, bf16[448,256]{1,0:T(8,128)(2,1)}, u32[]{:S(2)}, u32[]{:S(2)}) collective-permute-start(bf16[448,256]{1,0:T(8,128)(2,1)} %get-tuple-element.33), channel_id=1, source_target_pairs={{0,14},{1,15},{2,12},{3,13},{4,10},{5,11},{6,8},{7,9},{8,6},{9,7},... | collective-permute-start | bytes 688136 | tf_op jit(solution)/shard_map/ppermute | solution.py:341
  42.0 54.3 %collective-permute-start.5 = (bf16[448,256]{1,0:T(8,128)(2,1)}, bf16[448,256]{1,0:T(8,128)(2,1)}, u32[]{:S(2)}, u32[]{:S(2)}) collective-permute-start(bf16[448,256]{1,0:T(8,128)(2,1)} %get-tuple-element.35), channel_id=1, source_target_pairs={{0,15},{1,14},{2,13},{3,12},{4,11},{5,10},{6,9},{7,8},{8,7},{9,6},... | collective-permute-start | bytes 688136 | tf_op jit(solution)/shard_map/ppermute | solution.py:341
  45.7 50.6 %collective-permute-start.6 = (bf16[448,256]{1,0:T(8,128)(2,1)}, bf16[448,256]{1,0:T(8,128)(2,1)}, u32[]{:S(2)}, u32[]{:S(2)}) collective-permute-start(bf16[448,256]{1,0:T(8,128)(2,1)} %get-tuple-element.36), channel_id=1, source_target_pairs={{0,8},{1,9},{2,10},{3,11},{4,12},{5,13},{6,14},{7,15},{8,0},{9,1},... | collective-permute-start | bytes 688136 | tf_op jit(solution)/shard_map/ppermute | solution.py:341
  45.7 50.6 %collective-permute-start.8 = (bf16[448,256]{1,0:T(8,128)(2,1)}, bf16[448,256]{1,0:T(8,128)(2,1)}, u32[]{:S(2)}, u32[]{:S(2)}) collective-permute-start(bf16[448,256]{1,0:T(8,128)(2,1)} %get-tuple-element.40), channel_id=1, source_target_pairs={{0,10},{1,11},{2,8},{3,9},{4,14},{5,15},{6,12},{7,13},{8,2},{9,3},... | collective-permute-start | bytes 688136 | tf_op jit(solution)/shard_map/ppermute | solution.py:341
  49.8 56.5 %collective-permute-start.7 = (bf16[448,256]{1,0:T(8,128)(2,1)}, bf16[448,256]{1,0:T(8,128)(2,1)}, u32[]{:S(2)}, u32[]{:S(2)}) collective-permute-start(bf16[448,256]{1,0:T(8,128)(2,1)} %get-tuple-element.38), channel_id=1, source_target_pairs={{0,9},{1,8},{2,11},{3,10},{4,13},{5,12},{6,15},{7,14},{8,1},{9,0},... | collective-permute-start | bytes 688136 | tf_op jit(solution)/shard_map/ppermute | solution.py:341
  49.8 31.0 %copy-start.2 = (bf16[448,256]{1,0:T(8,128)(2,1)S(1)}, bf16[448,256]{1,0:T(8,128)(2,1)}, u32[]{:S(2)}) copy-start(bf16[448,256]{1,0:T(8,128)(2,1)} %get-tuple-element.34) | copy-start | bytes 688132
  80.9 30.7 %collective-permute-start.4 = (bf16[448,256]{1,0:T(8,128)(2,1)S(1)}, bf16[448,256]{1,0:T(8,128)(2,1)S(1)}, u32[]{:S(2)}, u32[]{:S(2)}) collective-permute-start(bf16[448,256]{1,0:T(8,128)(2,1)S(1)} %copy-done.2), channel_id=1, source_target_pairs={{0,11},{1,10},{2,9},{3,8},{4,15},{5,14},{6,13},{7,12},{8,3},{9,2},... | collective-permute-start | bytes 688136 | tf_op jit(solution)/shard_map/ppermute | solution.py:341

commit v6 on v3

--- a/solution.py
+++ b/solution.py
@@ -377,11 +377,13 @@
     prepared = precondition(after(query_grads, *ready), left_inv, right_inv)
     for k in second:
         came[k] = swap(after(pieces[k], *ready), k)
-    for k, earlier in zip(third, second[::-1]):
-        came[k] = swap(after(pieces[k], came[earlier], prepared), k)
+    for i, k in enumerate(third):
+        before = [came[second[0]]] if i else ready
+        came[k] = swap(after(pieces[k], prepared, *before), k)
     total = score_near(base, prepared, near, width, half)
-    total = score_pieces(me, prepared, {k: came[k] for k in first}, total, width, 1.0)
-    return score_pieces(me, prepared, {k: came[k] for k in second + third}, total, width, scale)
+    others = [*first, *second, *third[:-1]]
+    total = score_pieces(me, prepared, {k: came[k] for k in others}, total, width, 1.0)
+    return score_pieces(me, prepared, {k: came[k] for k in third[-1:]}, total, width, scale)
 
 
 def solution(mesh):

time: 121 us -> 117 us (0.967)
  waiting for transfers between devices: 50.6 us -> 48.2 us
  starting transfers between devices: 25.5 us -> 23.2 us
    ppermute x9, waiting for transfers between devices: 44.1 us -> 41.6 us  [swap(): return lax.ppermute(values, 'docs', [(i, i ^ k) for i in range(devices)])]
    ppermute x9, starting transfers between devices: 17.1 us -> 14.8 us  [swap(): return lax.ppermute(values, 'docs', [(i, i ^ k) for i in range(devices)])]
  transfers between devices with their start and end apart: 11 -> 11, of which waited for: 5 -> 6; matrix products, arithmetic and copies ran while one was open for 2% -> 3% of each run, Pallas kernels for 28% -> 31%
where the time goes in v6:
time: 117 us; the launch traced here: 116 us
  waiting for transfers between devices  48.2 us (41%)
  Pallas kernels  41.4 us (35%)
  starting transfers between devices  23.2 us (20%)
  local copies, waits for them, and re-layouts  2.95 us (3%)
    ppermute x9, waiting for transfers between devices, swap(): return lax.ppermute(values, 'docs', [(i, i ^ k) for i in range(devices)])  41.6 us
    ppermute x9, starting transfers between devices, swap(): return lax.ppermute(values, 'docs', [(i, i ^ k) for i in range(devices)])  14.8 us
    pallas_call x1, Pallas kernels, precondition(): call(kernel, jax.ShapeDtypeStruct(queries.shape, queries.dtype), (total /...  13.1 us
    pallas_call x1, Pallas kernels, gather_rows(): call(kernel, pltpu.HBM((count, features, entries), tables[0].dtype), (cou...  8.02 us
    pallas_call x1, Pallas kernels, score_near(): call(kernel, jax.ShapeDtypeStruct((queries, entries), jnp.float32), (coun...  7.03 us
    all_to_all x1, waiting for transfers between devices, exchange(): lax.all_to_all(values, 'docs', split_axis=0, concat_axis=0, tiled=True)  6.54 us
    pallas_call x2, Pallas kernels, gather_pieces(): call(kernel, [pltpu.HBM((features, entries), tables[0][0].dtype)] * count...  5.71 us
    pallas_call x2, Pallas kernels, score_pieces(): call(kernel, jax.ShapeDtypeStruct((queries, entries), jnp.float32), (1,),...  5.53 us
  transfers between devices with their start and end apart: 11, of which 6 were waited for; matrix products, arithmetic and copies ran while one was open for 3% of the time, Pallas kernels for 31%

profile of v6, /device:TPU:0, one launch (start us, length us, event | category | flops | bytes accessed | tf_op | source)
XLA Modules:
  0.0 115.8 jit_solution(15273916778628602401)
XLA Ops:
  0.0 2.0 %shard_map.64 = (bf16[64,2048]{1,0:T(8,128)(2,1)}, s32[16,1,256]{2,1,0:T(1,128)}) custom-call(bf16[2048,512]{1,0:T(8,128)(2,1)} %docs_hbm.1, s32[1,256]{1,0:T(1,128)} %bitcast.7, s32[1,256]{1,0:T(1,128)} %bitcast.8), custom_call_target="tpu_custom_call" | custom-call | bytes 786432 | tf_op jit(solution)/shard_map/pallas_call | solution.py:63
  2.0 4.1 %collective-permute-start = (bf16[64,2048]{1,0:T(8,128)(2,1)}, bf16[64,2048]{1,0:T(8,128)(2,1)S(1)}, u32[]{:S(2)}, u32[]{:S(2)}) collective-permute-start(bf16[64,2048]{1,0:T(8,128)(2,1)} %get-tuple-element.27), channel_id=1, source_target_pairs={{0,8},{1,9},{2,10},{3,11},{4,12},{5,13},{6,14},{7,15},{8,0},{9,1},... | collective-permute-start | bytes 786440 | tf_op jit(solution)/shard_map/ppermute | solution.py:341
  6.1 3.9 %all-to-all-start = ((s32[16,1,256]{2,1,0:T(1,128)}), s32[16,1,256]{2,1,0:T(1,128)S(1)}, u32[]{:S(2)}, u32[]{:S(2)}) async-start(s32[16,1,256]{2,1,0:T(1,128)} %get-tuple-element.26), calls=%async_computation | async-start | bytes 32768 | tf_op jit(solution)/shard_map/all_to_all | solution.py:344
  10.0 2.9 %copy.7 = bf16[2048,512]{0,1:T(8,128)(2,1)S(1)} copy(bf16[2048,512]{1,0:T(8,128)(2,1)} %docs_hbm.1) | data formatting | bytes 4194304 | tf_op jit(solution)/shard_map/optimization_barrier | solution.py:327
  12.9 6.5 %all-to-all-done.refs_0_.refs_1_.refs_2_.refs_3_.refs_4_.refs_5_.ids_ref = s32[16,1,256]{2,1,0:T(1,128)S(1)} async-done(((s32[16,1,256]{2,1,0:T(1,128)}), s32[16,1,256]{2,1,0:T(1,128)S(1)}, u32[]{:S(2)}, u32[]{:S(2)}) %all-to-all-start) | async-done | bytes 16416 | tf_op jit(solution)/shard_map/all_to_all | solution.py:344
  19.5 0.0 collective-permute-done.refs_1_
  19.5 1.9 %shard_map.65 = (bf16[448,256]{1,0:T(8,128)(2,1)}, bf16[448,256]{1,0:T(8,128)(2,1)}) custom-call(s32[1]{0:T(128)} %bitcast.me_ref, s32[16,1,256]{2,1,0:T(1,128)S(1)} %all-to-all-done.refs_0_.refs_1_.refs_2_.refs_3_.refs_4_.refs_5_.ids_ref, s32[16,1,256]{2,1,0:T(1,128)S(1)} %all-to-all-done.refs_0_.refs_1_.refs_2_.refs_3_.refs_4_.refs_5_.ids_ref, ...), custom_call_target="tpu_custom_call" | custom-call | flops 1000 | bytes 1000 | tf_op jit(solution)/shard_map/pallas_call | solution.py:130
  21.4 2.2 %collective-permute-start.2 = (bf16[448,256]{1,0:T(8,128)(2,1)}, bf16[448,256]{1,0:T(8,128)(2,1)S(1)}, u32[]{:S(2)}, u32[]{:S(2)}) collective-permute-start(bf16[448,256]{1,0:T(8,128)(2,1)} %get-tuple-element.31), channel_id=1, source_target_pairs={{0,9},{1,8},{2,11},{3,10},{4,13},{5,12},{6,15},{7,14},{8,1},{9,0},... | collective-permute-start | bytes 688136 | tf_op jit(solution)/shard_map/ppermute | solution.py:341
  23.6 0.5 collective-permute-start.1
  24.1 3.8 %shard_map.67 = (bf16[448,256]{1,0:T(8,128)(2,1)}, bf16[448,256]{1,0:T(8,128)(2,1)}, bf16[448,256]{1,0:T(8,128)(2,1)}, bf16[448,256]{1,0:T(8,128)(2,1)}, bf16[44...) custom-call(s32[1]{0:T(128)} %bitcast.me_ref, ...), custom_call_target="tpu_custom_call" | custom-call | flops 1000 | bytes 1000 | tf_op jit(solution)/shard_map/pallas_call | solution.py:130
  27.9 8.0 %shard_map.68 = bf16[8,576,256]{2,1,0:T(8,128)(2,1)} custom-call(s32[1]{0:T(128)S(6)} %and.4.base_ref, s32[16,1,256]{2,1,0:T(1,128)S(1)} %all-to-all-done.refs_0_.refs_1_.refs_2_.refs_3_.refs_4_.refs_5_.ids_ref, bf16[512,2048]{1,0:T(8,128)(2,1)S(1)} %bitcast.6, bf16[64,2048]{1,0:T(8,128)(2,1)S(1)} %collective-permute-done.refs_1_), custom_call_target="tpu_custom_call" | custom-call | flops 1000 | bytes 1000 | tf_op jit(solution)/shard_map/pallas_call | solution.py:101
  35.9 0.0 copy-start
  35.9 0.0 copy-start.1
  35.9 4.5 %all-to-all-start.1 = ((bf16[8,576,256]{2,1,0:T(8,128)(2,1)}), bf16[8,576,256]{2,1,0:T(8,128)(2,1)}, u32[]{:S(2)}, u32[]{:S(2)}) async-start(bf16[8,576,256]{2,1,0:T(8,128)(2,1)} %shard_map.68), calls=%async_computation.1 | async-start | bytes 4718592 | tf_op jit(solution)/shard_map/all_to_all | solution.py:368
  40.4 0.0 collective-permute-done.2.refs_8_
  40.5 4.8 %collective-permute-done.1.refs_7_ = bf16[448,256]{1,0:T(8,128)(2,1)S(1)} collective-permute-done((bf16[448,256]{1,0:T(8,128)(2,1)}, bf16[448,256]{1,0:T(8,128)(2,1)S(1)}, u32[]{:S(2)}, u32[]{:S(2)}) %collective-permute-start.1) | collective-permute-done | bytes 229408 | tf_op jit(solution)/shard_map/ppermute | solution.py:341
  45.3 3.5 %collective-permute-start.3 = (bf16[448,256]{1,0:T(8,128)(2,1)}, bf16[448,256]{1,0:T(8,128)(2,1)}, u32[]{:S(2)}, u32[]{:S(2)}) collective-permute-start(bf16[448,256]{1,0:T(8,128)(2,1)} %get-tuple-element.36), channel_id=1, source_target_pairs={{0,12},{1,13},{2,14},{3,15},{4,8},{5,9},{6,10},{7,11},{8,4},{9,5},... | collective-permute-start | bytes 688136 | tf_op jit(solution)/shard_map/ppermute | solution.py:341
  48.8 0.0 collective-permute-start.7
  48.8 3.9 %collective-permute-start.6 = (bf16[448,256]{1,0:T(8,128)(2,1)}, bf16[448,256]{1,0:T(8,128)(2,1)}, u32[]{:S(2)}, u32[]{:S(2)}) collective-permute-start(bf16[448,256]{1,0:T(8,128)(2,1)} %get-tuple-element.41), channel_id=1, source_target_pairs={{0,14},{1,15},{2,12},{3,13},{4,10},{5,11},{6,8},{7,9},{8,6},{9,7},... | collective-permute-start | bytes 688136 | tf_op jit(solution)/shard_map/ppermute | solution.py:341
  52.7 0.6 collective-permute-start.5
  53.2 0.0 copy-done
  53.2 0.0 copy-done.1
  53.3 0.0 copy-start.3
  53.3 0.0 copy-start.2
  53.3 13.1 %shard_map.66.own_ref.far_ref.refs_0_.refs_1_.refs_2_.refs_3_.refs_4_.refs_5_.refs_6_ = bf16[512,8192]{1,0:T(8,128)(2,1)} custom-call(bf16[512,8192]{1,0:T(8,128)(2,1)} %queries_ref, bf16[2,32,32]{2,1,0:T(8,128)(2,1)S(1)} %copy-done.1, bf16[2,128,128]{2,1,0:T(8,128)(2,1)S(1)} %copy-done), custom_call_target="tpu_custom_call" | custom-call | flops 167772160000 | bytes 16777216 | tf_op jit(solution)/shard_map/pallas_call | solution.py:306
  66.4 0.0 copy-done.3
  66.4 0.0 collective-permute-start.8
  66.4 15.0 %collective-permute-done.3.refs_9_ = bf16[448,256]{1,0:T(8,128)(2,1)} collective-permute-done((bf16[448,256]{1,0:T(8,128)(2,1)}, bf16[448,256]{1,0:T(8,128)(2,1)}, u32[]{:S(2)}, u32[]{:S(2)}) %collective-permute-start.3) | collective-permute-done | bytes 229408 | tf_op jit(solution)/shard_map/ppermute | solution.py:341
  81.4 0.0 copy-done.2
  81.4 0.0 collective-permute-start.4
  81.4 0.0 all-to-all-done.1.chosen_ref
  81.4 7.0 %shard_map.69.refs_14_ = f32[512,256]{1,0:T(8,128)S(1)} custom-call(s32[1]{0:T(128)S(6)} %and.4.base_ref, bf16[512,8192]{1,0:T(8,128)(2,1)} %shard_map.66.own_ref.far_ref.refs_0_.refs_1_.refs_2_.refs_3_.refs_4_.refs_5_.refs_6_, bf16[512,8192]{1,0:T(8,128)(2,1)} %shard_map.66.own_ref.far_ref.refs_0_.refs_1_.refs_2_.refs_3_.refs_4_.refs_5_.refs_6_, ...), custom_call_target="tpu_custom_call" | custom-call | flops 1207959552 | bytes 7602176 | tf_op jit(solution)/shard_map/pallas_call | solution.py:193
  88.5 0.0 collective-permute-done.7.refs_12_
  88.5 4.4 %collective-permute-done.6.refs_11_ = bf16[448,256]{1,0:T(8,128)(2,1)} collective-permute-done((bf16[448,256]{1,0:T(8,128)(2,1)}, bf16[448,256]{1,0:T(8,128)(2,1)}, u32[]{:S(2)}, u32[]{:S(2)}) %collective-permute-start.6) | collective-permute-done | bytes 229408 | tf_op jit(solution)/shard_map/ppermute | solution.py:341
  92.8 2.4 %collective-permute-done.5.refs_10_ = bf16[448,256]{1,0:T(8,128)(2,1)} collective-permute-done((bf16[448,256]{1,0:T(8,128)(2,1)}, bf16[448,256]{1,0:T(8,128)(2,1)}, u32[]{:S(2)}, u32[]{:S(2)}) %collective-permute-start.5) | collective-permute-done | bytes 229408 | tf_op jit(solution)/shard_map/ppermute | solution.py:341
  95.2 15.1 %collective-permute-done.8.refs_13_ = bf16[448,256]{1,0:T(8,128)(2,1)S(1)} collective-permute-done((bf16[448,256]{1,0:T(8,128)(2,1)S(1)}, bf16[448,256]{1,0:T(8,128)(2,1)S(1)}, u32[]{:S(2)}, u32[]{:S(2)}) %collective-permute-start.8) | collective-permute-done | bytes 229408 | tf_op jit(solution)/shard_map/ppermute | solution.py:341
  110.3 3.4 %shard_map.70.refs_2_ = f32[512,256]{1,0:T(8,128)S(1)} custom-call(s32[1]{0:T(128)} %bitcast.me_ref, bf16[512,8192]{1,0:T(8,128)(2,1)} %shard_map.66.own_ref.far_ref.refs_0_.refs_1_.refs_2_.refs_3_.refs_4_.refs_5_.refs_6_, bf16[512,8192]{1,0:T(8,128)(2,1)} %shard_map.66.own_ref.far_ref.refs_0_.refs_1_.refs_2_.refs_3_.refs_4_.refs_5_.refs_6_, ...), custom_call_target="tpu_custom_call" | custom-call | flops 822083584 | bytes 5865472 | tf_op jit(solution)/shard_map/pallas_call | solution.py:160
  113.7 0.0 collective-permute-done.4.refs_1_
  113.7 2.1 %shard_map.71 = f32[512,256]{1,0:T(8,128)} custom-call(s32[1]{0:T(128)} %bitcast.me_ref, bf16[512,8192]{1,0:T(8,128)(2,1)} %shard_map.66.own_ref.far_ref.refs_0_.refs_1_.refs_2_.refs_3_.refs_4_.refs_5_.refs_6_, bf16[448,256]{1,0:T(8,128)(2,1)S(1)} %collective-permute-done.4.refs_1_, f32[512,256]{1,0:T(8,128)S(1)} %shard_map.70.refs_2_), custom_call_target="tpu_custom_call" | custom-call | flops 117440512 | bytes 1736704 | tf_op jit(solution)/shard_map/pallas_call | solution.py:160
Async XLA Ops:
  2.0 17.5 %collective-permute-start = (bf16[64,2048]{1,0:T(8,128)(2,1)}, bf16[64,2048]{1,0:T(8,128)(2,1)S(1)}, u32[]{:S(2)}, u32[]{:S(2)}) collective-permute-start(bf16[64,2048]{1,0:T(8,128)(2,1)} %get-tuple-element.27), channel_id=1, source_target_pairs={{0,8},{1,9},{2,10},{3,11},{4,12},{5,13},{6,14},{7,15},{8,0},{9,1},... | collective-permute-start | bytes 786440 | tf_op jit(solution)/shard_map/ppermute | solution.py:341
  6.1 13.4 %all-to-all-start = ((s32[16,1,256]{2,1,0:T(1,128)}), s32[16,1,256]{2,1,0:T(1,128)S(1)}, u32[]{:S(2)}, u32[]{:S(2)}) async-start(s32[16,1,256]{2,1,0:T(1,128)} %get-tuple-element.26), calls=%async_computation | async-start | bytes 32768 | tf_op jit(solution)/shard_map/all_to_all | solution.py:344
  21.4 19.0 %collective-permute-start.2 = (bf16[448,256]{1,0:T(8,128)(2,1)}, bf16[448,256]{1,0:T(8,128)(2,1)S(1)}, u32[]{:S(2)}, u32[]{:S(2)}) collective-permute-start(bf16[448,256]{1,0:T(8,128)(2,1)} %get-tuple-element.31), channel_id=1, source_target_pairs={{0,9},{1,8},{2,11},{3,10},{4,13},{5,12},{6,15},{7,14},{8,1},{9,0},... | collective-permute-start | bytes 688136 | tf_op jit(solution)/shard_map/ppermute | solution.py:341
  23.6 21.7 %collective-permute-start.1 = (bf16[448,256]{1,0:T(8,128)(2,1)}, bf16[448,256]{1,0:T(8,128)(2,1)S(1)}, u32[]{:S(2)}, u32[]{:S(2)}) collective-permute-start(bf16[448,256]{1,0:T(8,128)(2,1)} %get-tuple-element.30), channel_id=1, source_target_pairs={{0,8},{1,9},{2,10},{3,11},{4,12},{5,13},{6,14},{7,15},{8,0},{9,1},... | collective-permute-start | bytes 688136 | tf_op jit(solution)/shard_map/ppermute | solution.py:341
  35.9 17.3 %copy-start = (bf16[2,128,128]{2,1,0:T(8,128)(2,1)S(1)}, bf16[2,128,128]{2,1,0:T(8,128)(2,1)}, u32[]{:S(2)}) copy-start(bf16[2,128,128]{2,1,0:T(8,128)(2,1)} %right_inv_ref.1) | copy-start | bytes 196612
  35.9 17.3 %copy-start.1 = (bf16[2,32,32]{2,1,0:T(8,128)(2,1)S(1)}, bf16[2,32,32]{2,1,0:T(8,128)(2,1)}, u32[]{:S(2)}) copy-start(bf16[2,32,32]{2,1,0:T(8,128)(2,1)} %left_inv_ref.1) | copy-start | bytes 12292
  35.9 45.5 %all-to-all-start.1 = ((bf16[8,576,256]{2,1,0:T(8,128)(2,1)}), bf16[8,576,256]{2,1,0:T(8,128)(2,1)}, u32[]{:S(2)}, u32[]{:S(2)}) async-start(bf16[8,576,256]{2,1,0:T(8,128)(2,1)} %shard_map.68), calls=%async_computation.1 | async-start | bytes 4718592 | tf_op jit(solution)/shard_map/all_to_all | solution.py:368
  45.3 36.1 %collective-permute-start.3 = (bf16[448,256]{1,0:T(8,128)(2,1)}, bf16[448,256]{1,0:T(8,128)(2,1)}, u32[]{:S(2)}, u32[]{:S(2)}) collective-permute-start(bf16[448,256]{1,0:T(8,128)(2,1)} %get-tuple-element.36), channel_id=1, source_target_pairs={{0,12},{1,13},{2,14},{3,15},{4,8},{5,9},{6,10},{7,11},{8,4},{9,5},... | collective-permute-start | bytes 688136 | tf_op jit(solution)/shard_map/ppermute | solution.py:341
  48.8 39.7 %collective-permute-start.7 = (bf16[448,256]{1,0:T(8,128)(2,1)}, bf16[448,256]{1,0:T(8,128)(2,1)}, u32[]{:S(2)}, u32[]{:S(2)}) collective-permute-start(bf16[448,256]{1,0:T(8,128)(2,1)} %get-tuple-element.43), channel_id=1, source_target_pairs={{0,15},{1,14},{2,13},{3,12},{4,11},{5,10},{6,9},{7,8},{8,7},{9,6},... | collective-permute-start | bytes 688136 | tf_op jit(solution)/shard_map/ppermute | solution.py:341
  48.8 44.1 %collective-permute-start.6 = (bf16[448,256]{1,0:T(8,128)(2,1)}, bf16[448,256]{1,0:T(8,128)(2,1)}, u32[]{:S(2)}, u32[]{:S(2)}) collective-permute-start(bf16[448,256]{1,0:T(8,128)(2,1)} %get-tuple-element.41), channel_id=1, source_target_pairs={{0,14},{1,15},{2,12},{3,13},{4,10},{5,11},{6,8},{7,9},{8,6},{9,7},... | collective-permute-start | bytes 688136 | tf_op jit(solution)/shard_map/ppermute | solution.py:341
  52.7 42.5 %collective-permute-start.5 = (bf16[448,256]{1,0:T(8,128)(2,1)}, bf16[448,256]{1,0:T(8,128)(2,1)}, u32[]{:S(2)}, u32[]{:S(2)}) collective-permute-start(bf16[448,256]{1,0:T(8,128)(2,1)} %get-tuple-element.39), channel_id=1, source_target_pairs={{0,13},{1,12},{2,15},{3,14},{4,9},{5,8},{6,11},{7,10},{8,5},{9,4},... | collective-permute-start | bytes 688136 | tf_op jit(solution)/shard_map/ppermute | solution.py:341
  53.3 13.1 %copy-start.3 = (bf16[448,256]{1,0:T(8,128)(2,1)S(1)}, bf16[448,256]{1,0:T(8,128)(2,1)}, u32[]{:S(2)}) copy-start(bf16[448,256]{1,0:T(8,128)(2,1)} %get-tuple-element.45) | copy-start | bytes 688132
  53.3 28.2 %copy-start.2 = (bf16[448,256]{1,0:T(8,128)(2,1)S(1)}, bf16[448,256]{1,0:T(8,128)(2,1)}, u32[]{:S(2)}) copy-start(bf16[448,256]{1,0:T(8,128)(2,1)} %get-tuple-element.37) | copy-start | bytes 688132
  66.4 43.9 %collective-permute-start.8 = (bf16[448,256]{1,0:T(8,128)(2,1)S(1)}, bf16[448,256]{1,0:T(8,128)(2,1)S(1)}, u32[]{:S(2)}, u32[]{:S(2)}) collective-permute-start(bf16[448,256]{1,0:T(8,128)(2,1)S(1)} %copy-done.3), channel_id=1, source_target_pairs={{0,10},{1,11},{2,8},{3,9},{4,14},{5,15},{6,12},{7,13},{8,2},{9,3},... | collective-permute-start | bytes 688136 | tf_op jit(solution)/shard_map/ppermute | solution.py:341
  81.4 32.3 %collective-permute-start.4 = (bf16[448,256]{1,0:T(8,128)(2,1)S(1)}, bf16[448,256]{1,0:T(8,128)(2,1)S(1)}, u32[]{:S(2)}, u32[]{:S(2)}) collective-permute-start(bf16[448,256]{1,0:T(8,128)(2,1)S(1)} %copy-done.2), channel_id=1, source_target_pairs={{0,11},{1,10},{2,9},{3,8},{4,15},{5,14},{6,13},{7,12},{8,3},{9,2},... | collective-permute-start | bytes 688136 | tf_op jit(solution)/shard_map/ppermute | solution.py:341

commit v7 on v5

--- a/solution.py
+++ b/solution.py
@@ -343,7 +343,7 @@
     def exchange(values):
         return lax.all_to_all(values, "docs", split_axis=0, concat_axis=0, tiled=True)
 
-    tail = width // 8 if width % (4 * LANES) == 0 else 0
+    tail = width // 32 * 3 if width % (4 * LANES) == 0 else 0
     if not tail:
         own_ids = cand_owner[:, 0] * doc_count + cand_row
         ids = exchange(jnp.broadcast_to(own_ids, (devices, 1, entries)))

time: 115 us -> 115 us (level)
    ppermute x9, waiting for transfers between devices: 29.8 us -> 35.6 us  [swap(): return lax.ppermute(values, 'docs', [(i, i ^ k) for i in range(devices)])]
    all_to_all x1, waiting for transfers between devices: 6.54 us -> 3.73 us  [exchange(): lax.all_to_all(values, 'docs', split_axis=0, concat_axis=0, tiled=True)]
    all_to_all x1, waiting for transfers between devices: 8.42 us -> 6.05 us  [on_device(): lax.all_to_all(picked, 'docs', split_axis=0, concat_axis=0, axis_index_gr...]
  transfers between devices with their start and end apart: 11 -> 11, of which waited for: 5 -> 6; matrix products, arithmetic and copies ran while one was open for 3% -> 3% of each run, Pallas kernels for 30% -> 30%
where the time goes in v7:
time: 115 us; the launch traced here: 114 us
  waiting for transfers between devices  45.3 us (39%)
  Pallas kernels  41.4 us (36%)
  starting transfers between devices  24.6 us (21%)
  local copies, waits for them, and re-layouts  2.95 us (3%)
    ppermute x9, waiting for transfers between devices, swap(): return lax.ppermute(values, 'docs', [(i, i ^ k) for i in range(devices)])  35.6 us
    ppermute x9, starting transfers between devices, swap(): return lax.ppermute(values, 'docs', [(i, i ^ k) for i in range(devices)])  16.1 us
    pallas_call x1, Pallas kernels, precondition(): call(kernel, jax.ShapeDtypeStruct(queries.shape, queries.dtype), (total /...  13.1 us
    pallas_call x1, Pallas kernels, gather_rows(): call(kernel, pltpu.HBM((count, features, entries), tables[0].dtype), (cou...  7.85 us
    pallas_call x1, Pallas kernels, score_near(): call(kernel, jax.ShapeDtypeStruct((queries, entries), jnp.float32), (coun...  7.01 us
    all_to_all x1, waiting for transfers between devices, on_device(): lax.all_to_all(picked, 'docs', split_axis=0, concat_axis=0, axis_index_gr...  6.05 us
    pallas_call x2, Pallas kernels, gather_pieces(): call(kernel, [pltpu.HBM((features, entries), tables[0][0].dtype)] * count...  5.9 us
    pallas_call x2, Pallas kernels, score_pieces(): call(kernel, jax.ShapeDtypeStruct((queries, entries), jnp.float32), (1,),...  5.63 us
  transfers between devices with their start and end apart: 11, of which 6 were waited for; matrix products, arithmetic and copies ran while one was open for 3% of the time, Pallas kernels for 30%

profile of v7, /device:TPU:0, one launch (start us, length us, event | category | flops | bytes accessed | tf_op | source)
XLA Modules:
  0.0 114.4 jit_solution(14594747080727381524)
XLA Ops:
  0.0 1.9 %shard_map.64 = (bf16[48,2048]{1,0:T(8,128)(2,1)}, s32[16,1,256]{2,1,0:T(1,128)}) custom-call(bf16[2048,512]{1,0:T(8,128)(2,1)} %docs_hbm.1, s32[1,256]{1,0:T(1,128)} %bitcast.7, s32[1,256]{1,0:T(1,128)} %bitcast.8), custom_call_target="tpu_custom_call" | custom-call | bytes 720896 | tf_op jit(solution)/shard_map/pallas_call | solution.py:63
  1.9 4.1 %collective-permute-start = (bf16[48,2048]{1,0:T(8,128)(2,1)}, bf16[48,2048]{1,0:T(8,128)(2,1)S(1)}, u32[]{:S(2)}, u32[]{:S(2)}) collective-permute-start(bf16[48,2048]{1,0:T(8,128)(2,1)} %get-tuple-element.24), channel_id=1, source_target_pairs={{0,8},{1,9},{2,10},{3,11},{4,12},{5,13},{6,14},{7,15},{8,0},{9,1},... | collective-permute-start | bytes 589832 | tf_op jit(solution)/shard_map/ppermute | solution.py:341
  6.0 3.9 %all-to-all-start = ((s32[16,1,256]{2,1,0:T(1,128)}), s32[16,1,256]{2,1,0:T(1,128)S(1)}, u32[]{:S(2)}, u32[]{:S(2)}) async-start(s32[16,1,256]{2,1,0:T(1,128)} %get-tuple-element.23), calls=%async_computation | async-start | bytes 32768 | tf_op jit(solution)/shard_map/all_to_all | solution.py:344
  10.0 2.9 %copy.7 = bf16[2048,512]{0,1:T(8,128)(2,1)S(1)} copy(bf16[2048,512]{1,0:T(8,128)(2,1)} %docs_hbm.1) | data formatting | bytes 4194304 | tf_op jit(solution)/shard_map/optimization_barrier | solution.py:327
  12.9 3.7 %all-to-all-done.refs_0_.refs_1_.refs_2_.refs_3_.ids_ref = s32[16,1,256]{2,1,0:T(1,128)S(1)} async-done(((s32[16,1,256]{2,1,0:T(1,128)}), s32[16,1,256]{2,1,0:T(1,128)S(1)}, u32[]{:S(2)}, u32[]{:S(2)}) %all-to-all-start) | async-done | bytes 16416 | tf_op jit(solution)/shard_map/all_to_all | solution.py:344
  16.6 0.0 collective-permute-done.refs_1_
  16.7 3.0 %shard_map.65 = (bf16[464,256]{1,0:T(8,128)(2,1)}, bf16[464,256]{1,0:T(8,128)(2,1)}, bf16[464,256]{1,0:T(8,128)(2,1)}, bf16[464,256]{1,0:T(8,128)(2,1)}) custom-call(s32[1]{0:T(128)} %bitcast.me_ref, s32[16,1,256]{2,1,0:T(1,128)S(1)} %all-to-all-done.refs_0_.refs_1_.refs_2_.refs_3_.ids_ref, ...), custom_call_target="tpu_custom_call" | custom-call | flops 1000 | bytes 1000 | tf_op jit(solution)/shard_map/pallas_call | solution.py:130
  19.6 3.2 %collective-permute-start.2 = (bf16[464,256]{1,0:T(8,128)(2,1)}, bf16[464,256]{1,0:T(8,128)(2,1)S(1)}, u32[]{:S(2)}, u32[]{:S(2)}) collective-permute-start(bf16[464,256]{1,0:T(8,128)(2,1)} %get-tuple-element.28), channel_id=1, source_target_pairs={{0,13},{1,12},{2,15},{3,14},{4,9},{5,8},{6,11},{7,10},{8,5},{9,4},... | collective-permute-start | bytes 712712 | tf_op jit(solution)/shard_map/ppermute | solution.py:341
  22.8 0.3 collective-permute-start.1
  23.1 7.8 %shard_map.67 = bf16[8,560,256]{2,1,0:T(8,128)(2,1)} custom-call(s32[1]{0:T(128)S(6)} %and.4.base_ref, s32[16,1,256]{2,1,0:T(1,128)S(1)} %all-to-all-done.refs_0_.refs_1_.refs_2_.refs_3_.ids_ref, bf16[512,2048]{1,0:T(8,128)(2,1)S(1)} %bitcast.5, bf16[48,2048]{1,0:T(8,128)(2,1)S(1)} %collective-permute-done.refs_1_), custom_call_target="tpu_custom_call" | custom-call | flops 1000 | bytes 1000 | tf_op jit(solution)/shard_map/pallas_call | solution.py:101
  31.0 0.0 copy-start
  31.0 0.0 copy-start.1
  31.0 4.5 %all-to-all-start.1 = ((bf16[8,560,256]{2,1,0:T(8,128)(2,1)}), bf16[8,560,256]{2,1,0:T(8,128)(2,1)}, u32[]{:S(2)}, u32[]{:S(2)}) async-start(bf16[8,560,256]{2,1,0:T(8,128)(2,1)} %shard_map.67), calls=%async_computation.1 | async-start | bytes 4587520 | tf_op jit(solution)/shard_map/all_to_all | solution.py:365
  35.5 3.5 %collective-permute-start.3 = (bf16[464,256]{1,0:T(8,128)(2,1)}, bf16[464,256]{1,0:T(8,128)(2,1)}, u32[]{:S(2)}, u32[]{:S(2)}) collective-permute-start(bf16[464,256]{1,0:T(8,128)(2,1)} %get-tuple-element.33), channel_id=1, source_target_pairs={{0,14},{1,15},{2,12},{3,13},{4,10},{5,11},{6,8},{7,9},{8,6},{9,7},... | collective-permute-start | bytes 712712 | tf_op jit(solution)/shard_map/ppermute | solution.py:341
  39.1 0.9 collective-permute-start.5
  40.0 2.9 %shard_map.68 = (bf16[464,256]{1,0:T(8,128)(2,1)}, bf16[464,256]{1,0:T(8,128)(2,1)}, bf16[464,256]{1,0:T(8,128)(2,1)}, bf16[464,256]{1,0:T(8,128)(2,1)}) custom-call(s32[1]{0:T(128)} %bitcast.me_ref, s32[16,1,256]{2,1,0:T(1,128)S(1)} %all-to-all-done.refs_0_.refs_1_.refs_2_.refs_3_.ids_ref, ...), custom_call_target="tpu_custom_call" | custom-call | flops 1000 | bytes 1000 | tf_op jit(solution)/shard_map/pallas_call | solution.py:130
  42.9 0.0 collective-permute-start.6
  42.9 0.0 collective-permute-done.2.refs_8_
  42.9 0.0 collective-permute-done.1.refs_7_
  42.9 4.0 %collective-permute-start.8 = (bf16[464,256]{1,0:T(8,128)(2,1)}, bf16[464,256]{1,0:T(8,128)(2,1)}, u32[]{:S(2)}, u32[]{:S(2)}) collective-permute-start(bf16[464,256]{1,0:T(8,128)(2,1)} %get-tuple-element.40), channel_id=1, source_target_pairs={{0,10},{1,11},{2,8},{3,9},{4,14},{5,15},{6,12},{7,13},{8,2},{9,3},... | collective-permute-start | bytes 712712 | tf_op jit(solution)/shard_map/ppermute | solution.py:341
  47.0 0.0 collective-permute-start.7
  47.0 0.0 copy-done
  47.0 0.0 copy-done.1
  47.0 0.0 copy-start.2
  47.0 13.1 %shard_map.66.own_ref.far_ref.refs_0_.refs_1_.refs_2_.refs_3_.refs_4_.refs_5_.refs_6_ = bf16[512,8192]{1,0:T(8,128)(2,1)} custom-call(bf16[512,8192]{1,0:T(8,128)(2,1)} %queries_ref, bf16[2,32,32]{2,1,0:T(8,128)(2,1)S(1)} %copy-done.1, bf16[2,128,128]{2,1,0:T(8,128)(2,1)S(1)} %copy-done), custom_call_target="tpu_custom_call" | custom-call | flops 167772160000 | bytes 16777216 | tf_op jit(solution)/shard_map/pallas_call | solution.py:306
  60.1 16.8 %collective-permute-done.3.refs_9_ = bf16[464,256]{1,0:T(8,128)(2,1)} collective-permute-done((bf16[464,256]{1,0:T(8,128)(2,1)}, bf16[464,256]{1,0:T(8,128)(2,1)}, u32[]{:S(2)}, u32[]{:S(2)}) %collective-permute-start.3) | collective-permute-done | bytes 237600 | tf_op jit(solution)/shard_map/ppermute | solution.py:341
  76.8 0.0 copy-done.2
  76.8 0.0 collective-permute-start.4
  76.8 6.1 %all-to-all-done.1.chosen_ref = bf16[8,560,256]{2,1,0:T(8,128)(2,1)} async-done(((bf16[8,560,256]{2,1,0:T(8,128)(2,1)}), bf16[8,560,256]{2,1,0:T(8,128)(2,1)}, u32[]{:S(2)}, u32[]{:S(2)}) %all-to-all-start.1) | async-done | bytes 2293792 | tf_op jit(solution)/shard_map/all_to_all | solution.py:365
  82.9 7.0 %shard_map.69.refs_14_ = f32[512,256]{1,0:T(8,128)S(1)} custom-call(s32[1]{0:T(128)S(6)} %and.4.base_ref, bf16[512,8192]{1,0:T(8,128)(2,1)} %shard_map.66.own_ref.far_ref.refs_0_.refs_1_.refs_2_.refs_3_.refs_4_.refs_5_.refs_6_, bf16[512,8192]{1,0:T(8,128)(2,1)} %shard_map.66.own_ref.far_ref.refs_0_.refs_1_.refs_2_.refs_3_.refs_4_.refs_5_.refs_6_, ...), custom_call_target="tpu_custom_call" | custom-call | flops 1174405120 | bytes 7405568 | tf_op jit(solution)/shard_map/pallas_call | solution.py:193
  89.9 0.0 collective-permute-done.5.refs_10_
  89.9 0.0 collective-permute-done.6.refs_11_
  89.9 13.2 %collective-permute-done.8.refs_13_ = bf16[464,256]{1,0:T(8,128)(2,1)} collective-permute-done((bf16[464,256]{1,0:T(8,128)(2,1)}, bf16[464,256]{1,0:T(8,128)(2,1)}, u32[]{:S(2)}, u32[]{:S(2)}) %collective-permute-start.8) | collective-permute-done | bytes 237600 | tf_op jit(solution)/shard_map/ppermute | solution.py:341
  103.2 3.7 %collective-permute-done.7.refs_12_ = bf16[464,256]{1,0:T(8,128)(2,1)} collective-permute-done((bf16[464,256]{1,0:T(8,128)(2,1)}, bf16[464,256]{1,0:T(8,128)(2,1)}, u32[]{:S(2)}, u32[]{:S(2)}) %collective-permute-start.7) | collective-permute-done | bytes 237600 | tf_op jit(solution)/shard_map/ppermute | solution.py:341
  106.9 3.5 %shard_map.70.refs_2_ = f32[512,256]{1,0:T(8,128)S(1)} custom-call(s32[1]{0:T(128)} %bitcast.me_ref, bf16[512,8192]{1,0:T(8,128)(2,1)} %shard_map.66.own_ref.far_ref.refs_0_.refs_1_.refs_2_.refs_3_.refs_4_.refs_5_.refs_6_, bf16[512,8192]{1,0:T(8,128)(2,1)} %shard_map.66.own_ref.far_ref.refs_0_.refs_1_.refs_2_.refs_3_.refs_4_.refs_5_.refs_6_, ...), custom_call_target="tpu_custom_call" | custom-call | flops 851443712 | bytes 6037504 | tf_op jit(solution)/shard_map/pallas_call | solution.py:160
  110.4 1.8 %collective-permute-done.4.refs_1_ = bf16[464,256]{1,0:T(8,128)(2,1)S(1)} collective-permute-done((bf16[464,256]{1,0:T(8,128)(2,1)S(1)}, bf16[464,256]{1,0:T(8,128)(2,1)S(1)}, u32[]{:S(2)}, u32[]{:S(2)}) %collective-permute-start.4) | collective-permute-done | bytes 237600 | tf_op jit(solution)/shard_map/ppermute | solution.py:341
  112.2 2.1 %shard_map.71 = f32[512,256]{1,0:T(8,128)} custom-call(s32[1]{0:T(128)} %bitcast.me_ref, bf16[512,8192]{1,0:T(8,128)(2,1)} %shard_map.66.own_ref.far_ref.refs_0_.refs_1_.refs_2_.refs_3_.refs_4_.refs_5_.refs_6_, bf16[464,256]{1,0:T(8,128)(2,1)S(1)} %collective-permute-done.4.refs_1_, f32[512,256]{1,0:T(8,128)S(1)} %shard_map.70.refs_2_), custom_call_target="tpu_custom_call" | custom-call | flops 121634816 | bytes 1761280 | tf_op jit(solution)/shard_map/pallas_call | solution.py:160
Async XLA Ops:
  1.9 14.7 %collective-permute-start = (bf16[48,2048]{1,0:T(8,128)(2,1)}, bf16[48,2048]{1,0:T(8,128)(2,1)S(1)}, u32[]{:S(2)}, u32[]{:S(2)}) collective-permute-start(bf16[48,2048]{1,0:T(8,128)(2,1)} %get-tuple-element.24), channel_id=1, source_target_pairs={{0,8},{1,9},{2,10},{3,11},{4,12},{5,13},{6,14},{7,15},{8,0},{9,1},... | collective-permute-start | bytes 589832 | tf_op jit(solution)/shard_map/ppermute | solution.py:341
  6.0 10.6 %all-to-all-start = ((s32[16,1,256]{2,1,0:T(1,128)}), s32[16,1,256]{2,1,0:T(1,128)S(1)}, u32[]{:S(2)}, u32[]{:S(2)}) async-start(s32[16,1,256]{2,1,0:T(1,128)} %get-tuple-element.23), calls=%async_computation | async-start | bytes 32768 | tf_op jit(solution)/shard_map/all_to_all | solution.py:344
  19.6 23.3 %collective-permute-start.2 = (bf16[464,256]{1,0:T(8,128)(2,1)}, bf16[464,256]{1,0:T(8,128)(2,1)S(1)}, u32[]{:S(2)}, u32[]{:S(2)}) collective-permute-start(bf16[464,256]{1,0:T(8,128)(2,1)} %get-tuple-element.28), channel_id=1, source_target_pairs={{0,13},{1,12},{2,15},{3,14},{4,9},{5,8},{6,11},{7,10},{8,5},{9,4},... | collective-permute-start | bytes 712712 | tf_op jit(solution)/shard_map/ppermute | solution.py:341
  22.8 20.1 %collective-permute-start.1 = (bf16[464,256]{1,0:T(8,128)(2,1)}, bf16[464,256]{1,0:T(8,128)(2,1)S(1)}, u32[]{:S(2)}, u32[]{:S(2)}) collective-permute-start(bf16[464,256]{1,0:T(8,128)(2,1)} %get-tuple-element.27), channel_id=1, source_target_pairs={{0,12},{1,13},{2,14},{3,15},{4,8},{5,9},{6,10},{7,11},{8,4},{9,5},... | collective-permute-start | bytes 712712 | tf_op jit(solution)/shard_map/ppermute | solution.py:341
  31.0 16.0 %copy-start = (bf16[2,128,128]{2,1,0:T(8,128)(2,1)S(1)}, bf16[2,128,128]{2,1,0:T(8,128)(2,1)}, u32[]{:S(2)}) copy-start(bf16[2,128,128]{2,1,0:T(8,128)(2,1)} %right_inv_ref.1) | copy-start | bytes 196612
  31.0 16.0 %copy-start.1 = (bf16[2,32,32]{2,1,0:T(8,128)(2,1)S(1)}, bf16[2,32,32]{2,1,0:T(8,128)(2,1)}, u32[]{:S(2)}) copy-start(bf16[2,32,32]{2,1,0:T(8,128)(2,1)} %left_inv_ref.1) | copy-start | bytes 12292
  31.0 51.9 %all-to-all-start.1 = ((bf16[8,560,256]{2,1,0:T(8,128)(2,1)}), bf16[8,560,256]{2,1,0:T(8,128)(2,1)}, u32[]{:S(2)}, u32[]{:S(2)}) async-start(bf16[8,560,256]{2,1,0:T(8,128)(2,1)} %shard_map.67), calls=%async_computation.1 | async-start | bytes 4587520 | tf_op jit(solution)/shard_map/all_to_all | solution.py:365
  35.5 41.3 %collective-permute-start.3 = (bf16[464,256]{1,0:T(8,128)(2,1)}, bf16[464,256]{1,0:T(8,128)(2,1)}, u32[]{:S(2)}, u32[]{:S(2)}) collective-permute-start(bf16[464,256]{1,0:T(8,128)(2,1)} %get-tuple-element.33), channel_id=1, source_target_pairs={{0,14},{1,15},{2,12},{3,13},{4,10},{5,11},{6,8},{7,9},{8,6},{9,7},... | collective-permute-start | bytes 712712 | tf_op jit(solution)/shard_map/ppermute | solution.py:341
  39.1 50.9 %collective-permute-start.5 = (bf16[464,256]{1,0:T(8,128)(2,1)}, bf16[464,256]{1,0:T(8,128)(2,1)}, u32[]{:S(2)}, u32[]{:S(2)}) collective-permute-start(bf16[464,256]{1,0:T(8,128)(2,1)} %get-tuple-element.35), channel_id=1, source_target_pairs={{0,15},{1,14},{2,13},{3,12},{4,11},{5,10},{6,9},{7,8},{8,7},{9,6},... | collective-permute-start | bytes 712712 | tf_op jit(solution)/shard_map/ppermute | solution.py:341
  42.9 47.0 %collective-permute-start.6 = (bf16[464,256]{1,0:T(8,128)(2,1)}, bf16[464,256]{1,0:T(8,128)(2,1)}, u32[]{:S(2)}, u32[]{:S(2)}) collective-permute-start(bf16[464,256]{1,0:T(8,128)(2,1)} %get-tuple-element.36), channel_id=1, source_target_pairs={{0,8},{1,9},{2,10},{3,11},{4,12},{5,13},{6,14},{7,15},{8,0},{9,1},... | collective-permute-start | bytes 712712 | tf_op jit(solution)/shard_map/ppermute | solution.py:341
  42.9 60.3 %collective-permute-start.8 = (bf16[464,256]{1,0:T(8,128)(2,1)}, bf16[464,256]{1,0:T(8,128)(2,1)}, u32[]{:S(2)}, u32[]{:S(2)}) collective-permute-start(bf16[464,256]{1,0:T(8,128)(2,1)} %get-tuple-element.40), channel_id=1, source_target_pairs={{0,10},{1,11},{2,8},{3,9},{4,14},{5,15},{6,12},{7,13},{8,2},{9,3},... | collective-permute-start | bytes 712712 | tf_op jit(solution)/shard_map/ppermute | solution.py:341
  47.0 59.9 %collective-permute-start.7 = (bf16[464,256]{1,0:T(8,128)(2,1)}, bf16[464,256]{1,0:T(8,128)(2,1)}, u32[]{:S(2)}, u32[]{:S(2)}) collective-permute-start(bf16[464,256]{1,0:T(8,128)(2,1)} %get-tuple-element.38), channel_id=1, source_target_pairs={{0,9},{1,8},{2,11},{3,10},{4,13},{5,12},{6,15},{7,14},{8,1},{9,0},... | collective-permute-start | bytes 712712 | tf_op jit(solution)/shard_map/ppermute | solution.py:341
  47.0 29.8 %copy-start.2 = (bf16[464,256]{1,0:T(8,128)(2,1)S(1)}, bf16[464,256]{1,0:T(8,128)(2,1)}, u32[]{:S(2)}) copy-start(bf16[464,256]{1,0:T(8,128)(2,1)} %get-tuple-element.34) | copy-start | bytes 712708
  76.8 35.4 %collective-permute-start.4 = (bf16[464,256]{1,0:T(8,128)(2,1)S(1)}, bf16[464,256]{1,0:T(8,128)(2,1)S(1)}, u32[]{:S(2)}, u32[]{:S(2)}) collective-permute-start(bf16[464,256]{1,0:T(8,128)(2,1)S(1)} %copy-done.2), channel_id=1, source_target_pairs={{0,11},{1,10},{2,9},{3,8},{4,15},{5,14},{6,13},{7,12},{8,3},{9,2},... | collective-permute-start | bytes 712712 | tf_op jit(solution)/shard_map/ppermute | solution.py:341

commit v8 on v5

--- a/solution.py
+++ b/solution.py
@@ -358,8 +358,8 @@
     first, second = list(range(half + quarter, devices)), list(range(half, half + quarter))
     body = [(table, width - tail)]
     ids = after(ids, across)
-    pieces = dict(zip(first, gather_pieces(me, ids, body, first)))
-    came = {k: swap(pieces[k], k) for k in first}
+    pieces = dict(zip(first, gather_pieces(me, ids, body, first[:2])))
+    came = {k: swap(pieces[k], k) for k in first[:2]}
     ids = after(ids, pieces[first[0]])
     picked = gather_rows(base, ids, [table, across], half)
     near = lax.all_to_all(
@@ -371,7 +371,9 @@
         tiled=True,
     )
     ids = after(ids, picked)
-    pieces.update(zip(second, gather_pieces(me, ids, body, second)))
+    rest = first[2:] + second
+    pieces.update(zip(rest, gather_pieces(me, ids, body, rest)))
+    came.update({k: swap(pieces[k], k) for k in first[2:]})
     prepared = precondition(after(query_grads, *[came[k] for k in first[:2]]), left_inv, right_inv)
     for i, k in enumerate(second):
         before = [came[first[i - 1]]] if i else []

time: 115 us -> 116 us (level)
    ppermute x9, waiting for transfers between devices: 29.8 us -> 33.5 us  [swap(): return lax.ppermute(values, 'docs', [(i, i ^ k) for i in range(devices)])]
    all_to_all x1, waiting for transfers between devices: 8.42 us -> 5.61 us  [on_device(): lax.all_to_all(picked, 'docs', split_axis=0, concat_axis=0, axis_index_gr...]
  transfers between devices with their start and end apart: 11 -> 11, of which waited for: 5 -> 6; matrix products, arithmetic and copies ran while one was open for 3% -> 3% of each run, Pallas kernels for 30% -> 31%
where the time goes in v8:
time: 116 us; the launch traced here: 115 us
  waiting for transfers between devices  45.6 us (39%)
  Pallas kernels  41.4 us (36%)
  starting transfers between devices  24.6 us (21%)
  local copies, waits for them, and re-layouts  2.94 us (3%)
    ppermute x9, waiting for transfers between devices, swap(): return lax.ppermute(values, 'docs', [(i, i ^ k) for i in range(devices)])  33.5 us
    ppermute x9, starting transfers between devices, swap(): return lax.ppermute(values, 'docs', [(i, i ^ k) for i in range(devices)])  16.1 us
    pallas_call x1, Pallas kernels, precondition(): call(kernel, jax.ShapeDtypeStruct(queries.shape, queries.dtype), (total /...  13.1 us
    pallas_call x1, Pallas kernels, gather_rows(): call(kernel, pltpu.HBM((count, features, entries), tables[0].dtype), (cou...  8.01 us
    pallas_call x1, Pallas kernels, score_near(): call(kernel, jax.ShapeDtypeStruct((queries, entries), jnp.float32), (coun...  7 us
    all_to_all x1, waiting for transfers between devices, exchange(): lax.all_to_all(values, 'docs', split_axis=0, concat_axis=0, tiled=True)  6.54 us
    pallas_call x2, Pallas kernels, gather_pieces(): call(kernel, [pltpu.HBM((features, entries), tables[0][0].dtype)] * count...  5.77 us
    all_to_all x1, waiting for transfers between devices, on_device(): lax.all_to_all(picked, 'docs', split_axis=0, concat_axis=0, axis_index_gr...  5.61 us
  transfers between devices with their start and end apart: 11, of which 6 were waited for; matrix products, arithmetic and copies ran while one was open for 3% of the time, Pallas kernels for 31%

profile of v8, /device:TPU:0, one launch (start us, length us, event | category | flops | bytes accessed | tf_op | source)
XLA Modules:
  0.0 114.7 jit_solution(12465014272168923896)
XLA Ops:
  0.0 2.0 %shard_map.64 = (bf16[64,2048]{1,0:T(8,128)(2,1)}, s32[16,1,256]{2,1,0:T(1,128)}) custom-call(bf16[2048,512]{1,0:T(8,128)(2,1)} %docs_hbm.1, s32[1,256]{1,0:T(1,128)} %bitcast.7, s32[1,256]{1,0:T(1,128)} %bitcast.8), custom_call_target="tpu_custom_call" | custom-call | bytes 786432 | tf_op jit(solution)/shard_map/pallas_call | solution.py:63
  2.0 4.1 %collective-permute-start = (bf16[64,2048]{1,0:T(8,128)(2,1)}, bf16[64,2048]{1,0:T(8,128)(2,1)S(1)}, u32[]{:S(2)}, u32[]{:S(2)}) collective-permute-start(bf16[64,2048]{1,0:T(8,128)(2,1)} %get-tuple-element.24), channel_id=1, source_target_pairs={{0,8},{1,9},{2,10},{3,11},{4,12},{5,13},{6,14},{7,15},{8,0},{9,1},... | collective-permute-start | bytes 786440 | tf_op jit(solution)/shard_map/ppermute | solution.py:341
  6.1 3.9 %all-to-all-start = ((s32[16,1,256]{2,1,0:T(1,128)}), s32[16,1,256]{2,1,0:T(1,128)S(1)}, u32[]{:S(2)}, u32[]{:S(2)}) async-start(s32[16,1,256]{2,1,0:T(1,128)} %get-tuple-element.23), calls=%async_computation | async-start | bytes 32768 | tf_op jit(solution)/shard_map/all_to_all | solution.py:344
  10.0 2.9 %copy.7 = bf16[2048,512]{0,1:T(8,128)(2,1)S(1)} copy(bf16[2048,512]{1,0:T(8,128)(2,1)} %docs_hbm.1) | data formatting | bytes 4194304 | tf_op jit(solution)/shard_map/optimization_barrier | solution.py:327
  12.9 6.5 %all-to-all-done.refs_0_.refs_1_.ids_ref.refs_2_.refs_3_.refs_4_.refs_5_ = s32[16,1,256]{2,1,0:T(1,128)S(1)} async-done(((s32[16,1,256]{2,1,0:T(1,128)}), s32[16,1,256]{2,1,0:T(1,128)S(1)}, u32[]{:S(2)}, u32[]{:S(2)}) %all-to-all-start) | async-done | bytes 16416 | tf_op jit(solution)/shard_map/all_to_all | solution.py:344
  19.5 0.0 collective-permute-done.refs_1_
  19.5 1.9 %shard_map.65 = (bf16[448,256]{1,0:T(8,128)(2,1)}, bf16[448,256]{1,0:T(8,128)(2,1)}) custom-call(s32[1]{0:T(128)} %bitcast.me_ref, s32[16,1,256]{2,1,0:T(1,128)S(1)} %all-to-all-done.refs_0_.refs_1_.ids_ref.refs_2_.refs_3_.refs_4_.refs_5_, s32[16,1,256]{2,1,0:T(1,128)S(1)} %all-to-all-done.refs_0_.refs_1_.ids_ref.refs_2_.refs_3_.refs_4_.refs_5_, ...), custom_call_target="tpu_custom_call" | custom-call | flops 1000 | bytes 1000 | tf_op jit(solution)/shard_map/pallas_call | solution.py:130
  21.4 3.2 %collective-permute-start.2 = (bf16[448,256]{1,0:T(8,128)(2,1)}, bf16[448,256]{1,0:T(8,128)(2,1)S(1)}, u32[]{:S(2)}, u32[]{:S(2)}) collective-permute-start(bf16[448,256]{1,0:T(8,128)(2,1)} %get-tuple-element.28), channel_id=1, source_target_pairs={{0,13},{1,12},{2,15},{3,14},{4,9},{5,8},{6,11},{7,10},{8,5},{9,4},... | collective-permute-start | bytes 688136 | tf_op jit(solution)/shard_map/ppermute | solution.py:341
  24.6 0.3 collective-permute-start.1
  24.9 8.0 %shard_map.67 = bf16[8,576,256]{2,1,0:T(8,128)(2,1)} custom-call(s32[1]{0:T(128)S(6)} %and.4.base_ref, s32[16,1,256]{2,1,0:T(1,128)S(1)} %all-to-all-done.refs_0_.refs_1_.ids_ref.refs_2_.refs_3_.refs_4_.refs_5_, bf16[512,2048]{1,0:T(8,128)(2,1)S(1)} %bitcast.5, bf16[64,2048]{1,0:T(8,128)(2,1)S(1)} %collective-permute-done.refs_1_), custom_call_target="tpu_custom_call" | custom-call | flops 1000 | bytes 1000 | tf_op jit(solution)/shard_map/pallas_call | solution.py:101
  33.0 0.0 copy-start
  33.0 0.0 copy-start.1
  33.0 4.5 %all-to-all-start.1 = ((bf16[8,576,256]{2,1,0:T(8,128)(2,1)}), bf16[8,576,256]{2,1,0:T(8,128)(2,1)}, u32[]{:S(2)}, u32[]{:S(2)}) async-start(bf16[8,576,256]{2,1,0:T(8,128)(2,1)} %shard_map.67), calls=%async_computation.1 | async-start | bytes 4718592 | tf_op jit(solution)/shard_map/all_to_all | solution.py:365
  37.5 3.9 %shard_map.68 = (bf16[448,256]{1,0:T(8,128)(2,1)}, bf16[448,256]{1,0:T(8,128)(2,1)}, bf16[448,256]{1,0:T(8,128)(2,1)}, bf16[448,256]{1,0:T(8,128)(2,1)}, bf16[44...) custom-call(s32[1]{0:T(128)} %bitcast.me_ref, ...), custom_call_target="tpu_custom_call" | custom-call | flops 1000 | bytes 1000 | tf_op jit(solution)/shard_map/pallas_call | solution.py:130
  41.3 3.5 %collective-permute-start.3 = (bf16[448,256]{1,0:T(8,128)(2,1)}, bf16[448,256]{1,0:T(8,128)(2,1)}, u32[]{:S(2)}, u32[]{:S(2)}) collective-permute-start(bf16[448,256]{1,0:T(8,128)(2,1)} %get-tuple-element.33), channel_id=1, source_target_pairs={{0,14},{1,15},{2,12},{3,13},{4,10},{5,11},{6,8},{7,9},{8,6},{9,7},... | collective-permute-start | bytes 688136 | tf_op jit(solution)/shard_map/ppermute | solution.py:341
  44.8 1.0 collective-permute-start.5
  45.8 0.0 collective-permute-start.6
  45.8 0.0 collective-permute-done.2.refs_8_
  45.8 0.0 collective-permute-done.1.refs_7_
  45.8 4.0 %collective-permute-start.8 = (bf16[448,256]{1,0:T(8,128)(2,1)}, bf16[448,256]{1,0:T(8,128)(2,1)}, u32[]{:S(2)}, u32[]{:S(2)}) collective-permute-start(bf16[448,256]{1,0:T(8,128)(2,1)} %get-tuple-element.40), channel_id=1, source_target_pairs={{0,10},{1,11},{2,8},{3,9},{4,14},{5,15},{6,12},{7,13},{8,2},{9,3},... | collective-permute-start | bytes 688136 | tf_op jit(solution)/shard_map/ppermute | solution.py:341
  49.8 0.0 collective-permute-start.7
  49.8 0.0 copy-done
  49.8 0.0 copy-done.1
  49.9 0.0 copy-start.2
  49.9 13.1 %shard_map.66.own_ref.far_ref.refs_0_.refs_1_.refs_2_.refs_3_.refs_4_.refs_5_.refs_6_ = bf16[512,8192]{1,0:T(8,128)(2,1)} custom-call(bf16[512,8192]{1,0:T(8,128)(2,1)} %queries_ref, bf16[2,32,32]{2,1,0:T(8,128)(2,1)S(1)} %copy-done.1, bf16[2,128,128]{2,1,0:T(8,128)(2,1)S(1)} %copy-done), custom_call_target="tpu_custom_call" | custom-call | flops 167772160000 | bytes 16777216 | tf_op jit(solution)/shard_map/pallas_call | solution.py:306
  63.0 17.0 %collective-permute-done.3.refs_9_ = bf16[448,256]{1,0:T(8,128)(2,1)} collective-permute-done((bf16[448,256]{1,0:T(8,128)(2,1)}, bf16[448,256]{1,0:T(8,128)(2,1)}, u32[]{:S(2)}, u32[]{:S(2)}) %collective-permute-start.3) | collective-permute-done | bytes 229408 | tf_op jit(solution)/shard_map/ppermute | solution.py:341
  79.9 0.0 copy-done.2
  79.9 0.0 collective-permute-start.4
  79.9 5.6 %all-to-all-done.1.chosen_ref = bf16[8,576,256]{2,1,0:T(8,128)(2,1)} async-done(((bf16[8,576,256]{2,1,0:T(8,128)(2,1)}), bf16[8,576,256]{2,1,0:T(8,128)(2,1)}, u32[]{:S(2)}, u32[]{:S(2)}) %all-to-all-start.1) | async-done | bytes 2359328 | tf_op jit(solution)/shard_map/all_to_all | solution.py:365
  85.6 7.0 %shard_map.69.refs_14_ = f32[512,256]{1,0:T(8,128)S(1)} custom-call(s32[1]{0:T(128)S(6)} %and.4.base_ref, bf16[512,8192]{1,0:T(8,128)(2,1)} %shard_map.66.own_ref.far_ref.refs_0_.refs_1_.refs_2_.refs_3_.refs_4_.refs_5_.refs_6_, bf16[512,8192]{1,0:T(8,128)(2,1)} %shard_map.66.own_ref.far_ref.refs_0_.refs_1_.refs_2_.refs_3_.refs_4_.refs_5_.refs_6_, ...), custom_call_target="tpu_custom_call" | custom-call | flops 1207959552 | bytes 7602176 | tf_op jit(solution)/shard_map/pallas_call | solution.py:193
  92.6 0.0 collective-permute-done.5.refs_10_
  92.6 0.0 collective-permute-done.6.refs_11_
  92.6 11.8 %collective-permute-done.8.refs_13_ = bf16[448,256]{1,0:T(8,128)(2,1)} collective-permute-done((bf16[448,256]{1,0:T(8,128)(2,1)}, bf16[448,256]{1,0:T(8,128)(2,1)}, u32[]{:S(2)}, u32[]{:S(2)}) %collective-permute-start.8) | collective-permute-done | bytes 229408 | tf_op jit(solution)/shard_map/ppermute | solution.py:341
  104.4 3.7 %collective-permute-done.7.refs_12_ = bf16[448,256]{1,0:T(8,128)(2,1)} collective-permute-done((bf16[448,256]{1,0:T(8,128)(2,1)}, bf16[448,256]{1,0:T(8,128)(2,1)}, u32[]{:S(2)}, u32[]{:S(2)}) %collective-permute-start.7) | collective-permute-done | bytes 229408 | tf_op jit(solution)/shard_map/ppermute | solution.py:341
  108.1 3.5 %shard_map.70.refs_2_ = f32[512,256]{1,0:T(8,128)S(1)} custom-call(s32[1]{0:T(128)} %bitcast.me_ref, bf16[512,8192]{1,0:T(8,128)(2,1)} %shard_map.66.own_ref.far_ref.refs_0_.refs_1_.refs_2_.refs_3_.refs_4_.refs_5_.refs_6_, bf16[512,8192]{1,0:T(8,128)(2,1)} %shard_map.66.own_ref.far_ref.refs_0_.refs_1_.refs_2_.refs_3_.refs_4_.refs_5_.refs_6_, ...), custom_call_target="tpu_custom_call" | custom-call | flops 822083584 | bytes 5865472 | tf_op jit(solution)/shard_map/pallas_call | solution.py:160
  111.5 1.0 collective-permute-done.4.refs_1_
  112.5 2.1 %shard_map.71 = f32[512,256]{1,0:T(8,128)} custom-call(s32[1]{0:T(128)} %bitcast.me_ref, bf16[512,8192]{1,0:T(8,128)(2,1)} %shard_map.66.own_ref.far_ref.refs_0_.refs_1_.refs_2_.refs_3_.refs_4_.refs_5_.refs_6_, bf16[448,256]{1,0:T(8,128)(2,1)S(1)} %collective-permute-done.4.refs_1_, f32[512,256]{1,0:T(8,128)S(1)} %shard_map.70.refs_2_), custom_call_target="tpu_custom_call" | custom-call | flops 117440512 | bytes 1736704 | tf_op jit(solution)/shard_map/pallas_call | solution.py:160
Async XLA Ops:
  2.0 17.5 %collective-permute-start = (bf16[64,2048]{1,0:T(8,128)(2,1)}, bf16[64,2048]{1,0:T(8,128)(2,1)S(1)}, u32[]{:S(2)}, u32[]{:S(2)}) collective-permute-start(bf16[64,2048]{1,0:T(8,128)(2,1)} %get-tuple-element.24), channel_id=1, source_target_pairs={{0,8},{1,9},{2,10},{3,11},{4,12},{5,13},{6,14},{7,15},{8,0},{9,1},... | collective-permute-start | bytes 786440 | tf_op jit(solution)/shard_map/ppermute | solution.py:341
  6.1 13.4 %all-to-all-start = ((s32[16,1,256]{2,1,0:T(1,128)}), s32[16,1,256]{2,1,0:T(1,128)S(1)}, u32[]{:S(2)}, u32[]{:S(2)}) async-start(s32[16,1,256]{2,1,0:T(1,128)} %get-tuple-element.23), calls=%async_computation | async-start | bytes 32768 | tf_op jit(solution)/shard_map/all_to_all | solution.py:344
  21.4 24.4 %collective-permute-start.2 = (bf16[448,256]{1,0:T(8,128)(2,1)}, bf16[448,256]{1,0:T(8,128)(2,1)S(1)}, u32[]{:S(2)}, u32[]{:S(2)}) collective-permute-start(bf16[448,256]{1,0:T(8,128)(2,1)} %get-tuple-element.28), channel_id=1, source_target_pairs={{0,13},{1,12},{2,15},{3,14},{4,9},{5,8},{6,11},{7,10},{8,5},{9,4},... | collective-permute-start | bytes 688136 | tf_op jit(solution)/shard_map/ppermute | solution.py:341
  24.6 21.2 %collective-permute-start.1 = (bf16[448,256]{1,0:T(8,128)(2,1)}, bf16[448,256]{1,0:T(8,128)(2,1)S(1)}, u32[]{:S(2)}, u32[]{:S(2)}) collective-permute-start(bf16[448,256]{1,0:T(8,128)(2,1)} %get-tuple-element.27), channel_id=1, source_target_pairs={{0,12},{1,13},{2,14},{3,15},{4,8},{5,9},{6,10},{7,11},{8,4},{9,5},... | collective-permute-start | bytes 688136 | tf_op jit(solution)/shard_map/ppermute | solution.py:341
  33.0 16.9 %copy-start = (bf16[2,128,128]{2,1,0:T(8,128)(2,1)S(1)}, bf16[2,128,128]{2,1,0:T(8,128)(2,1)}, u32[]{:S(2)}) copy-start(bf16[2,128,128]{2,1,0:T(8,128)(2,1)} %right_inv_ref.1) | copy-start | bytes 196612
  33.0 16.9 %copy-start.1 = (bf16[2,32,32]{2,1,0:T(8,128)(2,1)S(1)}, bf16[2,32,32]{2,1,0:T(8,128)(2,1)}, u32[]{:S(2)}) copy-start(bf16[2,32,32]{2,1,0:T(8,128)(2,1)} %left_inv_ref.1) | copy-start | bytes 12292
  33.0 52.6 %all-to-all-start.1 = ((bf16[8,576,256]{2,1,0:T(8,128)(2,1)}), bf16[8,576,256]{2,1,0:T(8,128)(2,1)}, u32[]{:S(2)}, u32[]{:S(2)}) async-start(bf16[8,576,256]{2,1,0:T(8,128)(2,1)} %shard_map.67), calls=%async_computation.1 | async-start | bytes 4718592 | tf_op jit(solution)/shard_map/all_to_all | solution.py:365
  41.3 38.6 %collective-permute-start.3 = (bf16[448,256]{1,0:T(8,128)(2,1)}, bf16[448,256]{1,0:T(8,128)(2,1)}, u32[]{:S(2)}, u32[]{:S(2)}) collective-permute-start(bf16[448,256]{1,0:T(8,128)(2,1)} %get-tuple-element.33), channel_id=1, source_target_pairs={{0,14},{1,15},{2,12},{3,13},{4,10},{5,11},{6,8},{7,9},{8,6},{9,7},... | collective-permute-start | bytes 688136 | tf_op jit(solution)/shard_map/ppermute | solution.py:341
  44.8 47.8 %collective-permute-start.5 = (bf16[448,256]{1,0:T(8,128)(2,1)}, bf16[448,256]{1,0:T(8,128)(2,1)}, u32[]{:S(2)}, u32[]{:S(2)}) collective-permute-start(bf16[448,256]{1,0:T(8,128)(2,1)} %get-tuple-element.35), channel_id=1, source_target_pairs={{0,15},{1,14},{2,13},{3,12},{4,11},{5,10},{6,9},{7,8},{8,7},{9,6},... | collective-permute-start | bytes 688136 | tf_op jit(solution)/shard_map/ppermute | solution.py:341
  45.8 46.8 %collective-permute-start.6 = (bf16[448,256]{1,0:T(8,128)(2,1)}, bf16[448,256]{1,0:T(8,128)(2,1)}, u32[]{:S(2)}, u32[]{:S(2)}) collective-permute-start(bf16[448,256]{1,0:T(8,128)(2,1)} %get-tuple-element.36), channel_id=1, source_target_pairs={{0,8},{1,9},{2,10},{3,11},{4,12},{5,13},{6,14},{7,15},{8,0},{9,1},... | collective-permute-start | bytes 688136 | tf_op jit(solution)/shard_map/ppermute | solution.py:341
  45.8 58.6 %collective-permute-start.8 = (bf16[448,256]{1,0:T(8,128)(2,1)}, bf16[448,256]{1,0:T(8,128)(2,1)}, u32[]{:S(2)}, u32[]{:S(2)}) collective-permute-start(bf16[448,256]{1,0:T(8,128)(2,1)} %get-tuple-element.40), channel_id=1, source_target_pairs={{0,10},{1,11},{2,8},{3,9},{4,14},{5,15},{6,12},{7,13},{8,2},{9,3},... | collective-permute-start | bytes 688136 | tf_op jit(solution)/shard_map/ppermute | solution.py:341
  49.8 58.3 %collective-permute-start.7 = (bf16[448,256]{1,0:T(8,128)(2,1)}, bf16[448,256]{1,0:T(8,128)(2,1)}, u32[]{:S(2)}, u32[]{:S(2)}) collective-permute-start(bf16[448,256]{1,0:T(8,128)(2,1)} %get-tuple-element.38), channel_id=1, source_target_pairs={{0,9},{1,8},{2,11},{3,10},{4,13},{5,12},{6,15},{7,14},{8,1},{9,0},... | collective-permute-start | bytes 688136 | tf_op jit(solution)/shard_map/ppermute | solution.py:341
  49.9 30.1 %copy-start.2 = (bf16[448,256]{1,0:T(8,128)(2,1)S(1)}, bf16[448,256]{1,0:T(8,128)(2,1)}, u32[]{:S(2)}) copy-start(bf16[448,256]{1,0:T(8,128)(2,1)} %get-tuple-element.34) | copy-start | bytes 688132
  79.9 32.6 %collective-permute-start.4 = (bf16[448,256]{1,0:T(8,128)(2,1)S(1)}, bf16[448,256]{1,0:T(8,128)(2,1)S(1)}, u32[]{:S(2)}, u32[]{:S(2)}) collective-permute-start(bf16[448,256]{1,0:T(8,128)(2,1)S(1)} %copy-done.2), channel_id=1, source_target_pairs={{0,11},{1,10},{2,9},{3,8},{4,15},{5,14},{6,13},{7,12},{8,3},{9,2},... | collective-permute-start | bytes 688136 | tf_op jit(solution)/shard_map/ppermute | solution.py:341
